TPU v7x, 128 devices: a whole 4x4x4 slice. The times are simulated.
128 devices in a mesh: seq: 32 (over y, z, core), section: 4 (over x).
Axes of the slice: x: 4, y: 4, z: 4, core: 2. Of those that a mesh axis runs over, the one named last changes fastest.
Arguments:
- tokens: bfloat16 [16384, 1280], P('seq'), may hold values from -6 to 6
- norm_gain: bfloat16 [1280], replicated, may hold values from 0.25 to 1.75
- w_qkv: bfloat16 [3, 1280, 1280], P(None, None, 'section')
- w_out: bfloat16 [1280, 1280], P('section'), may hold values from -0.15625 to 0.15625
- merge_gain: bfloat16 [1280], replicated, may hold values from 0.25 to 1.75
- seg_blocks: int32 [32], replicated, may hold values from 1 to 16, 256 in all
- mb_sizes: int32 [32], replicated, may hold values from 1 to 256, 4096 in all
- mb_receiver: int32 [32], replicated, may hold values from 0 to 31, each once
- merged_grad: bfloat16 [4096, 5120], P('seq'), may hold values from -6 to 6
Outputs:
- delivered: bfloat16 [8192, 5120], P('seq', 'section')
- grad_x: bfloat16 [16384, 1280], P('seq')
- grad_w_qkv: float32 [3, 1280, 1280], P(None, 'seq', 'section')
- grad_w_out: float32 [1280, 1280], P('section', 'seq')
Inputs may be any that keep to these rules, and one draw needn't show every extreme that they name: `seg_blocks`: images lie whole in the pack and sum to 16384 patches; the longest has exactly 1024 patches. `mb_sizes`: Micro-batches cover the 4096 merged rows in order; the largest has exactly 256 rows. `mb_receiver`: each receiver gets exactly one micro-batch.
All inputs are finite; a program needn't handle non-finite values.
Results may differ from a plain program's by a relative error of at most 0.022.
Values may be sent and summed in bfloat16 or wider, within the bound.
A program may use at most 192 MiB of HBM per device.

v0:
```python
from functools import reduce

import jax
import jax.numpy as jnp
from jax import lax
from jax.sharding import PartitionSpec as P

HEADS = 16


EPS = 1e-06
OFFSETS = (1, -1, 2, -2)


def passed_along(value, axis, steps):
    count = lax.axis_size(axis)
    leading, last = (max(0, -steps), min(count, count - steps))
    return lax.ppermute(value, axis, [(source, source + steps) for source in range(leading, last)])


def norm_forward(values, scale_gain):
    average = jnp.mean(values, axis=-1, keepdims=True)
    centered = values - average
    inv_scale = lax.rsqrt(jnp.mean(centered * centered, axis=-1, keepdims=True) + EPS)
    unit_rows = centered * inv_scale
    return (unit_rows * scale_gain.astype(jnp.float32), unit_rows, inv_scale)


def norm_backward(incoming, scale_gain, unit_rows, inv_scale):
    scaled = incoming * scale_gain.astype(jnp.float32)
    return inv_scale * (
        scaled
        - jnp.mean(scaled, axis=-1, keepdims=True)
        - unit_rows * jnp.mean(scaled * unit_rows, axis=-1, keepdims=True)
    )


def segment_of(positions, image_ends):
    return jnp.sum((positions[:, None] >= image_ends[None, :]).astype(jnp.int32), axis=1)


def contract_rows(left, right):
    return lax.dot_general(
        left, right, (((0,), (0,)), ((), ())), preferred_element_type=jnp.float32
    )


def contract_cols(left, right):
    return lax.dot_general(
        left, right, (((1,), (1,)), ((), ())), preferred_element_type=jnp.float32
    )


def local(
    tokens, norm_gain, w_qkv, w_out, merge_gain, seg_blocks, mb_sizes, mb_receiver, merged_grad
):
    tok_rows = tokens.shape[0]
    width = tokens.shape[1]
    head_dim = width // HEADS
    heads_here = w_qkv.shape[2] // head_dim
    factor = head_dim ** (-0.5)
    comp_rows = tok_rows // 4
    seq_index = lax.axis_index("seq")
    seq_count = lax.axis_size("seq")
    section_index = lax.axis_index("section")
    image_ends = 64 * jnp.cumsum(seg_blocks)
    row_ids = jnp.arange(tok_rows, dtype=jnp.int32)
    own_segment = segment_of(seq_index * tok_rows + row_ids, image_ends)

    def heads_of(values):
        return values.reshape(values.shape[0], heads_here, head_dim)

    inputs32 = tokens.astype(jnp.float32)
    normed_f, unit_one, inv_one = norm_forward(inputs32, norm_gain)
    normed = normed_f.astype(jnp.bfloat16)
    query = jnp.dot(normed, w_qkv[0], preferred_element_type=jnp.float32).astype(jnp.bfloat16)
    key_local = jnp.dot(normed, w_qkv[1], preferred_element_type=jnp.float32).astype(jnp.bfloat16)
    value_local = jnp.dot(normed, w_qkv[2], preferred_element_type=jnp.float32).astype(jnp.bfloat16)
    query_h = heads_of(query)
    local_pair = jnp.stack([key_local, value_local])
    key_pieces = [(local_pair, own_segment)]
    for offset in OFFSETS:
        arrived = passed_along(local_pair, "seq", offset)
        source = seq_index - offset
        inside = (source >= 0) & (source < seq_count)
        key_pieces.append(
            (arrived, jnp.where(inside, segment_of(source * tok_rows + row_ids, image_ends), -1))
        )
    blocks = []
    for pair, segment in key_pieces:
        scores = (
            jnp.einsum(
                "qhd,khd->hqk", query_h, heads_of(pair[0]), preferred_element_type=jnp.float32
            )
            * factor
        )
        allowed = (own_segment[:, None] == segment[None, :])[None]
        blocks.append((scores, allowed))
    highest = reduce(
        jnp.maximum,
        [jnp.max(jnp.where(allowed, scores, -jnp.inf), axis=2) for scores, allowed in blocks],
    )
    totals = reduce(
        jnp.add,
        [
            jnp.sum(jnp.where(allowed, jnp.exp(scores - highest[:, :, None]), 0.0), axis=2)
            for scores, allowed in blocks
        ],
    )
    log_total = highest + jnp.log(totals)

    def probs_of(scores, allowed, log_rows):
        return jnp.where(allowed, jnp.exp(scores - log_rows[:, :, None]), 0.0)

    attended_acc = jnp.zeros((tok_rows, heads_here, head_dim), jnp.float32)
    for (pair, segment), (scores, allowed) in zip(key_pieces, blocks):
        weights = probs_of(scores, allowed, log_total).astype(jnp.bfloat16)
        attended_acc = attended_acc + jnp.einsum(
            "hqk,khd->qhd", weights, heads_of(pair[1]), preferred_element_type=jnp.float32
        )
    attended = attended_acc.reshape(tok_rows, heads_here * head_dim).astype(jnp.bfloat16)
    partial_out = jnp.dot(attended, w_out, preferred_element_type=jnp.float32)
    layer_out = inputs32 + lax.psum(partial_out, "section")
    normed_two, unit_two, inv_two = norm_forward(layer_out, merge_gain)
    merged_all = normed_two.astype(jnp.bfloat16).reshape(comp_rows, 4, width)
    my_part = lax.dynamic_index_in_dim(merged_all, section_index, 1, keepdims=False)
    grad_incoming = merged_grad.reshape(tok_rows, width).astype(jnp.float32)
    grad_layer = norm_backward(grad_incoming, merge_gain, unit_two, inv_two).astype(jnp.bfloat16)
    batch_ids = jnp.arange(mb_receiver.shape[0], dtype=jnp.int32)
    starts = jnp.cumsum(mb_sizes) - mb_sizes
    everything = lax.all_gather(my_part, "seq", axis=0, tiled=True)
    total_rows = everything.shape[0]
    cap_rows = 2 * comp_rows
    picked = jnp.sum(jnp.where(mb_receiver == seq_index, batch_ids, 0))
    first_row = jnp.sum(jnp.where(batch_ids == picked, starts, 0))
    live_rows = jnp.sum(jnp.where(batch_ids == picked, mb_sizes, 0))
    slot_ids = jnp.arange(cap_rows, dtype=jnp.int32)
    taken = jnp.take(everything, jnp.minimum(first_row + slot_ids, total_rows - 1), axis=0)
    delivered = jnp.where((slot_ids < live_rows)[:, None], taken, jnp.zeros_like(taken))
    grad_att = contract_cols(grad_layer, w_out).astype(jnp.bfloat16)
    grad_w_out_part = contract_rows(attended, grad_layer)
    grad_att_h = heads_of(grad_att)
    row_delta = jnp.sum(
        grad_att_h.astype(jnp.float32) * heads_of(attended).astype(jnp.float32), axis=2
    ).T
    grad_query_acc = jnp.zeros((tok_rows, heads_here, head_dim), jnp.float32)
    key_acc = jnp.zeros((tok_rows, heads_here, head_dim), jnp.float32)
    value_acc = jnp.zeros((tok_rows, heads_here, head_dim), jnp.float32)
    for number, ((pair, segment), (scores, allowed)) in enumerate(zip(key_pieces, blocks)):
        probs = probs_of(scores, allowed, log_total)
        weights = probs.astype(jnp.bfloat16)
        grad_probs = jnp.einsum(
            "qhd,khd->hqk", grad_att_h, heads_of(pair[1]), preferred_element_type=jnp.float32
        )
        grad_scores = (probs * (grad_probs - row_delta[:, :, None])).astype(jnp.bfloat16)
        grad_query_acc = grad_query_acc + jnp.einsum(
            "hqk,khd->qhd", grad_scores, heads_of(pair[0]), preferred_element_type=jnp.float32
        )
        key_part = jnp.einsum(
            "hqk,qhd->khd", grad_scores, query_h, preferred_element_type=jnp.float32
        )
        value_part = jnp.einsum(
            "hqk,qhd->khd", weights, grad_att_h, preferred_element_type=jnp.float32
        )
        key_parts = jnp.stack([key_part, value_part])
        if number > 0:
            key_parts = passed_along(
                key_parts.astype(jnp.bfloat16), "seq", -OFFSETS[number - 1]
            ).astype(key_parts.dtype)
        key_acc = key_acc + key_parts[0]
        value_acc = value_acc + key_parts[1]
    grad_query = (grad_query_acc * factor).reshape(tok_rows, -1).astype(jnp.bfloat16)
    grad_key = (key_acc * factor).reshape(tok_rows, -1).astype(jnp.bfloat16)
    grad_value = value_acc.reshape(tok_rows, -1).astype(jnp.bfloat16)
    weight_terms = jnp.stack(
        [
            contract_rows(normed, grad_query),
            contract_rows(normed, grad_key),
            contract_rows(normed, grad_value),
        ]
    )
    grad_normed_part = (
        contract_cols(grad_query, w_qkv[0])
        + contract_cols(grad_key, w_qkv[1])
        + contract_cols(grad_value, w_qkv[2])
    )
    grad_normed = lax.psum(grad_normed_part.astype(jnp.bfloat16), "section").astype(jnp.float32)
    grad_x = (
        grad_layer.astype(jnp.float32) + norm_backward(grad_normed, norm_gain, unit_one, inv_one)
    ).astype(jnp.bfloat16)
    grad_w_qkv, grad_w_out = (
        lax.psum_scatter(
            weight_terms.astype(jnp.bfloat16), "seq", scatter_dimension=1, tiled=True
        ).astype(jnp.float32),
        lax.psum_scatter(
            grad_w_out_part.astype(jnp.bfloat16), "seq", scatter_dimension=1, tiled=True
        ).astype(jnp.float32),
    )
    return (delivered, grad_x, grad_w_qkv, grad_w_out)


def solution(mesh):
    placed = (
        P("seq", None),
        P(),
        P(None, None, "section"),
        P("section", None),
        P(),
        P(),
        P(),
        P(),
        P("seq", None),
    )
    return jax.shard_map(
        local,
        mesh=mesh,
        in_specs=placed,
        out_specs=(
            P("seq", "section"),
            P("seq", None),
            P(None, "seq", "section"),
            P("section", "seq"),
        ),
        check_vma=False,
    )
```

profile of v0, /device:TPU:1, one launch (start us, length us, event | category | flops | bytes accessed | tf_op | source)
XLA Modules:
  0.0 499.6 jit_solution(14464296338876369732)
XLA Ops:
  7.3 1.7 convert_reduce_fusion
  9.0 1.8 fusion.17
  14.2 5.2 %collective-permute-start.2 = (bf16[2,512,320]{1,2,0:T(8,128)(2,1)}, bf16[2,512,320]{1,2,0:T(8,128)(2,1)}, u32[]{:S(2)}, u32[]{:S(2)}) collective-permute-start(bf16[2,512,320]{1,2,0:T(8,128)(2,1)} %pad_maximum_fusion.1), channel_id=1, source_target_pairs={{0,8},{4,12},{8,16},{12,20},{16,24},{20,28},{24,32},{28,36},{32,40... | collective-permute-start | bytes 1966088 | tf_op jit(solution)/shard_map/ppermute | solution.py:18
  19.4 2.9 collective-permute-start.1
  22.3 2.7 collective-permute-start
  27.8 2.4 convolution_convert_fusion.14
  36.0 4.5 collective-permute-done
  46.6 5.5 %select_reduce_fusion.3 = (f32[4,512]{1,0:T(4,128)S(1)}, f32[4,512]{1,0:T(4,128)S(1)}, f32[4,512]{1,0:T(4,128)S(1)}, f32[4,512]{1,0:T(4,128)S(1)}, f32[4,512]{1,0:T(4,128)S(1)}) fusion(f32[4,512,512]{1,2,0:T(8,128)S(1)} %get-tuple-element.60, f32[4,512]{1,0:T(4,128)S(1)} %maximum_maximum_fusion, pred[512,512]{0,1:T(8,128)(4,1)S(1)} %get-tuple-element.46, ...), kind=kLoop, calls=%fused_computation.14 | loop fusion | flops 20961280 | bytes 22331392 | tf_op jit(solution)/shard_map/reduce_sum | solution.py:106
  58.2 2.3 fusion.84
  60.6 3.3 reshape.357
  63.9 67.3 %all-reduce.6.cloned.1.call-done = f32[512,1280]{1,0:T(8,128)} async-done(((f32[512,1280]{1,0:T(8,128)}), f32[512,1280]{1,0:T(8,128)}) %all-reduce.6.cloned.1.call-update) | async-done | bytes 2621456 | tf_op jit(solution)/shard_map/psum | solution.py:123
  131.3 2.2 fusion.79
  136.3 2.2 multiply_convert_fusion.5
  151.2 1.6 multiply_convert_fusion
  161.6 2.6 collective-permute-start.4
  165.9 3.2 collective-permute-start.5
  172.2 4.8 collective-permute-start.7
  178.9 1.9 convolution_convert_fusion
  180.8 2.4 fusion.28
  183.2 2.0 fusion.19
  195.7 1.7 pad_maximum_fusion
  197.4 7.7 %copy.129 = bf16[3,1280,320]{2,0,1:T(4,128)(2,1)} copy(bf16[3,1280,320]{1,2,0:T(8,128)(2,1)} %pad_maximum_fusion) | data formatting | bytes 4915200 | tf_op jit(solution)/shard_map/stack | solution.py:175
  206.1 2.2 fusion.39
  209.3 2.0 fusion.10
  212.8 2.0 constant_dynamic-slice_fusion
  221.1 36.5 %reduce-scatter.4.cloned.1.call-done = bf16[320,40]{0,1:T(8,128)(2,1)} async-done(((bf16[320,1280]{0,1:T(8,128)(2,1)}), bf16[320,40]{0,1:T(8,128)(2,1)}) %reduce-scatter.4.cloned.1.call-update) | async-done | bytes 25616
  258.9 114.0 %all-reduce.10.cloned.1.call-done = bf16[3,1280,320]{2,0,1:T(4,128)(2,1)} async-done(((bf16[3,1280,320]{2,0,1:T(4,128)(2,1)}), bf16[3,1280,320]{2,0,1:T(4,128)(2,1)}) %all-reduce.10.cloned.1.call-update) | async-done | bytes 2457616
  374.5 46.8 %all-reduce.8.cloned.1.call-done = bf16[512,1280]{1,0:T(8,128)(2,1)} async-done(((bf16[512,1280]{1,0:T(8,128)(2,1)}), bf16[512,1280]{1,0:T(8,128)(2,1)}) %all-reduce.8.cloned.1.call-update) | async-done | bytes 1310736 | tf_op jit(solution)/shard_map/psum | solution.py:187
  421.3 2.3 fusion.18
  423.6 2.2 fusion.16
  425.8 58.6 %all-gather.3.cloned.1.call-done = bf16[4096,1,1280]{2,0,1:T(8,128)(2,1)} async-done(((bf16[128,1,1280]{2,0,1:T(8,128)(2,1)}), bf16[4096,1,1280]{2,0,1:T(8,128)(2,1)}) %all-gather.3.cloned.1.call-update) | async-done | bytes 10485776 | tf_op jit(solution)/shard_map/all_gather | solution.py:131
  484.5 7.2 %gather_fusion = bf16[256,1280]{1,0:T(8,128)(2,1)S(1)} fusion(bf16[4096,1280]{1,0:T(8,128)(2,1)} %bitcast.235, s32[1024]{0:T(1024)S(1)} %pad_clamp_fusion), kind=kCustom, calls=%fused_computation | custom fusion | bytes 1311744 | tf_op jit(solution)/shard_map/jit(_take)/gather | solution.py:138
  (243 shorter events, 77.9 us)
Async XLA Ops:
  7.2 51.0 %copy-start = (bf16[320,1280]{1,0:T(8,128)(2,1)S(1)}, bf16[320,1280]{1,0:T(8,128)(2,1)}, u32[]{:S(2)}) copy-start(bf16[320,1280]{1,0:T(8,128)(2,1)} %param.12) | copy-start | bytes 2457604
  7.2 124.1 %all-reduce.6.cloned.1.call-start = ((), (), s32[]{:S(2)}) async-start(), calls=%async_computation.1 | async-start | bytes 5242880 | tf_op jit(solution)/shard_map/psum | solution.py:123
  11.9 18.3 %copy-start.31 = (bf16[512,320]{0,1:T(8,128)(2,1)}, bf16[512,320]{0,1:T(8,128)(2,1)S(1)}, u32[]{:S(2)}) copy-start(bf16[512,320]{0,1:T(8,128)(2,1)S(1)} %convolution_convert_fusion.13) | copy-start | bytes 983044
  12.0 14.4 %copy-start.64 = (s32[32]{0:T(128)S(1)}, s32[32]{0:T(128)}, u32[]{:S(2)}) copy-start(s32[32]{0:T(128)} %param.14) | copy-start | bytes 388
  14.2 18.1 %collective-permute-start.2 = (bf16[2,512,320]{1,2,0:T(8,128)(2,1)}, bf16[2,512,320]{1,2,0:T(8,128)(2,1)}, u32[]{:S(2)}, u32[]{:S(2)}) collective-permute-start(bf16[2,512,320]{1,2,0:T(8,128)(2,1)} %pad_maximum_fusion.1), channel_id=1, source_target_pairs={{0,8},{4,12},{8,16},{12,20},{16,24},{20,28},{24,32},{28,36},{32,40... | collective-permute-start | bytes 1966088 | tf_op jit(solution)/shard_map/ppermute | solution.py:18
  19.4 14.3 %collective-permute-start.1 = (bf16[2,512,320]{1,2,0:T(8,128)(2,1)}, bf16[2,512,320]{1,2,0:T(8,128)(2,1)}, u32[]{:S(2)}, u32[]{:S(2)}) collective-permute-start(bf16[2,512,320]{1,2,0:T(8,128)(2,1)} %pad_maximum_fusion.1), channel_id=1, source_target_pairs={{4,0},{8,4},{12,8},{16,12},{20,16},{24,20},{28,24},{32,28},{36,32}... | collective-permute-start | bytes 1966088 | tf_op jit(solution)/shard_map/ppermute | solution.py:18
  22.3 18.2 %collective-permute-start = (bf16[2,512,320]{1,2,0:T(8,128)(2,1)}, bf16[2,512,320]{1,2,0:T(8,128)(2,1)}, u32[]{:S(2)}, u32[]{:S(2)}) collective-permute-start(bf16[2,512,320]{1,2,0:T(8,128)(2,1)} %pad_maximum_fusion.1), channel_id=1, source_target_pairs={{0,4},{4,8},{8,12},{12,16},{16,20},{20,24},{24,28},{28,32},{32,36}... | collective-permute-start | bytes 1966088 | tf_op jit(solution)/shard_map/ppermute | solution.py:18
  25.0 19.0 %collective-permute-start.3 = (bf16[2,512,320]{1,2,0:T(8,128)(2,1)}, bf16[2,512,320]{1,2,0:T(8,128)(2,1)}, u32[]{:S(2)}, u32[]{:S(2)}) collective-permute-start(bf16[2,512,320]{1,2,0:T(8,128)(2,1)} %pad_maximum_fusion.1), channel_id=1, source_target_pairs={{8,0},{12,4},{16,8},{20,12},{24,16},{28,20},{32,24},{36,28},{40,32... | collective-permute-start | bytes 1966088 | tf_op jit(solution)/shard_map/ppermute | solution.py:18
  27.7 25.4 %copy-start.44 = (pred[512,512]{0,1:T(8,128)(4,1)}, pred[512,512]{0,1:T(8,128)(4,1)S(1)}, u32[]{:S(2)}) copy-start(pred[512,512]{0,1:T(8,128)(4,1)S(1)} %get-tuple-element.48) | copy-start | bytes 786436
  27.7 26.5 %copy-start.42 = (pred[512,512]{0,1:T(8,128)(4,1)}, pred[512,512]{0,1:T(8,128)(4,1)S(1)}, u32[]{:S(2)}) copy-start(pred[512,512]{0,1:T(8,128)(4,1)S(1)} %get-tuple-element.49) | copy-start | bytes 786436
  27.7 27.5 %copy-start.46 = (pred[512,512]{0,1:T(8,128)(4,1)}, pred[512,512]{0,1:T(8,128)(4,1)S(1)}, u32[]{:S(2)}) copy-start(pred[512,512]{0,1:T(8,128)(4,1)S(1)} %get-tuple-element.46) | copy-start | bytes 786436
  31.1 21.0 %copy-start.4 = (f32[4,512,512]{1,2,0:T(8,128)}, f32[4,512,512]{1,2,0:T(8,128)S(1)}, u32[]{:S(2)}) copy-start(f32[4,512,512]{1,2,0:T(8,128)S(1)} %get-tuple-element.58) | copy-start | bytes 12582916
  33.7 19.5 %copy-start.55 = (bf16[1,512,320]{1,2,0:T(8,128)(2,1)}, bf16[1,512,320]{1,2,0:T(8,128)(2,1)S(1)}, u32[]{:S(2)}) copy-start(bf16[1,512,320]{1,2,0:T(8,128)(2,1)S(1)} %get-tuple-element.42) | copy-start | bytes 983044
  35.0 21.3 %copy-start.50 = (bf16[1,512,320]{1,2,0:T(8,128)(2,1)}, bf16[1,512,320]{1,2,0:T(8,128)(2,1)S(1)}, u32[]{:S(2)}) copy-start(bf16[1,512,320]{1,2,0:T(8,128)(2,1)S(1)} %get-tuple-element.38) | copy-start | bytes 983044
  36.0 17.2 %copy-start.12 = (f32[4,512,512]{1,2,0:T(8,128)}, f32[4,512,512]{1,2,0:T(8,128)S(1)}, u32[]{:S(2)}) copy-start(f32[4,512,512]{1,2,0:T(8,128)S(1)} %get-tuple-element.54) | copy-start | bytes 12582916
  41.6 13.7 %copy-start.57 = (bf16[1,512,320]{1,2,0:T(8,128)(2,1)}, bf16[1,512,320]{1,2,0:T(8,128)(2,1)S(1)}, u32[]{:S(2)}) copy-start(bf16[1,512,320]{1,2,0:T(8,128)(2,1)S(1)} %get-tuple-element.40) | copy-start | bytes 983044
  42.5 13.8 %copy-start.7 = (f32[4,512,512]{1,2,0:T(8,128)}, f32[4,512,512]{1,2,0:T(8,128)S(1)}, u32[]{:S(2)}) copy-start(f32[4,512,512]{1,2,0:T(8,128)S(1)} %get-tuple-element.56) | copy-start | bytes 12582916
  43.5 11.8 %copy-start.16 = (f32[4,512,512]{1,2,0:T(8,128)}, f32[4,512,512]{1,2,0:T(8,128)S(1)}, u32[]{:S(2)}) copy-start(f32[4,512,512]{1,2,0:T(8,128)S(1)} %get-tuple-element.60) | copy-start | bytes 12582916
  60.5 197.0 %reduce-scatter.4.cloned.1.call-start = ((), (), s32[]{:S(2)}) async-start(), calls=%async_computation.5 | async-start | bytes 1013760
  138.4 40.4 %copy-start.21 = (bf16[512,1280]{1,0:T(8,128)(2,1)}, bf16[512,1280]{1,0:T(8,128)(2,1)S(1)}, u32[]{:S(2)}) copy-start(bf16[512,1280]{1,0:T(8,128)(2,1)S(1)} %get-tuple-element.36) | copy-start | bytes 3932164
  139.1 13.8 %copy-start.48 = (bf16[512,320]{0,1:T(8,128)(2,1)}, bf16[512,320]{0,1:T(8,128)(2,1)S(1)}, u32[]{:S(2)}) copy-start(bf16[512,320]{0,1:T(8,128)(2,1)S(1)} %convolution_convert_fusion.12) | copy-start | bytes 983044
  146.8 17.5 %copy-start.18 = (bf16[4,512,512]{1,2,0:T(8,128)(2,1)}, bf16[4,512,512]{1,2,0:T(8,128)(2,1)S(1)}, u32[]{:S(2)}) copy-start(bf16[4,512,512]{1,2,0:T(8,128)(2,1)S(1)} %multiply_convert_fusion.2) | copy-start | bytes 6291460
  155.0 22.0 %copy-start.19 = (bf16[4,512,512]{1,2,0:T(8,128)(2,1)}, bf16[4,512,512]{1,2,0:T(8,128)(2,1)S(1)}, u32[]{:S(2)}) copy-start(bf16[4,512,512]{1,2,0:T(8,128)(2,1)S(1)} %multiply_convert_fusion.4) | copy-start | bytes 6291460
  161.6 23.6 %collective-permute-start.4 = (bf16[2,512,4,80]{1,3,2,0:T(8,128)(2,1)}, bf16[2,512,4,80]{1,3,2,0:T(8,128)(2,1)}, u32[]{:S(2)}, u32[]{:S(2)}) collective-permute-start(bf16[2,512,4,80]{1,3,2,0:T(8,128)(2,1)} %pad_maximum_fusion.2), channel_id=1, source_target_pairs={{4,0},{8,4},{12,8},{16,12},{20,16},{24,20},{28,24},{32,28},{36,32}... | collective-permute-start | bytes 1966088 | tf_op jit(solution)/shard_map/ppermute | solution.py:18
  165.0 12.1 %copy-start.32 = (bf16[512,320]{0,1:T(8,128)(2,1)S(1)}, bf16[512,320]{0,1:T(8,128)(2,1)}, u32[]{:S(2)}) copy-start(bf16[512,320]{0,1:T(8,128)(2,1)} %copy-done.31) | copy-start | bytes 983044
  165.9 20.7 %collective-permute-start.5 = (bf16[2,512,4,80]{1,3,2,0:T(8,128)(2,1)}, bf16[2,512,4,80]{1,3,2,0:T(8,128)(2,1)}, u32[]{:S(2)}, u32[]{:S(2)}) collective-permute-start(bf16[2,512,4,80]{1,3,2,0:T(8,128)(2,1)} %pad_maximum_fusion.3), channel_id=1, source_target_pairs={{0,4},{4,8},{8,12},{12,16},{16,20},{20,24},{24,28},{28,32},{32,36}... | collective-permute-start | bytes 1966088 | tf_op jit(solution)/shard_map/ppermute | solution.py:18
  170.0 18.3 %collective-permute-start.6 = (bf16[2,512,4,80]{1,3,2,0:T(8,128)(2,1)}, bf16[2,512,4,80]{1,3,2,0:T(8,128)(2,1)}, u32[]{:S(2)}, u32[]{:S(2)}) collective-permute-start(bf16[2,512,4,80]{1,3,2,0:T(8,128)(2,1)} %pad_maximum_fusion.4), channel_id=1, source_target_pairs={{8,0},{12,4},{16,8},{20,12},{24,16},{28,20},{32,24},{36,28},{40,32... | collective-permute-start | bytes 1966088 | tf_op jit(solution)/shard_map/ppermute | solution.py:18
  172.2 17.9 %collective-permute-start.7 = (bf16[2,512,4,80]{1,3,2,0:T(8,128)(2,1)}, bf16[2,512,4,80]{1,3,2,0:T(8,128)(2,1)}, u32[]{:S(2)}, u32[]{:S(2)}) collective-permute-start(bf16[2,512,4,80]{1,3,2,0:T(8,128)(2,1)} %pad_maximum_fusion.5), channel_id=1, source_target_pairs={{0,8},{4,12},{8,16},{12,20},{16,24},{20,28},{24,32},{28,36},{32,40... | collective-permute-start | bytes 1966088 | tf_op jit(solution)/shard_map/ppermute | solution.py:18
  180.8 192.2 %all-reduce.10.cloned.1.call-start = ((), (), s32[]{:S(2)}) async-start(), calls=%async_computation.4 | async-start | bytes 7864320
  205.1 216.1 %all-reduce.8.cloned.1.call-start = ((), (), s32[]{:S(2)}) async-start(), calls=%async_computation.2 | async-start | bytes 2621440 | tf_op jit(solution)/shard_map/psum | solution.py:187
  211.3 273.2 %all-gather.3.cloned.1.call-start = ((), (), s32[]{:S(2)}) async-start(), calls=%async_computation.3 | async-start | bytes 10813440 | tf_op jit(solution)/shard_map/all_gather | solution.py:131
  214.8 208.8 %copy-start.22 = (bf16[512,1280]{1,0:T(8,128)(2,1)S(1)}, bf16[512,1280]{1,0:T(8,128)(2,1)}, u32[]{:S(2)}) copy-start(bf16[512,1280]{1,0:T(8,128)(2,1)} %copy-done.21) | copy-start | bytes 3932164
  (48 other events, 148.3 us)
Sparse Core Ops, SparseCore 0:
  60.7 70.5 all-reduce.5
  180.9 76.6 reduce-scatter.3
  261.4 111.5 all-reduce.9
  375.2 45.9 all-reduce.7
  424.2 60.2 all-gather.2
where the time goes:
time: 508 us; the launch traced here: 500 us
  waiting for transfers between devices  330 us (65%)
  matrix products  50.4 us (10%)
  other arithmetic  39.9 us (8%)
  local copies, waits for them, and re-layouts  38.7 us (8%)
  starting transfers between devices  24.1 us (5%)
  between operations  16.1 us (3%)
    unnamed x7, waiting for transfers between devices  151 us
    psum x1, waiting for transfers between devices, local(): layer_out = inputs32 + lax.psum(partial_out, 'section')  67.3 us
    all_gather x1, waiting for transfers between devices, local(): everything = lax.all_gather(my_part, 'seq', axis=0, tiled=True)  58.6 us
    psum x1, waiting for transfers between devices, local(): lax.psum(grad_normed_part.astype(jnp.bfloat16), 'section')  46.8 us
    ppermute x8, starting transfers between devices, passed_along(): lax.ppermute(value, axis, [(source, source + steps) for source in range(l...  23.9 us
    unnamed x137, local copies, waits for them, and re-layouts  11.4 us
  transfers between devices with their start and end apart: 13, of which 10 were waited for; matrix products, arithmetic and copies ran while one was open for 13% of the time, Pallas kernels for 0%

commit v1 on v0

v1 whole, which is shorter than its diff:
```python
import math

import jax
import jax.numpy as jnp
from jax import lax
from jax.experimental import pallas as pl
from jax.experimental.pallas import tpu as pltpu
from jax.sharding import PartitionSpec as P

HEADS = 16
EPS = 1e-06
HEAD_DIM = 80
PAIR = 160
BIG = -1e30
CHUNK = 256
BF16 = jnp.bfloat16
F32 = jnp.float32
MESH = pl.DeviceIdType.MESH
FACTOR = HEAD_DIM ** -0.5
LOG2E = 1.0 / math.log(2.0)
LN2 = math.log(2.0)


def dot_nn(left, right):
    return lax.dot_general(left, right, (((1,), (0,)), ((), ())), preferred_element_type=F32)


def dot_nt(left, right):
    return lax.dot_general(left, right, (((1,), (1,)), ((), ())), preferred_element_type=F32)


def place():
    section = lax.axis_index("section")
    seq = lax.axis_index("seq")
    return section, seq // 2, seq % 2


def shape(dims, dtype=BF16):
    return jax.ShapeDtypeStruct(dims, dtype)


def local_call(body, outs, ins, scratch=(), smem=0, limit=48):
    vmem = pl.BlockSpec(memory_space=pltpu.VMEM)
    scalar = pl.BlockSpec(memory_space=pltpu.SMEM)
    return pl.pallas_call(
        body,
        out_shape=outs,
        in_specs=[scalar] * smem + [vmem] * (len(ins) - smem),
        out_specs=[vmem] * len(outs),
        scratch_shapes=list(scratch),
        compiler_params=pltpu.CompilerParams(vmem_limit_bytes=limit << 20),
    )(*ins)


def exchange(number, outs, ins, peers, plan):
    with_peers = peers(*(0, 0, 0))
    count = len(with_peers)

    def body(*refs):
        in_refs, out_refs = refs[: len(ins)], refs[len(ins) : len(ins) + len(outs)]
        send_sems, recv_sems = refs[len(ins) + len(outs) :]
        spot = place()
        barrier = pltpu.get_barrier_semaphore()
        for peer in peers(*spot):
            pl.semaphore_signal(barrier, inc=1, device_id=peer, device_id_type=MESH)
        pl.semaphore_wait(barrier, count)
        copies = []
        for index, (source, target, device) in enumerate(plan(*spot, in_refs, out_refs)):
            if device is None:
                copy = pltpu.make_async_copy(source, target, recv_sems.at[index])
            else:
                copy = pltpu.make_async_remote_copy(
                    src_ref=source,
                    dst_ref=target,
                    send_sem=send_sems.at[index],
                    recv_sem=recv_sems.at[index],
                    device_id=device,
                    device_id_type=MESH,
                )
            copy.start()
            copies.append(copy)
        for copy in copies:
            copy.wait()

    return pl.pallas_call(
        body,
        out_shape=outs,
        in_specs=[pl.BlockSpec(memory_space=pl.ANY)] * len(ins),
        out_specs=[pl.BlockSpec(memory_space=pl.ANY)] * len(outs),
        scratch_shapes=[pltpu.SemaphoreType.DMA((20,)), pltpu.SemaphoreType.DMA((20,))],
        compiler_params=pltpu.CompilerParams(collective_id=number, has_side_effects=True),
    )(*ins)


def dev(chip, core, section):
    return (chip * 2 + core, section)


def around(chip, step):
    return (chip + step + 16) % 16


def project_body(tokens_ref, gain_ref, w_ref, qkv_ref, normed_t_ref, normed_ref):
    gain = gain_ref[...].astype(F32)
    for tile in range(4):
        rows = pl.ds(tile * 128, 128)
        values = tokens_ref[rows, :].astype(F32)
        centered = values - jnp.mean(values, axis=1, keepdims=True)
        inv = lax.rsqrt(jnp.mean(centered * centered, axis=1, keepdims=True) + EPS)
        normed = (centered * inv * gain).astype(BF16)
        normed_ref[rows, :] = normed
        normed_t_ref[:, rows] = normed.T
    for which in range(3):
        out = dot_nn(normed_ref[...], w_ref[which])
        if which == 0:
            out = out * (FACTOR * LOG2E)
        qkv_ref[which] = out.T.astype(BF16)


def membership(ends_ref, first, count):
    spots = first + lax.broadcasted_iota(jnp.int32, (32, count), 1)
    return (spots >= ends_ref[:, 0:1]) & (spots < ends_ref[:, 1:2])


def three_parts(row):
    high = row.astype(BF16)
    rest = row - high.astype(F32)
    middle = rest.astype(BF16)
    low = (rest - middle.astype(F32)).astype(BF16)
    return jnp.concatenate([high, middle, low, jnp.zeros((13, row.shape[1]), BF16)], axis=0)


def permutation(transposed):
    natural = lax.broadcasted_iota(jnp.int32, (512, 512), 1 if transposed else 0)
    moved = lax.broadcasted_iota(jnp.int32, (512, 512), 0 if transposed else 1)
    return jnp.where(natural == 4 * (moved % 128) + moved // 128, 1.0, 0.0).astype(BF16)


def forward_body(bounds_ref, ends_ref, q_ref, kv_ref, o_ref, op_ref, log_ref, qrow, kx, scores):
    chip = lax.axis_index("seq") // 2
    first = chip * 1024
    for head in range(2):
        feats = pl.ds(head * HEAD_DIM, HEAD_DIM)
        for block in range(4):
            lanes = pl.ds(block * 256, 256)
            inside = membership(ends_ref, first + block * 256, 256)
            joined = jnp.concatenate(
                [
                    q_ref[feats, lanes],
                    jnp.where(inside, 0.0, BIG).astype(BF16),
                    jnp.zeros((16, 256), BF16),
                ],
                axis=0,
            )
            qrow[head, lanes, :] = joined.T

    def build(chunk, carry):
        lanes = pl.ds(pl.multiple_of(chunk * CHUNK, CHUNK), CHUNK)
        inside = membership(ends_ref, first - 1024 + chunk * CHUNK, CHUNK)
        hot = jnp.where(inside, 1.0, 0.0).astype(BF16)
        for head in range(2):
            kx[head, 0:80, lanes] = kv_ref[0, pl.ds(head * HEAD_DIM, HEAD_DIM), lanes]
            kx[head, 80:112, lanes] = hot
            kx[head, 112:128, lanes] = jnp.zeros((16, CHUNK), BF16)
        return carry

    lax.fori_loop(bounds_ref[0, 0], bounds_ref[3, 1], build, 0)

    def tile_step(tile, carry):
        low, high = bounds_ref[tile, 0], bounds_ref[tile, 1]
        rows = pl.ds(pl.multiple_of(tile * 256, 256), 256)
        for head in range(2):
            feats = pl.ds(head * HEAD_DIM, HEAD_DIM)
            queries = qrow[head, rows, :]

            def score_step(chunk, top):
                lanes = pl.ds(pl.multiple_of(chunk * CHUNK, CHUNK), CHUNK)
                part = dot_nn(queries, kx[head, :, lanes])
                scores[:, lanes] = part
                return jnp.maximum(top, jnp.maximum(part[:, :128], part[:, 128:]))

            top = lax.fori_loop(low, high, score_step, jnp.full((256, 128), BIG, F32))
            top_col = jnp.max(top, axis=1, keepdims=True)
            top_row = jnp.max(top.T, axis=0, keepdims=True)

            def sum_step(chunk, carry):
                total, out = carry
                lanes = pl.ds(pl.multiple_of(chunk * CHUNK, CHUNK), CHUNK)
                probs = jnp.exp2(scores[:, lanes] - top_col)
                out = out + dot_nt(kv_ref[1, feats, lanes], probs.astype(BF16))
                return total + (probs[:, :128] + probs[:, 128:]), out

            total, out = lax.fori_loop(
                low,
                high,
                sum_step,
                (jnp.zeros((256, 128), F32), jnp.zeros((HEAD_DIM, 256), F32)),
            )
            total_row = jnp.sum(total.T, axis=0, keepdims=True)
            o_ref[feats, rows] = (out * (1.0 / total_row)).astype(BF16)
            log_ref[head : head + 1, rows] = top_row + jnp.log(total_row) * LOG2E
        return carry

    lax.fori_loop(0, 4, tile_step, 0)
    perm = permutation(False)
    for half in range(2):
        moved = dot_nn(o_ref[:, half * 512 : half * 512 + 512], perm).astype(BF16)
        for part in range(4):
            op_ref[half, part] = moved[:, part * 128 : part * 128 + 128]


def backward_body(
    bounds_ref, ends_ref, q_ref, kv_ref, o_ref, log_ref, gp_ref, dq_ref, dkv_ref,
    qrow, kx, vx, grow, gnat, acc,
):
    chip = lax.axis_index("seq") // 2
    first = chip * 1024
    back = permutation(True)
    for half in range(2):
        joined = jnp.concatenate([gp_ref[half, part] for part in range(4)], axis=1)
        gnat[:, half * 512 : half * 512 + 512] = dot_nn(joined, back).astype(BF16)
    for head in range(2):
        feats = pl.ds(head * HEAD_DIM, HEAD_DIM)
        for block in range(4):
            lanes = pl.ds(block * 256, 256)
            inside = membership(ends_ref, first + block * 256, 256)
            joined = jnp.concatenate(
                [
                    q_ref[feats, lanes],
                    jnp.where(inside, 0.0, BIG).astype(BF16),
                    three_parts(-log_ref[head : head + 1, lanes]),
                ],
                axis=0,
            )
            qrow[head, lanes, :] = joined.T
            grads = gnat[feats, lanes]
            delta = jnp.sum(
                grads.astype(F32) * o_ref[feats, lanes].astype(F32), axis=0, keepdims=True
            )
            joined = jnp.concatenate(
                [grads, three_parts(-delta), jnp.zeros((32, 256), BF16)], axis=0
            )
            grow[head, lanes, :] = joined.T

    ones = jnp.where(lax.broadcasted_iota(jnp.int32, (16, CHUNK), 0) < 3, 1.0, 0.0).astype(BF16)

    def build(chunk, carry):
        lanes = pl.ds(pl.multiple_of(chunk * CHUNK, CHUNK), CHUNK)
        inside = membership(ends_ref, first - 1024 + chunk * CHUNK, CHUNK)
        hot = jnp.where(inside, 1.0, 0.0).astype(BF16)
        for head in range(2):
            feats = pl.ds(head * HEAD_DIM, HEAD_DIM)
            kx[head, 0:80, lanes] = kv_ref[0, feats, lanes]
            kx[head, 80:112, lanes] = hot
            kx[head, 112:128, lanes] = ones
            vx[head, 0:80, lanes] = kv_ref[1, feats, lanes]
            vx[head, 80:96, lanes] = ones
            vx[head, 96:128, lanes] = jnp.zeros((32, CHUNK), BF16)
        return carry

    lax.fori_loop(bounds_ref[0, 0], bounds_ref[3, 1], build, 0)
    acc[...] = jnp.zeros_like(acc)

    def tile_step(tile, carry):
        low, high = bounds_ref[tile, 0], bounds_ref[tile, 1]
        rows = pl.ds(pl.multiple_of(tile * 256, 256), 256)
        for head in range(2):
            feats = pl.ds(head * HEAD_DIM, HEAD_DIM)
            queries, grads = qrow[head, rows, :], grow[head, rows, :]
            queries_t, grads_t = q_ref[feats, rows], gnat[feats, rows]

            def step(chunk, dq):
                lanes = pl.ds(pl.multiple_of(chunk * CHUNK, CHUNK), CHUNK)
                probs = jnp.exp2(dot_nn(queries, kx[head, :, lanes]))
                shifted = dot_nn(grads, vx[head, :, lanes])
                dscores = (probs * shifted).astype(BF16)
                acc[0, feats, lanes] += dot_nn(queries_t, dscores)
                acc[1, feats, lanes] += dot_nn(grads_t, probs.astype(BF16))
                return dq + dot_nt(kv_ref[0, feats, lanes], dscores)

            dq = lax.fori_loop(low, high, step, jnp.zeros((HEAD_DIM, 256), F32))
            dq_ref[feats, rows] = (dq * FACTOR).astype(BF16)
        return carry

    lax.fori_loop(0, 4, tile_step, 0)
    dkv_ref[0] = (acc[0] * LN2).astype(BF16)
    dkv_ref[1] = acc[1].astype(BF16)


def middle_body(
    att_ref, w_ref, tokens_ref, mgrad_ref, gain_ref, merged_ref, gl_ref, glt_ref, gat_ref
):
    section = lax.axis_index("section")
    row = lax.broadcasted_iota(jnp.int32, (128, 512), 0)
    column = lax.broadcasted_iota(jnp.int32, (128, 512), 1)
    chosen = jnp.where(column == 4 * row + section, 1.0, 0.0).astype(BF16)
    attended = att_ref[...].T
    layer = dot_nn(chosen, tokens_ref[...]) + dot_nn(attended, w_ref[...])
    gain = gain_ref[...].astype(F32)
    centered = layer - jnp.mean(layer, axis=1, keepdims=True)
    inv = lax.rsqrt(jnp.mean(centered * centered, axis=1, keepdims=True) + EPS)
    unit = centered * inv
    merged = (unit * gain).astype(BF16)
    row = lax.broadcasted_iota(jnp.int32, (128, 128), 0)
    column = lax.broadcasted_iota(jnp.int32, (128, 128), 1)
    order = jnp.where(column == 32 * (row % 4) + row // 4, 1.0, 0.0).astype(BF16)
    merged_ref[...] = dot_nn(order, merged).astype(BF16)
    scaled = mgrad_ref[...].astype(F32) * gain
    grad_layer = inv * (
        scaled
        - jnp.mean(scaled, axis=1, keepdims=True)
        - unit * jnp.mean(scaled * unit, axis=1, keepdims=True)
    )
    grad_layer = grad_layer.astype(BF16)
    gl_ref[...] = grad_layer
    glt_ref[...] = grad_layer.T
    gat_ref[...] = dot_nt(w_ref[...], grad_layer).astype(BF16)


def gradients_body(dq_ref, dkv_ref, w_ref, normed_t_ref, glt_ref, att_ref, gn_ref, p_ref, dj, djp, att, glt):
    for head in range(2):
        rows = pl.ds(head * PAIR, PAIR)
        dj[rows, :] = dq_ref[head]
        for which in range(2):
            total = dkv_ref[0, head, which].astype(F32) + dkv_ref[1, head, which].astype(F32)
            total = total + dkv_ref[2, head, which].astype(F32)
            dj[pl.ds(320 * (which + 1) + head * PAIR, PAIR), :] = total.astype(BF16)
        for part in range(4):
            att[rows, part * 128 : part * 128 + 128] = att_ref[head, part]
    for part in range(4):
        glt[:, part * 128 : part * 128 + 128] = glt_ref[part]
    djp[...] = dot_nn(dj[...], permutation(False)).astype(BF16)

    def step(index, carry):
        rows = pl.ds(pl.multiple_of(index * 256, 256), 256)
        total = dot_nn(w_ref[0, rows, :], djp[0:320, :])
        total = total + dot_nn(w_ref[1, rows, :], djp[320:640, :])
        total = total + dot_nn(w_ref[2, rows, :], djp[640:960, :])
        total = total.astype(BF16)
        for part in range(4):
            gn_ref[part, rows, :] = total[:, part * 128 : part * 128 + 128]
        normed = normed_t_ref[rows, :]
        p_ref[0, rows, :] = dot_nt(normed, dj[0:640, :]).astype(BF16)
        right = jnp.concatenate(
            [dot_nt(normed, dj[640:960, :]), dot_nt(glt[rows, :], att[...])], axis=1
        )
        p_ref[1, rows, :] = right.astype(BF16)
        return carry

    lax.fori_loop(0, 5, step, 0)


def first_norm_body(gn_ref, got_ref, tokens_ref, gain_ref, gl_ref, own_ref, other_ref, gx_ref, sum_ref):
    section = lax.axis_index("section")
    core = lax.axis_index("seq") % 2
    row = lax.broadcasted_iota(jnp.int32, (128, 512), 0)
    column = lax.broadcasted_iota(jnp.int32, (128, 512), 1)
    chosen = jnp.where(column == 4 * row + section, 1.0, 0.0).astype(BF16)
    values = dot_nn(chosen, tokens_ref[...])
    centered = values - jnp.mean(values, axis=1, keepdims=True)
    inv = lax.rsqrt(jnp.mean(centered * centered, axis=1, keepdims=True) + EPS)
    unit = centered * inv
    total = gn_ref[section].astype(F32) + got_ref[0].astype(F32)
    total = total + (got_ref[1].astype(F32) + got_ref[2].astype(F32))
    scaled = total.T * gain_ref[...].astype(F32)
    grad = inv * (
        scaled
        - jnp.mean(scaled, axis=1, keepdims=True)
        - unit * jnp.mean(scaled * unit, axis=1, keepdims=True)
    )
    gx_ref[...] = (gl_ref[...].astype(F32) + grad).astype(BF16)
    sum_ref[...] = (own_ref[core].astype(F32) + other_ref[...].astype(F32)).astype(BF16)


def sum_z_body(own_ref, got_ref, out_ref):
    z = (lax.axis_index("seq") // 2) % 4
    for y in range(4):
        total = own_ref[y, z].astype(F32) + got_ref[0, y].astype(F32)
        total = total + (got_ref[1, y].astype(F32) + got_ref[2, y].astype(F32))
        out_ref[y] = total.astype(BF16)


def sum_y_body(own_ref, got_ref, out_ref):
    y = lax.axis_index("seq") // 8
    total = own_ref[y].astype(F32) + got_ref[0].astype(F32)
    out_ref[...] = total + (got_ref[1].astype(F32) + got_ref[2].astype(F32))


def halo_peers(section, chip, core):
    found = [dev(chip, 1 - core, section)]
    for step in (1, -1):
        for other in (core, 1 - core):
            found.append(dev(around(chip, step), other, section))
    return found


def row_peers(section, chip, core):
    found = []
    for step in range(4):
        for turn in range(2):
            if step or turn:
                found.append(dev(chip, (core + turn) % 2, (section + step) % 4))
    return found


def section_peers(section, chip, core):
    return [dev(chip, core, (section + step) % 4) for step in range(1, 4)]


def partner(section, chip, core):
    return [dev(chip, 1 - core, section)]


def z_peers(section, chip, core):
    return [dev(chip // 4 * 4 + (chip + step) % 4, core, section) for step in range(1, 4)]


def y_peers(section, chip, core):
    return [dev((chip + 4 * step) % 16, core, section) for step in range(1, 4)]


def halo_plan(section, chip, core, ins, outs):
    (qkv,), (q, kv) = ins, outs
    own, other = pl.ds(core * PAIR, PAIR), pl.ds((1 - core) * PAIR, PAIR)
    mine = pl.ds(pl.multiple_of(core * 512, 512), 512)
    moves = []
    for step, base in ((1, 0), (-1, 2048)):
        lanes = pl.ds(pl.multiple_of(base + core * 512, 512), 512)
        for rows, target in ((own, core), (other, 1 - core)):
            moves.append(
                (qkv.at[1:3, rows, :], kv.at[:, :, lanes], dev(around(chip, step), target, section))
            )
    lanes = pl.ds(pl.multiple_of(1024 + core * 512, 512), 512)
    mate = dev(chip, 1 - core, section)
    moves.append((qkv.at[1:3, other, :], kv.at[:, :, lanes], mate))
    moves.append((qkv.at[0, other, :], q.at[:, mine], mate))
    moves.append((qkv.at[1:3, own, :], kv.at[:, :, lanes], None))
    moves.append((qkv.at[0, own, :], q.at[:, mine], None))
    return moves


def attended_plan(section, chip, core, ins, outs):
    (op,), (att, own) = ins, outs
    rows = pl.ds((section * 2 + core) * PAIR, PAIR)
    moves = []
    for step in (2, 1, 3, 0):
        for turn in range(2):
            to_section, to_core = (section + step) % 4, (core + turn) % 2
            device = dev(chip, to_core, to_section) if step or turn else None
            moves.append((op.at[to_core, to_section], att.at[rows, :], device))
    moves.append((op.at[1 - core], own.at[core], dev(chip, 1 - core, section)))
    moves.append((op.at[core], own.at[core], None))
    return moves


def grad_attended_plan(section, chip, core, ins, outs):
    (gat,), (gp,) = ins, outs
    moves = []
    for step in (2, 1, 3, 0):
        for turn in range(2):
            to_section, to_core = (section + step) % 4, (core + turn) % 2
            device = dev(chip, to_core, to_section) if step or turn else None
            rows = pl.ds((to_section * 2 + to_core) * PAIR, PAIR)
            moves.append((gat.at[rows, :], gp.at[core, section], device))
    return moves


def back_plan(section, chip, core, ins, outs):
    (dq, dkv, glt), (dq_all, dkv_all, glt_all) = ins, outs
    moves = []
    for step, base, slot in ((-1, 0, 0), (1, 2048, 1)):
        for target in (core, 1 - core):
            lanes = pl.ds(pl.multiple_of(base + target * 512, 512), 512)
            moves.append(
                (
                    dkv.at[:, :, lanes],
                    dkv_all.at[slot, core],
                    dev(around(chip, step), target, section),
                )
            )
    for target, device in ((1 - core, dev(chip, 1 - core, section)), (core, None)):
        lanes = pl.ds(pl.multiple_of(1024 + target * 512, 512), 512)
        moves.append((dkv.at[:, :, lanes], dkv_all.at[2, core], device))
        lanes = pl.ds(pl.multiple_of(target * 512, 512), 512)
        moves.append((dq.at[:, lanes], dq_all.at[core], device))
    for step in (2, 1, 3, 0):
        device = dev(chip, core, (section + step) % 4) if step else None
        moves.append((glt, glt_all.at[section], device))
    return moves


def sums_plan(section, chip, core, ins, outs):
    (gn, p), (got, other) = ins, outs
    moves = []
    for step in (2, 1, 3):
        to_section = (section + step) % 4
        moves.append((gn.at[to_section], got.at[step - 1], dev(chip, core, to_section)))
    moves.append((p.at[1 - core], other, dev(chip, 1 - core, section)))
    return moves


def rows_z_plan(section, chip, core, ins, outs):
    (gx, psum), (gx_all, got) = ins, outs
    moves = []
    for step in (2, 1, 3):
        z = (chip + step) % 4
        moves.append(
            (psum.at[:, z], got.at[step - 1], dev(chip // 4 * 4 + z, core, section))
        )
        moves.append((gx, gx_all.at[section], dev(chip, core, (section + step) % 4)))
    moves.append((gx, gx_all.at[section], None))
    return moves


def y_plan(section, chip, core, ins, outs):
    (psum,), (got,) = ins, outs
    moves = []
    for step in (2, 1, 3):
        to_chip = (chip + 4 * step) % 16
        moves.append((psum.at[to_chip // 4], got.at[step - 1], dev(to_chip, core, section)))
    return moves


def final_plan(section, chip, core, ins, outs):
    (total,), (both,) = ins, outs
    moves = []
    for target, device in ((1 - core, dev(chip, 1 - core, section)), (core, None)):
        moves.append((total.at[pl.ds(pl.multiple_of(target * 40, 8), 40), :], both.at[core], device))
    return moves


def local(
    tokens, norm_gain, w_qkv, w_out, merge_gain, seg_blocks, mb_sizes, mb_receiver, merged_grad
):
    section = lax.axis_index("section")
    seq = lax.axis_index("seq")
    chip = seq // 2
    w_full = lax.all_gather(w_out, "section", axis=0, tiled=True)
    ends = 64 * jnp.cumsum(seg_blocks)
    spans = jnp.stack([ends - 64 * seg_blocks, ends], axis=1)
    tile_first = chip * 1024 + 256 * jnp.arange(4, dtype=jnp.int32)[:, None]
    starts_in = jnp.max(jnp.where(spans[None, :, 0] <= tile_first, spans[None, :, 0], 0), axis=1)
    ends_in = jnp.min(jnp.where(ends[None, :] >= tile_first + 256, ends[None, :], 16384), axis=1)
    base = (chip - 1) * 1024
    bounds = jnp.stack(
        [(starts_in - base) // CHUNK, (ends_in - base + CHUNK - 1) // CHUNK], axis=1
    ).astype(jnp.int32)
    gain_one, gain_two = norm_gain.reshape(1, -1), merge_gain.reshape(1, -1)

    qkv, normed_t = local_call(
        project_body,
        [shape((3, 320, 512)), shape((1280, 512))],
        [tokens, gain_one, w_qkv],
        [pltpu.VMEM((512, 1280), BF16)],
    )
    q, kv = exchange(
        1, [shape((PAIR, 1024)), shape((2, PAIR, 3072))], [qkv], halo_peers, halo_plan
    )
    o, op, log_total = local_call(
        forward_body,
        [shape((PAIR, 1024)), shape((2, 4, PAIR, 128)), shape((2, 1024), F32)],
        [bounds, spans, q, kv],
        [
            pltpu.VMEM((2, 1024, 128), BF16),
            pltpu.VMEM((2, 128, 3072), BF16),
            pltpu.VMEM((256, 3072), F32),
        ],
        smem=1,
    )
    att, att_own = exchange(
        2, [shape((1280, 128)), shape((2, 4, PAIR, 128))], [op], row_peers, attended_plan
    )
    mgrad = lax.dynamic_slice_in_dim(merged_grad, section * 1280, 1280, 1)
    merged, grad_layer, glt, gat = local_call(
        middle_body,
        [shape((128, 1280)), shape((128, 1280)), shape((1280, 128)), shape((1280, 128))],
        [att, w_full, tokens, mgrad, gain_two],
    )
    (gp,) = exchange(3, [shape((2, 4, PAIR, 128))], [gat], row_peers, grad_attended_plan)
    dq, dkv = local_call(
        backward_body,
        [shape((PAIR, 1024)), shape((2, PAIR, 3072))],
        [bounds, spans, q, kv, o, log_total, gp],
        [
            pltpu.VMEM((2, 1024, 128), BF16),
            pltpu.VMEM((2, 128, 3072), BF16),
            pltpu.VMEM((2, 128, 3072), BF16),
            pltpu.VMEM((2, 1024, 128), BF16),
            pltpu.VMEM((PAIR, 1024), BF16),
            pltpu.VMEM((2, PAIR, 3072), F32),
        ],
        smem=1,
    )
    dq_all, dkv_all, glt_all = exchange(
        4,
        [shape((2, PAIR, 512)), shape((3, 2, 2, PAIR, 512)), shape((4, 1280, 128))],
        [dq, dkv, glt],
        lambda *spot: halo_peers(*spot) + section_peers(*spot),
        back_plan,
    )
    gn, p = local_call(
        gradients_body,
        [shape((4, 1280, 128)), shape((2, 1280, 640))],
        [dq_all, dkv_all, w_qkv, normed_t, glt_all, att_own],
        [
            pltpu.VMEM((960, 512), BF16),
            pltpu.VMEM((960, 512), BF16),
            pltpu.VMEM((320, 512), BF16),
            pltpu.VMEM((1280, 512), BF16),
        ],
    )
    gn_got, p_other = exchange(
        5,
        [shape((3, 1280, 128)), shape((1280, 640))],
        [gn, p],
        lambda *spot: section_peers(*spot) + partner(*spot),
        sums_plan,
    )
    gx, psum = local_call(
        first_norm_body,
        [shape((128, 1280)), shape((1280, 640))],
        [gn, gn_got, tokens, gain_one, grad_layer, p, p_other],
    )
    psum = psum.reshape(4, 4, 80, 640)
    gx_all, got_z = exchange(
        6,
        [shape((4, 128, 1280)), shape((3, 4, 80, 640))],
        [gx, psum],
        lambda *spot: section_peers(*spot) + z_peers(*spot),
        rows_z_plan,
    )
    (psum_z,) = local_call(sum_z_body, [shape((4, 80, 640))], [psum, got_z])
    (got_y,) = exchange(7, [shape((3, 80, 640))], [psum_z], y_peers, y_plan)
    (total,) = local_call(sum_y_body, [shape((80, 640), F32)], [psum_z, got_y])
    (both,) = exchange(8, [shape((2, 40, 640), F32)], [total], partner, final_plan)
    weights = both.transpose(1, 0, 2).reshape(40, 4, 320)
    grad_w_qkv = weights[:, :3].transpose(1, 0, 2)
    grad_w_out = weights[:, 3].T
    grad_x = gx_all.transpose(1, 0, 2).reshape(512, 1280)

    spread = lax.all_to_all(merged, "seq", 0, 0, tiled=True)
    receivers = jnp.arange(32, dtype=jnp.int32)
    mine = mb_receiver[None, :] == receivers[:, None]
    starts = jnp.cumsum(mb_sizes) - mb_sizes
    starts = jnp.sum(jnp.where(mine, starts[None, :], 0), axis=1)
    lives = jnp.sum(jnp.where(mine, mb_sizes[None, :], 0), axis=1)
    wanted = ((starts - seq + 31) // 32)[:, None] + jnp.arange(8, dtype=jnp.int32)[None, :]
    hot = wanted.reshape(256, 1) == jnp.arange(128, dtype=jnp.int32)[None, :]
    parcels = dot_nn(hot.astype(BF16), spread).astype(BF16)
    arrived = lax.all_to_all(parcels, "seq", 0, 0, tiled=True)
    my_start, my_live = starts[seq], lives[seq]
    slots = (receivers[:, None] - my_start) % 32 + 32 * jnp.arange(8, dtype=jnp.int32)[None, :]
    out_rows = jnp.arange(256, dtype=jnp.int32)[:, None]
    hot = (slots.reshape(1, 256) == out_rows) & (out_rows < my_live)
    delivered = dot_nn(hot.astype(BF16), arrived).astype(BF16)
    return (delivered, grad_x, grad_w_qkv, grad_w_out)


def solution(mesh):
    placed = (
        P("seq", None),
        P(),
        P(None, None, "section"),
        P("section", None),
        P(),
        P(),
        P(),
        P(),
        P("seq", None),
    )
    return jax.shard_map(
        local,
        mesh=mesh,
        in_specs=placed,
        out_specs=(
            P("seq", "section"),
            P("seq", None),
            P(None, "seq", "section"),
            P("section", "seq"),
        ),
        check_vma=False,
    )
```

time: 508 us -> 284 us (0.56); the launches traced: 500 us -> 283 us
  waiting for transfers between devices: 330 us -> 9.59 us
  Pallas kernels: 0 us -> 195 us
  matrix products: 50.4 us -> 4.55 us
  other arithmetic: 39.9 us -> 3.15 us
  starting transfers between devices: 24.1 us -> 11.1 us
  local copies, waits for them, and re-layouts: 38.7 us -> 45.2 us
    pallas_call x0 -> x16, Pallas kernels: none -> 195 us  [the longest x8 130 us: exchange(): pl.pallas_call(body, out_shape=outs, in_specs=[pl.BlockSpec(memory_space=...]
    unnamed x7 -> x1, waiting for transfers between devices: 151 us -> 0.68 us
    psum x2 -> x0, waiting for transfers between devices: 114 us -> none  [the longest x1 67.3 us: local(): layer_out = inputs32 + lax.psum(partial_out, 'section')]
    all_gather x1, waiting for transfers between devices: 58.6 us -> 0.02 us  [local(): w_full = lax.all_gather(w_out, 'section', axis=0, tiled=True)]
    dot_general x42 -> x2, matrix products: 50.4 us -> 4.55 us  [dot_nn(): lax.dot_general(left, right, (((1,), (0,)), ((), ())), preferred_element_...]
    ppermute x8 -> x0, starting transfers between devices: 23.9 us -> none  [passed_along(): lax.ppermute(value, axis, [(source, source + steps) for source in range(l...]
    unnamed x137 -> x77, local copies, waits for them, and re-layouts: 11.4 us -> 35.2 us
    reduce_sum x11 -> x1, other arithmetic: 17.1 us -> 0.11 us  [local(): lives = jnp.sum(jnp.where(mine, mb_sizes[None, :], 0), axis=1)]
  transfers between devices with their start and end apart: 13 -> 3, of which waited for: 10 -> 1; matrix products, arithmetic and copies ran while one was open for 13% -> 6% of each run, Pallas kernels for 0% -> 67%
where the time goes in v1:
time: 284 us; the launch traced here: 283 us
  Pallas kernels  195 us (69%)
  local copies, waits for them, and re-layouts  45.2 us (16%)
  between operations  14.5 us (5%)
  starting transfers between devices  11.1 us (4%)
  waiting for transfers between devices  9.59 us (3%)
  matrix products  4.55 us (2%)
  other arithmetic  3.15 us (1%)
    pallas_call x8, Pallas kernels, exchange(): pl.pallas_call(body, out_shape=outs, in_specs=[pl.BlockSpec(memory_space=...  130 us
    pallas_call x8, Pallas kernels, local_call(): pl.pallas_call(body, out_shape=outs, in_specs=[scalar] * smem + [vmem] *...  64.8 us
    unnamed x77, local copies, waits for them, and re-layouts  35.2 us
    all_to_all x1, waiting for transfers between devices, local(): spread = lax.all_to_all(merged, 'seq', 0, 0, tiled=True)  8.89 us
    all_to_all x1, starting transfers between devices, local(): spread = lax.all_to_all(merged, 'seq', 0, 0, tiled=True)  6.63 us
  transfers between devices with their start and end apart: 3, of which 1 were waited for; matrix products, arithmetic and copies ran while one was open for 6% of the time, Pallas kernels for 67%

profile of v1, /device:TPU:1, one launch (start us, length us, event | category | flops | bytes accessed | tf_op | source)
XLA Modules:
  0.0 282.8 jit_solution(10441919166850518089)
XLA Ops:
  10.1 5.4 %copy.71.w_ref = bf16[3,1280,320]{2,1,0:T(8,128)(2,1)} copy(bf16[3,1280,320]{1,2,0:T(8,128)(2,1)} %param.11) | data formatting | bytes 4915200 | tf_op args[2]
  15.5 4.7 %shard_map.120 = (bf16[3,320,512]{2,1,0:T(8,128)(2,1)S(1)}, bf16[1280,512]{1,0:T(8,128)(2,1)S(1)}) custom-call(bf16[512,1280]{1,0:T(8,128)(2,1)S(1)} %copy-done.1, bf16[1,1280]{1,0:T(2,128)(2,1)S(1)} %reshape.281.gain_ref, bf16[3,1280,320]{2,1,0:T(8,128)(2,1)} %copy.71.w_ref), custom_call_target="tpu_custom_call" | custom-call | tf_op jit(solution)/shard_map/pallas_call | solution.py:45
  22.3 24.0 %shard_map.121 = (bf16[160,1024]{1,0:T(8,128)(2,1)}, bf16[2,160,3072]{2,1,0:T(8,128)(2,1)}) custom-call(bf16[3,320,512]{2,1,0:T(8,128)(2,1)} %copy-done.20), custom_call_target="tpu_custom_call" | custom-call | tf_op jit(solution)/shard_map/pallas_call | solution.py:85
  46.5 1.5 copy-done.2
  49.0 19.7 %shard_map.122 = (bf16[160,1024]{1,0:T(8,128)(2,1)S(1)}, bf16[2,4,160,128]{3,2,1,0:T(8,128)(2,1)S(1)}, f32[2,1024]{1,0:T(2,128)S(1)}) custom-call(s32[4,2]{1,0:T(4,128)S(1)} %pad_add_fusion.1.bounds_ref, s32[32,2]{1,0:T(8,128)S(1)} %pad_add_fusion.ends_ref, bf16[160,1024]{1,0:T(8,128)(2,1)S(1)} %copy-done.15, bf16[2,160,3072]{2,1,0:T(8,128)(2,1)S(1)} %copy-done.2), custom_call_target="tpu_custom_call" | custom-call | tf_op jit(solution)/shard_map/pallas_call | solution.py:45
  70.2 10.7 %shard_map.123 = (bf16[1280,128]{1,0:T(8,128)(2,1)}, bf16[2,4,160,128]{3,2,1,0:T(8,128)(2,1)}) custom-call(bf16[2,4,160,128]{3,2,1,0:T(8,128)(2,1)} %copy-done.31), custom_call_target="tpu_custom_call" | custom-call | tf_op jit(solution)/shard_map/pallas_call | solution.py:85
  82.4 4.3 %shard_map.124 = (bf16[128,1280]{1,0:T(8,128)(2,1)S(1)}, bf16[128,1280]{1,0:T(8,128)(2,1)S(1)}, bf16[1280,128]{1,0:T(8,128)(2,1)S(1)}, bf16[1280,128]{1,0:T(8,128)(2,1)S(1)}) custom-call(bf16[1280,128]{1,0:T(8,128)(2,1)S(1)} %copy-done.23, bf16[1280,1280]{1,0:T(8,128)(2,1)} %all-gather.2.cloned.1.call-done.w_ref, bf16[512,1280]{1,0:T(8,128)(2,1)S(1)} %copy-done.1, ...), custom_call_target="tpu_custom_call" | custom-call | tf_op jit(solution)/shard_map/pallas_call | solution.py:45
  88.9 1.8 all_to_all.16
  90.7 6.6 %all-to-all-start = ((bf16[32,4,1280]{2,1,0:T(4,128)(2,1)}), bf16[32,4,1280]{2,1,0:T(4,128)(2,1)S(1)}, u32[]{:S(2)}, u32[]{:S(2)}) async-start(bf16[32,4,1280]{2,1,0:T(4,128)(2,1)} %all_to_all.16), calls=%async_computation | async-start | bytes 655360 | tf_op jit(solution)/shard_map/all_to_all | solution.py:641
  98.1 8.9 %all-to-all-done = bf16[32,4,1280]{2,1,0:T(4,128)(2,1)S(1)} async-done(((bf16[32,4,1280]{2,1,0:T(4,128)(2,1)}), bf16[32,4,1280]{2,1,0:T(4,128)(2,1)S(1)}, u32[]{:S(2)}, u32[]{:S(2)}) %all-to-all-start) | async-done | bytes 327712 | tf_op jit(solution)/shard_map/all_to_all | solution.py:641
  107.8 2.2 fusion
  110.1 4.4 %all-to-all-start.1 = ((bf16[32,8,1280]{2,1,0:T(8,128)(2,1)}), bf16[32,8,1280]{2,1,0:T(8,128)(2,1)}, u32[]{:S(2)}, u32[]{:S(2)}) async-start(bf16[32,8,1280]{2,1,0:T(8,128)(2,1)} %fusion), calls=%async_computation.1 | async-start | bytes 1310720 | tf_op jit(solution)/shard_map/all_to_all | solution.py:650
  116.6 8.4 %shard_map.125.gp_ref = bf16[2,4,160,128]{3,2,1,0:T(8,128)(2,1)} custom-call(bf16[1280,128]{1,0:T(8,128)(2,1)} %copy-done.29), custom_call_target="tpu_custom_call" | custom-call | tf_op jit(solution)/shard_map/pallas_call | solution.py:85
  125.0 1.5 copy-done.3
  128.5 21.3 %shard_map.126 = (bf16[160,1024]{1,0:T(8,128)(2,1)S(1)}, bf16[2,160,3072]{2,1,0:T(8,128)(2,1)S(1)}) custom-call(s32[4,2]{1,0:T(4,128)S(1)} %pad_add_fusion.1.bounds_ref, s32[32,2]{1,0:T(8,128)S(1)} %pad_add_fusion.ends_ref, bf16[160,1024]{1,0:T(8,128)(2,1)S(1)} %copy-done.16, bf16[2,160,3072]{2,1,0:T(8,128)(2,1)S(1)} %copy-done.3, ...), custom_call_target="tpu_custom_call" | custom-call | tf_op jit(solution)/shard_map/pallas_call | solution.py:45
  149.8 1.3 copy-done.10
  151.8 32.0 %shard_map.127 = (bf16[2,160,512]{2,1,0:T(8,128)(2,1)}, bf16[3,2,2,160,512]{4,3,2,1,0:T(8,128)(2,1)}, bf16[4,1280,128]{2,1,0:T(8,128)(2,1)}) custom-call(bf16[160,1024]{1,0:T(8,128)(2,1)} %copy-done.28, bf16[2,160,3072]{2,1,0:T(8,128)(2,1)} %copy-done.10, bf16[1280,128]{1,0:T(8,128)(2,1)} %copy-done.27), custom_call_target="tpu_custom_call" | custom-call | tf_op jit(solution)/shard_map/pallas_call | solution.py:85
  183.8 1.3 copy-done.12
  185.1 1.3 copy-done.13
  187.4 10.6 %shard_map.128 = (bf16[4,1280,128]{2,1,0:T(8,128)(2,1)S(1)}, bf16[2,1280,640]{2,1,0:T(8,128)(2,1)}) custom-call(bf16[2,160,512]{2,1,0:T(8,128)(2,1)S(1)} %copy-done.24, bf16[3,2,2,160,512]{4,3,2,1,0:T(8,128)(2,1)} %get-tuple-element.43.dkv_ref, bf16[3,1280,320]{2,1,0:T(8,128)(2,1)} %copy.71.w_ref, bf16[1280,512]{1,0:T(8,128)(2,1)S(1)} %copy-done.12, ...), custom_call_target="tpu_custom_call" | custom-call | tf_op jit(solution)/shard_map/pallas_call | solution.py:45
  199.1 18.3 %shard_map.129 = (bf16[3,1280,128]{2,1,0:T(8,128)(2,1)}, bf16[1280,640]{1,0:T(8,128)(2,1)}) custom-call(bf16[4,1280,128]{2,1,0:T(8,128)(2,1)} %copy-done.6, bf16[2,1280,640]{2,1,0:T(8,128)(2,1)} %get-tuple-element.48.refs_1_.own_ref), custom_call_target="tpu_custom_call" | custom-call | tf_op jit(solution)/shard_map/pallas_call | solution.py:85
  217.4 1.3 copy-done.7
  218.7 1.2 copy-done.19
  219.9 3.9 %shard_map.130 = (bf16[128,1280]{1,0:T(8,128)(2,1)S(1)}, bf16[1280,640]{1,0:T(8,128)(2,1)S(1)}) custom-call(bf16[4,1280,128]{2,1,0:T(8,128)(2,1)S(1)} %copy-done.7, bf16[3,1280,128]{2,1,0:T(8,128)(2,1)S(1)} %copy-done.19, bf16[512,1280]{1,0:T(8,128)(2,1)S(1)} %copy-done.1, bf16[1,1280]{1,0:T(2,128)(2,1)S(1)} %reshape.281.gain_ref, ...), custom_call_target="tpu_custom_call" | custom-call | tf_op jit(solution)/shard_map/pallas_call | solution.py:45
  223.8 1.2 copy-done.4
  225.8 22.6 %shard_map.131 = (bf16[4,128,1280]{2,1,0:T(8,128)(2,1)}, bf16[3,4,80,640]{3,2,1,0:T(8,128)(2,1)}) custom-call(bf16[128,1280]{1,0:T(8,128)(2,1)} %copy-done.32, bf16[4,4,80,640]{3,2,1,0:T(8,128)(2,1)} %bitcast.25), custom_call_target="tpu_custom_call" | custom-call | tf_op jit(solution)/shard_map/pallas_call | solution.py:85
  248.4 1.3 copy-done.17
  250.7 8.6 %shard_map.133.got_ref = bf16[3,80,640]{2,1,0:T(8,128)(2,1)} custom-call(bf16[4,80,640]{2,1,0:T(8,128)(2,1)} %copy-done.8), custom_call_target="tpu_custom_call" | custom-call | tf_op jit(solution)/shard_map/pallas_call | solution.py:85
  262.0 5.3 %shard_map.135 = f32[2,40,640]{2,1,0:T(8,128)} custom-call(f32[80,640]{1,0:T(8,128)} %copy-done.21), custom_call_target="tpu_custom_call" | custom-call | tf_op jit(solution)/shard_map/pallas_call | solution.py:85
  270.1 2.3 copy.73
  272.4 1.2 reshape.284
  273.7 2.3 convolution_convert_fusion
  (112 shorter events, 26.7 us)
Async XLA Ops:
  7.2 74.2 %copy-start = (bf16[128,5120]{1,0:T(8,128)(2,1)S(1)}, bf16[128,5120]{1,0:T(8,128)(2,1)}, u32[]{:S(2)}) copy-start(bf16[128,5120]{1,0:T(8,128)(2,1)} %param.17) | copy-start | bytes 3932164
  7.2 74.3 %all-gather.2.cloned.1.call-start = ((), (), s32[]{:S(2)}) async-start(), calls=%async_computation.2 | async-start | bytes 4096000 | tf_op jit(solution)/shard_map/all_gather | solution.py:538
  10.1 5.4 %copy-start.33 = (bf16[1280]{0:T(1024)(128)(2,1)S(1)}, bf16[1280]{0:T(1024)(128)(2,1)}, u32[]{:S(2)}) copy-start(bf16[1280]{0:T(1024)(128)(2,1)} %param.10) | copy-start | bytes 7684
  10.1 5.4 %copy-start.1 = (bf16[512,1280]{1,0:T(8,128)(2,1)S(1)}, bf16[512,1280]{1,0:T(8,128)(2,1)}, u32[]{:S(2)}) copy-start(bf16[512,1280]{1,0:T(8,128)(2,1)} %tokens_ref.5) | copy-start | bytes 3932164
  20.2 1.1 copy-start.11
  21.2 1.0 copy-start.20
  46.5 1.5 copy-start.2
  48.1 1.0 copy-start.15
  49.0 31.9 %copy-start.34 = (bf16[1280]{0:T(1024)(128)(2,1)S(1)}, bf16[1280]{0:T(1024)(128)(2,1)}, u32[]{:S(2)}) copy-start(bf16[1280]{0:T(1024)(128)(2,1)} %param.13) | copy-start | bytes 7684
  49.0 31.9 %copy-start.35 = (s32[32]{0:T(128)S(1)}, s32[32]{0:T(128)}, u32[]{:S(2)}) copy-start(s32[32]{0:T(128)} %param.15) | copy-start | bytes 388
  49.0 32.2 %copy-start.36 = (s32[32]{0:T(128)S(1)}, s32[32]{0:T(128)}, u32[]{:S(2)}) copy-start(s32[32]{0:T(128)} %param.16) | copy-start | bytes 388
  81.5 1.0 copy-start.23
  90.7 16.3 %all-to-all-start = ((bf16[32,4,1280]{2,1,0:T(4,128)(2,1)}), bf16[32,4,1280]{2,1,0:T(4,128)(2,1)S(1)}, u32[]{:S(2)}, u32[]{:S(2)}) async-start(bf16[32,4,1280]{2,1,0:T(4,128)(2,1)} %all_to_all.16), calls=%async_computation | async-start | bytes 655360 | tf_op jit(solution)/shard_map/all_to_all | solution.py:641
  107.8 17.1 %copy-start.16 = (bf16[160,1024]{1,0:T(8,128)(2,1)S(1)}, bf16[160,1024]{1,0:T(8,128)(2,1)}, u32[]{:S(2)}) copy-start(bf16[160,1024]{1,0:T(8,128)(2,1)} %get-tuple-element.31.q_ref) | copy-start | bytes 983044
  110.1 163.6 %all-to-all-start.1 = ((bf16[32,8,1280]{2,1,0:T(8,128)(2,1)}), bf16[32,8,1280]{2,1,0:T(8,128)(2,1)}, u32[]{:S(2)}, u32[]{:S(2)}) async-start(bf16[32,8,1280]{2,1,0:T(8,128)(2,1)} %fusion), calls=%async_computation.1 | async-start | bytes 1310720 | tf_op jit(solution)/shard_map/all_to_all | solution.py:650
  125.0 1.5 copy-start.3
  126.5 1.0 copy-start.14
  127.5 1.0 copy-start.26
  149.8 1.3 copy-start.10
  151.8 32.0 %copy-start.22 = (bf16[2,4,160,128]{3,2,1,0:T(8,128)(2,1)S(1)}, bf16[2,4,160,128]{3,2,1,0:T(8,128)(2,1)}, u32[]{:S(2)}) copy-start(bf16[2,4,160,128]{3,2,1,0:T(8,128)(2,1)} %get-tuple-element.46.att_ref) | copy-start | bytes 983044
  183.8 1.3 copy-start.12
  185.1 1.3 copy-start.13
  186.4 1.0 copy-start.24
  198.0 1.1 copy-start.6
  217.4 1.3 copy-start.7
  218.7 1.2 copy-start.19
  223.8 1.2 copy-start.4
  225.8 22.7 %copy-start.5 = (bf16[1280,640]{1,0:T(8,128)(2,1)S(1)}, bf16[1280,640]{1,0:T(8,128)(2,1)}, u32[]{:S(2)}) copy-start(bf16[1280,640]{1,0:T(8,128)(2,1)} %copy-done.4) | copy-start | bytes 4915204
  248.4 1.3 copy-start.17
  249.9 0.8 copy-start.8
  259.3 1.0 copy-start.9
  260.3 1.0 copy-start.18
  (8 other events, 5.8 us)
Sparse Core Ops, SparseCore 0:
  9.7 43.8 all-gather.1

commit v2 on v1

v2 whole, which is shorter than its diff:
```python
import math

import jax
import jax.numpy as jnp
from jax import lax
from jax.experimental import pallas as pl
from jax.experimental.pallas import tpu as pltpu
from jax.sharding import PartitionSpec as P

HEADS = 16
EPS = 1e-06
HEAD_DIM = 80
PAIR = 160
BIG = -1e30
CHUNK = 256
BF16 = jnp.bfloat16
F32 = jnp.float32
MESH = pl.DeviceIdType.MESH
FACTOR = HEAD_DIM ** -0.5
LOG2E = 1.0 / math.log(2.0)
LN2 = math.log(2.0)


def dot_nn(left, right):
    return lax.dot_general(left, right, (((1,), (0,)), ((), ())), preferred_element_type=F32)


def dot_nt(left, right):
    return lax.dot_general(left, right, (((1,), (1,)), ((), ())), preferred_element_type=F32)


def place():
    section = lax.axis_index("section")
    seq = lax.axis_index("seq")
    return section, seq // 2, seq % 2


def shape(dims, dtype=BF16):
    return jax.ShapeDtypeStruct(dims, dtype)


class Copies:
    def __init__(self, send_sems, recv_sems):
        self.send_sems, self.recv_sems, self.used = send_sems, recv_sems, 0

    def start(self, source, target, device):
        index = self.used
        self.used = index + 1
        if device is None:
            copy = pltpu.make_async_copy(source, target, self.recv_sems.at[index])
        else:
            copy = pltpu.make_async_remote_copy(
                src_ref=source,
                dst_ref=target,
                send_sem=self.send_sems.at[index],
                recv_sem=self.recv_sems.at[index],
                device_id=device,
                device_id_type=MESH,
            )
        copy.start()
        return copy


def wait_all(copies):
    for copy in copies:
        copy.wait()


def greet(peers):
    barrier = pltpu.get_barrier_semaphore()
    for peer in peers:
        pl.semaphore_signal(barrier, inc=1, device_id=peer, device_id_type=MESH)
    pl.semaphore_wait(barrier, len(peers))


def linked_call(number, body, outs, ins, scratch, copies, limit=48):
    vmem = pl.BlockSpec(memory_space=pltpu.VMEM)
    return pl.pallas_call(
        body,
        out_shape=outs,
        in_specs=[vmem] * len(ins),
        out_specs=[vmem] * len(outs),
        scratch_shapes=list(scratch)
        + [pltpu.SemaphoreType.DMA((copies,)), pltpu.SemaphoreType.DMA((copies,))],
        compiler_params=pltpu.CompilerParams(
            collective_id=number, has_side_effects=True, vmem_limit_bytes=limit << 20
        ),
    )(*ins)


def local_call(body, outs, ins, scratch=(), smem=0, limit=48):
    vmem = pl.BlockSpec(memory_space=pltpu.VMEM)
    scalar = pl.BlockSpec(memory_space=pltpu.SMEM)
    return pl.pallas_call(
        body,
        out_shape=outs,
        in_specs=[scalar] * smem + [vmem] * (len(ins) - smem),
        out_specs=[vmem] * len(outs),
        scratch_shapes=list(scratch),
        compiler_params=pltpu.CompilerParams(vmem_limit_bytes=limit << 20),
    )(*ins)


def dev(chip, core, section):
    return (chip * 2 + core, section)


def around(chip, step):
    return (chip + step + 16) % 16


def project_body(
    tokens_ref, gain_ref, w_ref, q_ref, kv_ref, normed_t_ref, normed_ref, out_ref, send, recv
):
    section, chip, core = place()
    copies = Copies(send, recv)
    gain = gain_ref[...].astype(F32)
    for tile in range(4):
        rows = pl.ds(tile * 128, 128)
        values = tokens_ref[rows, :].astype(F32)
        centered = values - jnp.mean(values, axis=1, keepdims=True)
        inv = lax.rsqrt(jnp.mean(centered * centered, axis=1, keepdims=True) + EPS)
        normed_ref[rows, :] = (centered * inv * gain).astype(BF16)
    own = pl.ds(pl.multiple_of(core * PAIR, 16), PAIR)
    other = pl.ds(pl.multiple_of((1 - core) * PAIR, 16), PAIR)
    mate = dev(chip, 1 - core, section)
    waits = []
    for which in (1, 2, 0):
        out = dot_nt(w_ref[which], normed_ref[...])
        if which == 0:
            out = out * (FACTOR * LOG2E)
        out_ref[which] = out.astype(BF16)
        if which == 1:
            greet(halo_peers(section, chip, core))
        if which:
            for step, base in ((1, 0), (-1, 2048)):
                lanes = pl.ds(pl.multiple_of(base + core * 512, 512), 512)
                for rows, target in ((own, core), (other, 1 - core)):
                    device = dev(around(chip, step), target, section)
                    waits.append(
                        copies.start(out_ref.at[which, rows, :], kv_ref.at[which - 1, :, lanes], device)
                    )
            lanes = pl.ds(pl.multiple_of(1024 + core * 512, 512), 512)
            target = kv_ref.at[which - 1, :, lanes]
        else:
            target = q_ref.at[:, pl.ds(pl.multiple_of(core * 512, 512), 512)]
        waits.append(copies.start(out_ref.at[which, other, :], target, mate))
        waits.append(copies.start(out_ref.at[which, own, :], target, None))
    for tile in range(4):
        rows = pl.ds(tile * 128, 128)
        normed_t_ref[:, rows] = normed_ref[rows, :].T
    wait_all(waits)


def membership(ends_ref, first, count):
    spots = first + lax.broadcasted_iota(jnp.int32, (32, count), 1)
    return (spots >= ends_ref[:, 0:1]) & (spots < ends_ref[:, 1:2])


def three_parts(row):
    high = row.astype(BF16)
    rest = row - high.astype(F32)
    middle = rest.astype(BF16)
    low = (rest - middle.astype(F32)).astype(BF16)
    return jnp.concatenate([high, middle, low, jnp.zeros((13, row.shape[1]), BF16)], axis=0)


def permutation(transposed):
    natural = lax.broadcasted_iota(jnp.int32, (512, 512), 1 if transposed else 0)
    moved = lax.broadcasted_iota(jnp.int32, (512, 512), 0 if transposed else 1)
    return jnp.where(natural == 4 * (moved % 128) + moved // 128, 1.0, 0.0).astype(BF16)


def forward_body(bounds_ref, ends_ref, q_ref, kv_ref, o_ref, op_ref, log_ref, qrow, kx, scores):
    chip = lax.axis_index("seq") // 2
    first = chip * 1024
    for head in range(2):
        feats = pl.ds(head * HEAD_DIM, HEAD_DIM)
        for block in range(4):
            lanes = pl.ds(block * 256, 256)
            inside = membership(ends_ref, first + block * 256, 256)
            joined = jnp.concatenate(
                [
                    q_ref[feats, lanes],
                    jnp.where(inside, 0.0, BIG).astype(BF16),
                    jnp.zeros((16, 256), BF16),
                ],
                axis=0,
            )
            qrow[head, lanes, :] = joined.T

    def build(chunk, carry):
        lanes = pl.ds(pl.multiple_of(chunk * CHUNK, CHUNK), CHUNK)
        inside = membership(ends_ref, first - 1024 + chunk * CHUNK, CHUNK)
        hot = jnp.where(inside, 1.0, 0.0).astype(BF16)
        for head in range(2):
            kx[head, 0:80, lanes] = kv_ref[0, pl.ds(head * HEAD_DIM, HEAD_DIM), lanes]
            kx[head, 80:112, lanes] = hot
            kx[head, 112:128, lanes] = jnp.zeros((16, CHUNK), BF16)
        return carry

    lax.fori_loop(bounds_ref[0, 0], bounds_ref[3, 1], build, 0)

    def tile_step(tile, carry):
        low, high = bounds_ref[tile, 0], bounds_ref[tile, 1]
        rows = pl.ds(pl.multiple_of(tile * 256, 256), 256)
        queries = [qrow[head, rows, :] for head in range(2)]

        def score_step(chunk, tops):
            lanes = pl.ds(pl.multiple_of(chunk * CHUNK, CHUNK), CHUNK)
            found = []
            for head in range(2):
                part = dot_nn(queries[head], kx[head, :, lanes])
                scores[head, :, lanes] = part
                found.append(jnp.maximum(tops[head], jnp.maximum(part[:, :128], part[:, 128:])))
            return tuple(found)

        start = jnp.full((256, 128), BIG, F32)
        tops = lax.fori_loop(low, high, score_step, (start, start))
        columns = [jnp.max(top, axis=1, keepdims=True) for top in tops]

        def sum_step(chunk, carry):
            lanes = pl.ds(pl.multiple_of(chunk * CHUNK, CHUNK), CHUNK)
            found = []
            for head in range(2):
                total, out = carry[head]
                feats = pl.ds(head * HEAD_DIM, HEAD_DIM)
                probs = jnp.exp2(scores[head, :, lanes] - columns[head])
                out = out + dot_nt(kv_ref[1, feats, lanes], probs.astype(BF16))
                found.append((total + (probs[:, :128] + probs[:, 128:]), out))
            return tuple(found)

        start = (jnp.zeros((256, 128), F32), jnp.zeros((HEAD_DIM, 256), F32))
        sums = lax.fori_loop(low, high, sum_step, (start, start))
        for head in range(2):
            total, out = sums[head]
            top_row = jnp.max(tops[head].T, axis=0, keepdims=True)
            total_row = jnp.sum(total.T, axis=0, keepdims=True)
            o_ref[pl.ds(head * HEAD_DIM, HEAD_DIM), rows] = (out * (1.0 / total_row)).astype(BF16)
            log_ref[head : head + 1, rows] = top_row + jnp.log(total_row) * LOG2E
        return carry

    lax.fori_loop(0, 4, tile_step, 0)
    perm = permutation(False)
    for half in range(2):
        moved = dot_nn(o_ref[:, half * 512 : half * 512 + 512], perm).astype(BF16)
        for part in range(4):
            op_ref[half, part] = moved[:, part * 128 : part * 128 + 128]


def backward_body(
    bounds_ref, ends_ref, q_ref, kv_ref, o_ref, log_ref, gp_ref, dq_ref, dkv_ref,
    qrow, kx, vx, grow, gnat, acc,
):
    chip = lax.axis_index("seq") // 2
    first = chip * 1024
    back = permutation(True)
    for half in range(2):
        joined = jnp.concatenate([gp_ref[half, part] for part in range(4)], axis=1)
        gnat[:, half * 512 : half * 512 + 512] = dot_nn(joined, back).astype(BF16)
    for head in range(2):
        feats = pl.ds(head * HEAD_DIM, HEAD_DIM)
        for block in range(4):
            lanes = pl.ds(block * 256, 256)
            inside = membership(ends_ref, first + block * 256, 256)
            joined = jnp.concatenate(
                [
                    q_ref[feats, lanes],
                    jnp.where(inside, 0.0, BIG).astype(BF16),
                    three_parts(-log_ref[head : head + 1, lanes]),
                ],
                axis=0,
            )
            qrow[head, lanes, :] = joined.T
            grads = gnat[feats, lanes]
            delta = jnp.sum(
                grads.astype(F32) * o_ref[feats, lanes].astype(F32), axis=0, keepdims=True
            )
            joined = jnp.concatenate(
                [grads, three_parts(-delta), jnp.zeros((32, 256), BF16)], axis=0
            )
            grow[head, lanes, :] = joined.T

    ones = jnp.where(lax.broadcasted_iota(jnp.int32, (16, CHUNK), 0) < 3, 1.0, 0.0).astype(BF16)

    def build(chunk, carry):
        lanes = pl.ds(pl.multiple_of(chunk * CHUNK, CHUNK), CHUNK)
        inside = membership(ends_ref, first - 1024 + chunk * CHUNK, CHUNK)
        hot = jnp.where(inside, 1.0, 0.0).astype(BF16)
        for head in range(2):
            feats = pl.ds(head * HEAD_DIM, HEAD_DIM)
            kx[head, 0:80, lanes] = kv_ref[0, feats, lanes]
            kx[head, 80:112, lanes] = hot
            kx[head, 112:128, lanes] = ones
            vx[head, 0:80, lanes] = kv_ref[1, feats, lanes]
            vx[head, 80:96, lanes] = ones
            vx[head, 96:128, lanes] = jnp.zeros((32, CHUNK), BF16)
        return carry

    lax.fori_loop(bounds_ref[0, 0], bounds_ref[3, 1], build, 0)
    acc[...] = jnp.zeros_like(acc)

    def tile_step(tile, carry):
        low, high = bounds_ref[tile, 0], bounds_ref[tile, 1]
        rows = pl.ds(pl.multiple_of(tile * 256, 256), 256)
        features = [pl.ds(head * HEAD_DIM, HEAD_DIM) for head in range(2)]

        def step(chunk, sums):
            lanes = pl.ds(pl.multiple_of(chunk * CHUNK, CHUNK), CHUNK)
            found = []
            for head in range(2):
                feats = features[head]
                probs = jnp.exp2(dot_nn(qrow[head, rows, :], kx[head, :, lanes]))
                shifted = dot_nn(grow[head, rows, :], vx[head, :, lanes])
                dscores = (probs * shifted).astype(BF16)
                acc[0, feats, lanes] += dot_nn(q_ref[feats, rows], dscores)
                acc[1, feats, lanes] += dot_nn(gnat[feats, rows], probs.astype(BF16))
                found.append(sums[head] + dot_nt(kv_ref[0, feats, lanes], dscores))
            return tuple(found)

        start = jnp.zeros((HEAD_DIM, 256), F32)
        sums = lax.fori_loop(low, high, step, (start, start))
        for head in range(2):
            dq_ref[features[head], rows] = (sums[head] * FACTOR).astype(BF16)
        return carry

    lax.fori_loop(0, 4, tile_step, 0)
    dkv_ref[0] = (acc[0] * LN2).astype(BF16)
    dkv_ref[1] = acc[1].astype(BF16)


def middle_body(
    op_ref, w_ref, tokens_ref, mgrad_ref, gain_ref,
    gl_ref, glt_ref, gp_ref, own_ref, table_ref,
    att, gat, packed, send, recv,
):
    section, chip, core = place()
    copies = Copies(send, recv)
    greet(row_peers(section, chip, core) + core_peers(section, chip, core))
    rows = pl.ds(pl.multiple_of((section * 2 + core) * PAIR, 16), PAIR)
    waits = []
    for step in (2, 1, 3, 0):
        for turn in range(2):
            to_section, to_core = (section + step) % 4, (core + turn) % 2
            device = dev(chip, to_core, to_section) if step or turn else None
            waits.append(copies.start(op_ref.at[to_core, to_section], att.at[rows, :], device))
    late = [
        copies.start(op_ref.at[1 - core], own_ref.at[core], dev(chip, 1 - core, section)),
        copies.start(op_ref.at[core], own_ref.at[core], None),
    ]
    row = lax.broadcasted_iota(jnp.int32, (128, 512), 0)
    column = lax.broadcasted_iota(jnp.int32, (128, 512), 1)
    chosen = jnp.where(column == 4 * row + section, 1.0, 0.0).astype(BF16)
    values = dot_nn(chosen, tokens_ref[...])
    gain = gain_ref[...].astype(F32)
    scaled = mgrad_ref[...].astype(F32) * gain
    scaled_mean = jnp.mean(scaled, axis=1, keepdims=True)
    row = lax.broadcasted_iota(jnp.int32, (128, 128), 0)
    column = lax.broadcasted_iota(jnp.int32, (128, 128), 1)
    order = jnp.where(column == 16 * (row % 8) + row // 8, 1.0, 0.0).astype(BF16)
    wait_all(waits)
    layer = values + dot_nn(att[...].T, w_ref[...])
    centered = layer - jnp.mean(layer, axis=1, keepdims=True)
    inv = lax.rsqrt(jnp.mean(centered * centered, axis=1, keepdims=True) + EPS)
    unit = centered * inv
    grad_layer = inv * (
        scaled - scaled_mean - unit * jnp.mean(scaled * unit, axis=1, keepdims=True)
    )
    grad_layer = grad_layer.astype(BF16)
    gat[...] = dot_nt(w_ref[...], grad_layer).astype(BF16)
    for step in (2, 1, 3, 0):
        for turn in range(2):
            to_section, to_core = (section + step) % 4, (core + turn) % 2
            device = dev(chip, to_core, to_section) if step or turn else None
            rows = pl.ds(pl.multiple_of((to_section * 2 + to_core) * PAIR, 16), PAIR)
            late.append(copies.start(gat.at[rows, :], gp_ref.at[core, section], device))
    moved = dot_nn(order, (unit * gain).astype(BF16))
    for chip_to in range(16):
        eight = moved[chip_to * 8 : chip_to * 8 + 8]
        packed[chip_to] = jnp.concatenate([eight[:, :640], eight[:, 640:]], axis=0).astype(BF16)
    for step in range(16):
        to_chip = (chip + step) % 16
        device = dev(to_chip, core, section) if step else None
        late.append(copies.start(packed.at[to_chip], table_ref.at[chip], device))
    gl_ref[...] = grad_layer
    glt_ref[...] = grad_layer.T
    wait_all(late)


def tail_body(
    dq_ref, dkv_ref, glt_ref, own_ref, table_ref, starts_ref, live_ref, gl_ref, tokens_ref,
    gain_ref, w_ref, normed_t_ref,
    delivered_ref, gx_ref, weights_ref,
    dq_in, dkv_in, dj, rows_ref, gn, gn_in, gx_own, gx_all, att, glt,
    parcels, arrived, p_mine, p_away, p_in,
    sum_a, sum_b, in_a, in_b, sub_a, sub_b, late_a, late_b, total, send, recv,
):
    section, chip, core = place()
    y, z = chip // 4, chip % 4
    copies = Copies(send, recv)
    mate = dev(chip, 1 - core, section)
    greet(plane_peers(section, chip, core) + section_peers(section, chip, core))
    back = []
    for half in range(2):
        waits = []
        for step, base, slot in ((-1, 0, 0), (1, 2048, 1)):
            for target in (core, 1 - core):
                lanes = pl.ds(pl.multiple_of(base + target * 512 + half * 256, 256), 256)
                device = dev(around(chip, step), target, section)
                waits.append(
                    copies.start(dkv_ref.at[:, :, lanes], dkv_in.at[half, slot, core], device)
                )
        for target, device in ((1 - core, mate), (core, None)):
            lanes = pl.ds(pl.multiple_of(1024 + target * 512 + half * 256, 256), 256)
            waits.append(copies.start(dkv_ref.at[:, :, lanes], dkv_in.at[half, 2, core], device))
            lanes = pl.ds(pl.multiple_of(target * 512 + half * 256, 256), 256)
            waits.append(copies.start(dq_ref.at[:, lanes], dq_in.at[half, core], device))
        back.append(waits)

    begin = starts_ref[...]
    block, offset = begin // 128, begin % 128
    first = 8 * ((block + 1 - core) // 2)
    first = first + jnp.where(block % 2 == core, (offset - chip + 15) // 16, 0)
    out_row = lax.broadcasted_iota(jnp.int32, (512, 256), 0)
    in_row = lax.broadcasted_iota(jnp.int32, (512, 256), 1)
    wanted = first + out_row % 8
    wanted = (wanted // 8) * 16 + wanted % 8 + 8 * ((out_row // 8) % 2)
    hot = jnp.where(in_row == wanted, 1.0, 0.0).astype(BF16)
    table = table_ref[...].reshape(256, 640)
    parcels[...] = dot_nn(hot, table).astype(BF16).reshape(32, 16, 640)

    for head in range(2):
        for part in range(4):
            att[head * PAIR : head * PAIR + PAIR, part * 128 : part * 128 + 128] = own_ref[head, part]
    for part in range(4):
        glt[:, part * 128 : part * 128 + 128] = glt_ref[part]

    row = lax.broadcasted_iota(jnp.int32, (256, 256), 0)
    column = lax.broadcasted_iota(jnp.int32, (256, 256), 1)
    by_part = jnp.where(column == 4 * (row % 64) + row // 64, 1.0, 0.0).astype(BF16)
    natural = jnp.where(row == 4 * (column % 64) + column // 64, 1.0, 0.0).astype(BF16)
    w_all = w_ref[...]
    sums = []
    for half in range(2):
        wait_all(back[half])
        lanes = pl.ds(half * 256, 256)
        for head in range(2):
            dj[head * PAIR : head * PAIR + PAIR, lanes] = dq_in[half, head]
            for which in range(2):
                grad = dkv_in[half, 0, head, which].astype(F32)
                grad = grad + dkv_in[half, 1, head, which].astype(F32)
                grad = grad + dkv_in[half, 2, head, which].astype(F32)
                start = 320 * (which + 1) + head * PAIR
                dj[start : start + PAIR, lanes] = grad.astype(BF16)
        rows_ref[...] = dot_nt(by_part, dj[:, lanes]).astype(BF16)
        gn[half] = dot_nn(rows_ref[...], w_all).astype(BF16).reshape(4, 64, 1280)
        waits = []
        for step in (2, 1, 3):
            to_section = (section + step) % 4
            device = dev(chip, core, to_section)
            waits.append(copies.start(gn.at[half, to_section], gn_in.at[half, step - 1], device))
        sums.append(waits)

    deliveries = []
    for step in range(16):
        for turn in range(2):
            to_chip, to_core = (chip + step) % 16, (core + turn) % 2
            device = dev(to_chip, to_core, section) if step or turn else None
            deliveries.append(
                copies.start(parcels.at[to_chip * 2 + to_core], arrived.at[chip * 2 + core], device)
            )

    def products(index, core_of):
        rows = pl.ds(index * 320, 320)
        normed = normed_t_ref[rows, :]
        if core_of == 0:
            return dot_nt(normed, dj[0:640, :])
        return jnp.concatenate(
            [dot_nt(normed, dj[640:960, :]), dot_nt(glt[rows, :], att[...])], axis=1
        )

    pairs = []
    for index in range(4):
        for core_of in range(2):
            @pl.when(core != core_of)
            def _():
                p_away[index] = products(index, core_of).astype(BF16).reshape(4, 80, 640)

        pairs.append(copies.start(p_away.at[index], p_in.at[index], mate))
    for index in range(4):
        for core_of in range(2):
            @pl.when(core == core_of)
            def _():
                p_mine[index] = products(index, core_of).reshape(4, 80, 640)

    gathers = []

    def finish_norm(half):
        row = lax.broadcasted_iota(jnp.int32, (64, 256), 0)
        column = lax.broadcasted_iota(jnp.int32, (64, 256), 1)
        chosen = jnp.where(column == 4 * row + section, 1.0, 0.0).astype(BF16)
        values = dot_nn(chosen, tokens_ref[half * 256 : half * 256 + 256, :])
        centered = values - jnp.mean(values, axis=1, keepdims=True)
        inv = lax.rsqrt(jnp.mean(centered * centered, axis=1, keepdims=True) + EPS)
        unit = centered * inv
        wait_all(sums[half])
        grad = gn[half, section].astype(F32) + gn_in[half, 0].astype(F32)
        grad = grad + (gn_in[half, 1].astype(F32) + gn_in[half, 2].astype(F32))
        scaled = grad * gain_ref[...].astype(F32)
        grad = inv * (
            scaled
            - jnp.mean(scaled, axis=1, keepdims=True)
            - unit * jnp.mean(scaled * unit, axis=1, keepdims=True)
        )
        grad = grad + gl_ref[half * 64 : half * 64 + 64, :].astype(F32)
        gx_own[half] = grad.astype(BF16)
        waits = []
        for step in (2, 1, 3, 0):
            device = dev(chip, core, (section + step) % 4) if step else None
            waits.append(copies.start(gx_own.at[half], gx_all.at[half, section], device))
        gathers.append(waits)

    finish_norm(0)
    firsts = [[], []]
    for index in range(4):
        pairs[index].wait()
        summed = (p_mine[index] + p_in[index].astype(F32)).astype(BF16)
        sum_a[index] = summed[:, :, :384]
        sum_b[index] = summed[:, :, 384:]
    for step in (2, 1, 3):
        to_z, to_y = (z + step) % 4, (y + step) % 4
        device = dev(y * 4 + to_z, core, section)
        firsts[0].append(copies.start(sum_a.at[:, to_z], in_a.at[step - 1], device))
        device = dev(to_y * 4 + z, core, section)
        firsts[1].append(copies.start(sum_b.at[to_y], in_b.at[step - 1], device))
    finish_norm(1)
    seconds = []
    wait_all(firsts[1])
    grad = sum_b[y].astype(F32) + in_b[0].astype(F32)
    sub_b[...] = (grad + (in_b[1].astype(F32) + in_b[2].astype(F32))).astype(BF16)
    for step in (2, 1, 3):
        to_z = (z + step) % 4
        device = dev(y * 4 + to_z, core, section)
        seconds.append(copies.start(sub_b.at[to_z], late_b.at[step - 1], device))
    wait_all(firsts[0])
    for index in range(4):
        grad = sum_a[index, z].astype(F32) + in_a[0, index].astype(F32)
        grad = grad + (in_a[1, index].astype(F32) + in_a[2, index].astype(F32))
        sub_a[index] = grad.astype(BF16)
    for step in (2, 1, 3):
        to_y = (y + step) % 4
        device = dev(to_y * 4 + z, core, section)
        seconds.append(copies.start(sub_a.at[to_y], late_a.at[step - 1], device))

    lane = lax.broadcasted_iota(jnp.int32, (1, 512), 1)
    from_chip, from_core, side, number = lane // 32, (lane // 16) % 2, (lane // 8) % 2, lane % 8
    begin, live = live_ref[0:1, :], live_ref[1:2, :]
    block, offset = begin // 128, begin % 128
    spot = 8 * ((block + 1 - from_core) // 2) + number
    spot = spot + jnp.where(block % 2 == from_core, (offset - from_chip + 15) // 16, 0)
    slot = (2 * (spot // 8) + from_core) * 128 + 16 * (spot % 8) + from_chip - begin
    out_row = lax.broadcasted_iota(jnp.int32, (256, 512), 0)
    taken = (out_row == slot) & (out_row < live)
    wait_all(deliveries)
    rows = arrived[...].reshape(512, 640)
    for which in range(2):
        hot = jnp.where(taken & (side == which), 1.0, 0.0).astype(BF16)
        delivered_ref[:, which * 640 : which * 640 + 640] = dot_nn(hot, rows).astype(BF16)

    wait_all(seconds)
    grad = sub_a[y].astype(F32) + late_a[0].astype(F32)
    total[:, :384] = grad + (late_a[1].astype(F32) + late_a[2].astype(F32))
    grad = sub_b[z].astype(F32) + late_b[0].astype(F32)
    total[:, 384:] = grad + (late_b[1].astype(F32) + late_b[2].astype(F32))
    lasts = []
    for target, device in ((1 - core, mate), (core, None)):
        rows = pl.ds(pl.multiple_of(target * 40, 8), 40)
        lasts.append(copies.start(total.at[rows, :], weights_ref.at[core], device))
    for half in range(2):
        wait_all(gathers[half])
        rows = gx_all[half].reshape(256, 1280)
        gx_ref[half * 256 : half * 256 + 256, :] = dot_nn(natural, rows).astype(BF16)
    wait_all(lasts)


def halo_peers(section, chip, core):
    found = [dev(chip, 1 - core, section)]
    for step in (1, -1):
        for other in (core, 1 - core):
            found.append(dev(around(chip, step), other, section))
    return found


def row_peers(section, chip, core):
    found = []
    for step in range(4):
        for turn in range(2):
            if step or turn:
                found.append(dev(chip, (core + turn) % 2, (section + step) % 4))
    return found


def section_peers(section, chip, core):
    return [dev(chip, core, (section + step) % 4) for step in range(1, 4)]


def core_peers(section, chip, core):
    return [dev((chip + step) % 16, core, section) for step in range(1, 16)]


def plane_peers(section, chip, core):
    found = [dev(chip, 1 - core, section)]
    for step in range(1, 16):
        for turn in range(2):
            found.append(dev((chip + step) % 16, (core + turn) % 2, section))
    return found


def local(
    tokens, norm_gain, w_qkv, w_out, merge_gain, seg_blocks, mb_sizes, mb_receiver, merged_grad
):
    section = lax.axis_index("section")
    seq = lax.axis_index("seq")
    chip = seq // 2
    w_full = lax.all_gather(w_out, "section", axis=0, tiled=True)
    w_rows = w_qkv.transpose(0, 2, 1)
    ends = 64 * jnp.cumsum(seg_blocks)
    spans = jnp.stack([ends - 64 * seg_blocks, ends], axis=1)
    tile_first = chip * 1024 + 256 * jnp.arange(4, dtype=jnp.int32)[:, None]
    starts_in = jnp.max(jnp.where(spans[None, :, 0] <= tile_first, spans[None, :, 0], 0), axis=1)
    ends_in = jnp.min(jnp.where(ends[None, :] >= tile_first + 256, ends[None, :], 16384), axis=1)
    base = (chip - 1) * 1024
    bounds = jnp.stack(
        [(starts_in - base) // CHUNK, (ends_in - base + CHUNK - 1) // CHUNK], axis=1
    ).astype(jnp.int32)
    mine = mb_receiver[None, :] == jnp.arange(32, dtype=jnp.int32)[:, None]
    starts = jnp.cumsum(mb_sizes) - mb_sizes
    starts = jnp.sum(jnp.where(mine, starts[None, :], 0), axis=1)
    lives = jnp.sum(jnp.where(mine, mb_sizes[None, :], 0), axis=1)
    start_rows = jnp.repeat(starts, 16).reshape(512, 1)
    here = jnp.broadcast_to(jnp.stack([starts[seq], lives[seq]])[:, None], (2, 512))
    gain_one, gain_two = norm_gain.reshape(1, -1), merge_gain.reshape(1, -1)
    mgrad = lax.dynamic_slice_in_dim(merged_grad, section * 1280, 1280, 1)

    q, kv, normed_t = linked_call(
        1,
        project_body,
        [shape((PAIR, 1024)), shape((2, PAIR, 3072)), shape((1280, 512))],
        [tokens, gain_one, w_rows],
        [pltpu.VMEM((512, 1280), BF16), pltpu.VMEM((3, 320, 512), BF16)],
        16,
    )
    o, op, log_total = local_call(
        forward_body,
        [shape((PAIR, 1024)), shape((2, 4, PAIR, 128)), shape((2, 1024), F32)],
        [bounds, spans, q, kv],
        [
            pltpu.VMEM((2, 1024, 128), BF16),
            pltpu.VMEM((2, 128, 3072), BF16),
            pltpu.VMEM((2, 256, 3072), F32),
        ],
        smem=1,
    )
    grad_layer, glt, gp, att_own, table = linked_call(
        2,
        middle_body,
        [
            shape((128, 1280)),
            shape((1280, 128)),
            shape((2, 4, PAIR, 128)),
            shape((2, 4, PAIR, 128)),
            shape((16, 16, 640)),
        ],
        [op, w_full, tokens, mgrad, gain_two],
        [
            pltpu.VMEM((1280, 128), BF16),
            pltpu.VMEM((1280, 128), BF16),
            pltpu.VMEM((16, 16, 640), BF16),
        ],
        34,
    )
    glt_all = lax.all_gather(glt, "section")
    dq, dkv = local_call(
        backward_body,
        [shape((PAIR, 1024)), shape((2, PAIR, 3072))],
        [bounds, spans, q, kv, o, log_total, gp],
        [
            pltpu.VMEM((2, 1024, 128), BF16),
            pltpu.VMEM((2, 128, 3072), BF16),
            pltpu.VMEM((2, 128, 3072), BF16),
            pltpu.VMEM((2, 1024, 128), BF16),
            pltpu.VMEM((PAIR, 1024), BF16),
            pltpu.VMEM((2, PAIR, 3072), F32),
        ],
        smem=1,
    )
    delivered, grad_x, weights = linked_call(
        3,
        tail_body,
        [shape((256, 1280)), shape((512, 1280)), shape((2, 40, 640), F32)],
        [
            dq, dkv, glt_all, att_own, table, start_rows, here, grad_layer, tokens,
            gain_one, w_rows.reshape(960, 1280), normed_t,
        ],
        [
            pltpu.VMEM((2, 2, PAIR, 256), BF16),
            pltpu.VMEM((2, 3, 2, 2, PAIR, 256), BF16),
            pltpu.VMEM((960, 512), BF16),
            pltpu.VMEM((256, 960), BF16),
            pltpu.VMEM((2, 4, 64, 1280), BF16),
            pltpu.VMEM((2, 3, 64, 1280), BF16),
            pltpu.VMEM((2, 64, 1280), BF16),
            pltpu.VMEM((2, 4, 64, 1280), BF16),
            pltpu.VMEM((320, 512), BF16),
            pltpu.VMEM((1280, 512), BF16),
            pltpu.VMEM((32, 16, 640), BF16),
            pltpu.VMEM((32, 16, 640), BF16),
            pltpu.VMEM((4, 4, 80, 640), F32),
            pltpu.VMEM((4, 4, 80, 640), BF16),
            pltpu.VMEM((4, 4, 80, 640), BF16),
            pltpu.VMEM((4, 4, 80, 384), BF16),
            pltpu.VMEM((4, 4, 80, 256), BF16),
            pltpu.VMEM((3, 4, 80, 384), BF16),
            pltpu.VMEM((3, 4, 80, 256), BF16),
            pltpu.VMEM((4, 80, 384), BF16),
            pltpu.VMEM((4, 80, 256), BF16),
            pltpu.VMEM((3, 80, 384), BF16),
            pltpu.VMEM((3, 80, 256), BF16),
            pltpu.VMEM((80, 640), F32),
        ],
        90,
    )
    sums = weights.transpose(1, 0, 2).reshape(40, 4, 320)
    grad_w_qkv = sums[:, :3].transpose(1, 0, 2)
    grad_w_out = sums[:, 3].T
    return (delivered, grad_x, grad_w_qkv, grad_w_out)


def solution(mesh):
    placed = (
        P("seq", None),
        P(),
        P(None, None, "section"),
        P("section", None),
        P(),
        P(),
        P(),
        P(),
        P("seq", None),
    )
    return jax.shard_map(
        local,
        mesh=mesh,
        in_specs=placed,
        out_specs=(
            P("seq", "section"),
            P("seq", None),
            P(None, "seq", "section"),
            P("section", "seq"),
        ),
        check_vma=False,
    )
```

time: 284 us -> 181 us (0.64)
  Pallas kernels: 195 us -> 132 us
  local copies, waits for them, and re-layouts: 45.2 us -> 29.7 us
  starting transfers between devices: 11.1 us -> 0.08 us
  waiting for transfers between devices: 9.59 us -> 0.72 us
  matrix products: 4.55 us -> 0 us
    pallas_call x8 -> x2, Pallas kernels: 64.8 us -> 25.1 us  [local_call(): pl.pallas_call(body, out_shape=outs, in_specs=[scalar] * smem + [vmem] *...]
    pallas_call x8 -> x3, Pallas kernels: 130 us -> 107 us  [linked_call(): pl.pallas_call(body, out_shape=outs, in_specs=[vmem] * len(ins), out_spec...]
    unnamed x77 -> x54, local copies, waits for them, and re-layouts: 35.2 us -> 23.6 us
    all_to_all x2 -> x0, starting transfers between devices: 11 us -> none  [the longest x1 6.63 us: local(): spread = lax.all_to_all(merged, 'seq', 0, 0, tiled=True)]
    all_to_all x2 -> x0, waiting for transfers between devices: 8.89 us -> none  [the longest x1 8.89 us: local(): spread = lax.all_to_all(merged, 'seq', 0, 0, tiled=True)]
    dot_general x2 -> x0, matrix products: 4.55 us -> none  [dot_nn(): lax.dot_general(left, right, (((1,), (0,)), ((), ())), preferred_element_...]
  transfers between devices with their start and end apart: 3 -> 2, of which waited for: 1 -> 0; matrix products, arithmetic and copies ran while one was open for 6% -> 4% of each run, Pallas kernels for 67% -> 28%
where the time goes in v2:
time: 181 us; the launch traced here: 180 us
  Pallas kernels  132 us (73%)
  local copies, waits for them, and re-layouts  29.7 us (16%)
  between operations  14.3 us (8%)
  other arithmetic  3.04 us (2%)
    pallas_call x3, Pallas kernels, linked_call(): pl.pallas_call(body, out_shape=outs, in_specs=[vmem] * len(ins), out_spec...  107 us
    pallas_call x2, Pallas kernels, local_call(): pl.pallas_call(body, out_shape=outs, in_specs=[scalar] * smem + [vmem] *...  25.1 us
    unnamed x54, local copies, waits for them, and re-layouts  23.6 us
  transfers between devices with their start and end apart: 2, of which 0 were waited for; matrix products, arithmetic and copies ran while one was open for 4% of the time, Pallas kernels for 28%

profile of v2, /device:TPU:1, one launch (start us, length us, event | category | flops | bytes accessed | tf_op | source)
XLA Modules:
  0.0 180.2 jit_solution(7793102834252603448)
XLA Ops:
  8.0 0.7 copy.54
  11.6 1.3 copy-done.1
  12.9 26.0 %shard_map.120 = (bf16[160,1024]{1,0:T(8,128)(2,1)S(1)}, bf16[2,160,3072]{2,1,0:T(8,128)(2,1)S(1)}, bf16[1280,512]{1,0:T(8,128)(2,1)S(1)}) custom-call(bf16[512,1280]{1,0:T(8,128)(2,1)S(1)} %copy-done.1, bf16[1,1280]{1,0:T(2,128)(2,1)S(1)} %reshape.192.gain_ref, bf16[3,320,1280]{2,1,0:T(8,128)(2,1)} %bitcast.21), custom_call_target="tpu_custom_call" | custom-call | tf_op jit(solution)/shard_map/pallas_call | solution.py:78
  39.0 1.0 copy-done.6
  40.2 11.3 %shard_map.121 = (bf16[160,1024]{1,0:T(8,128)(2,1)S(1)}, bf16[2,4,160,128]{3,2,1,0:T(8,128)(2,1)S(1)}, f32[2,1024]{1,0:T(2,128)S(1)}) custom-call(s32[4,2]{1,0:T(4,128)S(1)} %pad_add_fusion.1.bounds_ref, s32[32,2]{1,0:T(8,128)S(1)} %pad_add_fusion.ends_ref, bf16[160,1024]{1,0:T(8,128)(2,1)S(1)} %get-tuple-element.20.q_ref, ...), custom_call_target="tpu_custom_call" | custom-call | tf_op jit(solution)/shard_map/pallas_call | solution.py:94
  51.5 1.3 copy-done.3
  52.8 0.7 copy-done.16
  53.5 0.7 copy-done.18
  54.3 1.0 copy-done.17
  55.3 23.6 %shard_map.122 = (bf16[128,1280]{1,0:T(8,128)(2,1)S(1)}, bf16[1280,128]{1,0:T(8,128)(2,1)S(1)}, bf16[2,4,160,128]{3,2,1,0:T(8,128)(2,1)S(1)}, bf16[2,4,160,128]{...) custom-call(bf16[2,4,160,128]{3,2,1,0:T(8,128)(2,1)S(1)} %copy-done.17, bf16[1280,1280]{1,0:T(8,128)(2,1)} %all-gather.4.cloned.1.call-done.w_ref, ...), custom_call_target="tpu_custom_call" | custom-call | tf_op jit(solution)/shard_map/pallas_call | solution.py:78
  78.8 0.7 copy-done.8
  79.6 0.7 copy-done.10
  80.3 0.7 copy-done.12
  81.0 0.7 copy-done.20
  81.7 0.7 copy-done.22
  84.3 1.4 pad_add_fusion.2
  85.7 1.5 copy-done.4
  87.2 1.0 copy-done.19
  88.2 1.0 copy-done.21
  89.2 13.8 %shard_map.123 = (bf16[160,1024]{1,0:T(8,128)(2,1)S(1)}, bf16[2,160,3072]{2,1,0:T(8,128)(2,1)S(1)}) custom-call(s32[4,2]{1,0:T(4,128)S(1)} %pad_add_fusion.1.bounds_ref, s32[32,2]{1,0:T(8,128)S(1)} %pad_add_fusion.ends_ref, bf16[160,1024]{1,0:T(8,128)(2,1)S(1)} %get-tuple-element.20.q_ref, bf16[2,160,3072]{2,1,0:T(8,128)(2,1)S(1)} %copy-done.4, ...), custom_call_target="tpu_custom_call" | custom-call | tf_op jit(solution)/shard_map/pallas_call | solution.py:94
  103.0 1.3 copy-done.5
  104.2 0.7 copy-done.14
  105.0 1.3 copy-done.7
  106.3 1.0 copy-done.9
  107.3 1.0 copy-done.11
  108.3 1.0 copy-done.13
  109.3 1.0 copy-done.15
  110.2 57.8 %shard_map.124 = (bf16[256,1280]{1,0:T(8,128)(2,1)S(1)}, bf16[512,1280]{1,0:T(8,128)(2,1)S(1)}, f32[2,40,640]{2,1,0:T(8,128)S(1)}) custom-call(bf16[160,1024]{1,0:T(8,128)(2,1)S(1)} %copy-done.15, bf16[2,160,3072]{2,1,0:T(8,128)(2,1)} %copy-done.5, bf16[4,1280,128]{2,1,0:T(8,128)(2,1)S(1)} %bitcast.19, bf16[2,4,160,128]{3,2,1,0:T(8,128)(2,1)S(1)} %copy-done.11, ...), custom_call_target="tpu_custom_call" | custom-call | tf_op jit(solution)/shard_map/pallas_call | solution.py:78
  168.0 0.8 copy.66
  168.8 1.2 reshape.197
  171.5 0.8 copy.73
  172.3 1.1 copy.74
  (67 shorter events, 7.2 us)
Async XLA Ops:
  7.2 47.1 %copy-start = (bf16[128,5120]{1,0:T(8,128)(2,1)S(1)}, bf16[128,5120]{1,0:T(8,128)(2,1)}, u32[]{:S(2)}) copy-start(bf16[128,5120]{1,0:T(8,128)(2,1)} %param.17) | copy-start | bytes 3932164
  7.2 47.1 %all-gather.4.cloned.1.call-start = ((), (), s32[]{:S(2)}) async-start(), calls=%async_computation | async-start | bytes 4096000 | tf_op jit(solution)/shard_map/all_gather | solution.py:625
  7.9 97.0 %all-gather.6.cloned.1.call-start = ((), (), s32[]{:S(2)}) async-start(), calls=%async_computation.1 | async-start | bytes 1638400 | tf_op jit(solution)/shard_map/all_gather | solution.py:682
  11.6 1.3 copy-start.1
  39.0 1.1 copy-start.6
  40.2 14.1 %copy-start.2 = (bf16[512,1280]{1,0:T(8,128)(2,1)S(1)}, bf16[512,1280]{1,0:T(8,128)(2,1)}, u32[]{:S(2)}) copy-start(bf16[512,1280]{1,0:T(8,128)(2,1)} %tokens_ref.5) | copy-start | bytes 3932164
  51.5 1.3 copy-start.3
  52.8 0.7 copy-start.16
  53.5 0.7 copy-start.18
  54.3 1.0 copy-start.17
  55.3 27.2 %copy-start.23 = (s32[32]{0:T(128)S(1)}, s32[32]{0:T(128)}, u32[]{:S(2)}) copy-start(s32[32]{0:T(128)} %param.15) | copy-start | bytes 388
  55.3 27.5 %copy-start.24 = (s32[32]{0:T(128)S(1)}, s32[32]{0:T(128)}, u32[]{:S(2)}) copy-start(s32[32]{0:T(128)} %param.16) | copy-start | bytes 388
  78.8 0.7 copy-start.8
  79.5 0.7 copy-start.10
  80.3 0.7 copy-start.12
  81.0 0.7 copy-start.20
  81.7 0.7 copy-start.22
  85.7 1.5 copy-start.4
  87.2 1.0 copy-start.19
  88.2 1.0 copy-start.21
  102.9 1.3 copy-start.5
  104.2 0.7 copy-start.14
  105.0 1.3 copy-start.7
  106.3 1.0 copy-start.9
  107.3 1.0 copy-start.11
  108.3 1.0 copy-start.13
  109.3 1.0 copy-start.15
Sparse Core Ops, SparseCore 0:
  9.7 43.8 all-gather.3
  82.6 22.2 all-gather.5

commit v3 on v2

--- a/solution.py
+++ b/solution.py
@@ -13,6 +13,7 @@
 PAIR = 160
 BIG = -1e30
 CHUNK = 256
+SAFE = 60.0
 BF16 = jnp.bfloat16
 F32 = jnp.float32
 MESH = pl.DeviceIdType.MESH
@@ -73,32 +74,22 @@
     pl.semaphore_wait(barrier, len(peers))
 
 
-def linked_call(number, body, outs, ins, scratch, copies, limit=48):
-    vmem = pl.BlockSpec(memory_space=pltpu.VMEM)
+VMEM = pl.BlockSpec(memory_space=pltpu.VMEM)
+SMEM = pl.BlockSpec(memory_space=pltpu.SMEM)
+HBM = pl.BlockSpec(memory_space=pltpu.HBM)
+
+
+def call(body, outs, ins, scratch=(), copies=0, number=None, limit=14):
+    more = {} if number is None else {"collective_id": number, "has_side_effects": True}
+    semaphores = [pltpu.SemaphoreType.DMA((copies,))] * (0 if not copies else 1 if number is None else 2)
     return pl.pallas_call(
         body,
-        out_shape=outs,
-        in_specs=[vmem] * len(ins),
-        out_specs=[vmem] * len(outs),
-        scratch_shapes=list(scratch)
-        + [pltpu.SemaphoreType.DMA((copies,)), pltpu.SemaphoreType.DMA((copies,))],
-        compiler_params=pltpu.CompilerParams(
-            collective_id=number, has_side_effects=True, vmem_limit_bytes=limit << 20
-        ),
-    )(*ins)
-
-
-def local_call(body, outs, ins, scratch=(), smem=0, limit=48):
-    vmem = pl.BlockSpec(memory_space=pltpu.VMEM)
-    scalar = pl.BlockSpec(memory_space=pltpu.SMEM)
-    return pl.pallas_call(
-        body,
-        out_shape=outs,
-        in_specs=[scalar] * smem + [vmem] * (len(ins) - smem),
-        out_specs=[vmem] * len(outs),
-        scratch_shapes=list(scratch),
-        compiler_params=pltpu.CompilerParams(vmem_limit_bytes=limit << 20),
-    )(*ins)
+        out_shape=[array for _, array in outs],
+        in_specs=[place for place, _ in ins],
+        out_specs=[place for place, _ in outs],
+        scratch_shapes=list(scratch) + semaphores,
+        compiler_params=pltpu.CompilerParams(vmem_limit_bytes=limit << 20, **more),
+    )(*[array for _, array in ins])
 
 
 def dev(chip, core, section):
@@ -110,11 +101,28 @@
 
 
 def project_body(
-    tokens_ref, gain_ref, w_ref, q_ref, kv_ref, normed_t_ref, normed_ref, out_ref, send, recv
+    tokens_hbm, gain_ref, w_hbm, w_out_hbm, q_ref, kv_ref, normed_t_hbm, w_full,
+    tokens_ref, w_ref, normed_ref, normed_t_ref, out_ref, send, recv,
 ):
     section, chip, core = place()
     copies = Copies(send, recv)
-    gain = gain_ref[...].astype(F32)
+    load_tokens = copies.start(tokens_hbm, tokens_ref, None)
+    load_w = copies.start(w_hbm, w_ref, None)
+    greet(halo_peers(section, chip, core) + section_peers(section, chip, core)[::2])
+    mate = dev(chip, 1 - core, section)
+    ahead, behind = (section + 1) % 4, (section + 3) % 4
+    ahead_dev, behind_dev = dev(chip, core, ahead), dev(chip, core, behind)
+
+    def w_rows(owner, start, count):
+        return w_full.at[pl.ds(pl.multiple_of(owner * 320 + core * PAIR + start, 16), count), :]
+
+    mine = w_out_hbm.at[pl.ds(pl.multiple_of(core * PAIR, 16), PAIR), :]
+    to_ahead = copies.start(mine, w_rows(section, 0, PAIR), ahead_dev)
+    to_behind = copies.start(mine, w_rows(section, 0, PAIR), behind_dev)
+    keep = w_full.at[pl.ds(pl.multiple_of(section * 320, 16), 320), :]
+    waits = [copies.start(w_out_hbm, keep, None)]
+    load_tokens.wait()
+    gain = gain_ref[...].reshape(1, 1280).astype(F32)
     for tile in range(4):
         rows = pl.ds(tile * 128, 128)
         values = tokens_ref[rows, :].astype(F32)
@@ -123,15 +131,12 @@
         normed_ref[rows, :] = (centered * inv * gain).astype(BF16)
     own = pl.ds(pl.multiple_of(core * PAIR, 16), PAIR)
     other = pl.ds(pl.multiple_of((1 - core) * PAIR, 16), PAIR)
-    mate = dev(chip, 1 - core, section)
-    waits = []
+    load_w.wait()
     for which in (1, 2, 0):
         out = dot_nt(w_ref[which], normed_ref[...])
         if which == 0:
             out = out * (FACTOR * LOG2E)
         out_ref[which] = out.astype(BF16)
-        if which == 1:
-            greet(halo_peers(section, chip, core))
         if which:
             for step, base in ((1, 0), (-1, 2048)):
                 lanes = pl.ds(pl.multiple_of(base + core * 512, 512), 512)
@@ -149,12 +154,46 @@
     for tile in range(4):
         rows = pl.ds(tile * 128, 128)
         normed_t_ref[:, rows] = normed_ref[rows, :].T
+    waits.append(copies.start(normed_t_ref, normed_t_hbm, None))
+
+    to_ahead.wait()
+    relay = [copies.start(w_rows(behind, 0, 80), w_rows(behind, 0, 80), ahead_dev)]
+    to_behind.wait()
+    relay.append(copies.start(w_rows(ahead, 80, 80), w_rows(ahead, 80, 80), behind_dev))
+    waits.append(copies.start(w_rows(behind, 0, PAIR), w_rows(behind, 0, PAIR), mate))
+    waits.append(copies.start(w_rows(ahead, 0, PAIR), w_rows(ahead, 0, PAIR), mate))
+    far = (section + 2) % 4
+    for copy, start in zip(relay, (0, 80)):
+        copy.wait()
+        waits.append(copies.start(w_rows(far, start, 80), w_rows(far, start, 80), mate))
     wait_all(waits)
 
 
-def membership(ends_ref, first, count):
+def spans_and_bounds(seg_ref, first, spans_ref, bounds_ref):
+    row = lax.broadcasted_iota(jnp.int32, (32, 128), 0)
+    begins, ends = jnp.zeros((32, 128), jnp.int32), jnp.zeros((32, 128), jnp.int32)
+    end = jnp.int32(0)
+    low = [jnp.int32(0)] * 4
+    high = [jnp.int32(16384)] * 4
+    for image in range(32):
+        begin = end
+        end = begin + 64 * seg_ref[image]
+        begins = jnp.where(row == image, begin, begins)
+        ends = jnp.where(row == image, end, ends)
+        for tile in range(4):
+            start = first + 256 * tile
+            low[tile] = jnp.where(begin <= start, begin, low[tile])
+            high[tile] = jnp.where((begin < start + 256) & (end >= start + 256), end, high[tile])
+    spans_ref[0] = begins
+    spans_ref[1] = ends
+    for tile in range(4):
+        bounds_ref[tile, 0] = (low[tile] - (first - 1024)) // CHUNK
+        bounds_ref[tile, 1] = (high[tile] - (first - 1024) + CHUNK - 1) // CHUNK
+
+
+def membership(spans_ref, first, count):
     spots = first + lax.broadcasted_iota(jnp.int32, (32, count), 1)
-    return (spots >= ends_ref[:, 0:1]) & (spots < ends_ref[:, 1:2])
+    return (spots >= spans_ref[0, :, 0:1]) & (spots < spans_ref[1, :, 0:1])
 
 
 def three_parts(row):
@@ -166,19 +205,25 @@
 
 
 def permutation(transposed):
+    moved = lax.broadcasted_iota(jnp.int32, (512, 1) if transposed else (1, 512), 0 if transposed else 1)
     natural = lax.broadcasted_iota(jnp.int32, (512, 512), 1 if transposed else 0)
-    moved = lax.broadcasted_iota(jnp.int32, (512, 512), 0 if transposed else 1)
     return jnp.where(natural == 4 * (moved % 128) + moved // 128, 1.0, 0.0).astype(BF16)
 
 
-def forward_body(bounds_ref, ends_ref, q_ref, kv_ref, o_ref, op_ref, log_ref, qrow, kx, scores):
-    chip = lax.axis_index("seq") // 2
-    first = chip * 1024
+def forward_body(
+    seg_ref, q_ref, kv_ref, o_hbm, kv_hbm, op_ref, log_ref,
+    spans_ref, bounds_ref, o_ref, qrow, kx, vrow, sems,
+):
+    first = (lax.axis_index("seq") // 2) * 1024
+    keep = pltpu.make_async_copy(kv_ref, kv_hbm, sems.at[0])
+    keep.start()
+    spans_and_bounds(seg_ref, first, spans_ref, bounds_ref)
+    longest = []
     for head in range(2):
         feats = pl.ds(head * HEAD_DIM, HEAD_DIM)
         for block in range(4):
             lanes = pl.ds(block * 256, 256)
-            inside = membership(ends_ref, first + block * 256, 256)
+            inside = membership(spans_ref, first + block * 256, 256)
             joined = jnp.concatenate(
                 [
                     q_ref[feats, lanes],
@@ -188,81 +233,140 @@
                 axis=0,
             )
             qrow[head, lanes, :] = joined.T
-
-    def build(chunk, carry):
+        values = q_ref[feats, :].astype(F32)
+        longest.append(jnp.max(jnp.sum(values * values, axis=0, keepdims=True)))
+
+    ones = jnp.where(lax.broadcasted_iota(jnp.int32, (16, CHUNK), 0) < 3, 1.0, 0.0).astype(BF16)
+
+    def build(chunk, tops):
+        found = []
         lanes = pl.ds(pl.multiple_of(chunk * CHUNK, CHUNK), CHUNK)
-        inside = membership(ends_ref, first - 1024 + chunk * CHUNK, CHUNK)
+        inside = membership(spans_ref, first - 1024 + chunk * CHUNK, CHUNK)
         hot = jnp.where(inside, 1.0, 0.0).astype(BF16)
         for head in range(2):
-            kx[head, 0:80, lanes] = kv_ref[0, pl.ds(head * HEAD_DIM, HEAD_DIM), lanes]
+            feats = pl.ds(head * HEAD_DIM, HEAD_DIM)
+            kx[head, 0:80, lanes] = kv_ref[0, feats, lanes]
             kx[head, 80:112, lanes] = hot
-            kx[head, 112:128, lanes] = jnp.zeros((16, CHUNK), BF16)
+            kx[head, 112:128, lanes] = ones
+            joined = jnp.concatenate(
+                [kv_ref[1, feats, lanes], ones, jnp.zeros((32, CHUNK), BF16)], axis=0
+            )
+            vrow[head, lanes, :] = joined.T
+            values = kv_ref[0, feats, lanes].astype(F32)
+            found.append(jnp.maximum(tops[head], jnp.sum(values * values, axis=0, keepdims=True)))
+        return tuple(found)
+
+    start = jnp.zeros((1, CHUNK), F32)
+    tops = lax.fori_loop(bounds_ref[0, 0], bounds_ref[3, 1], build, (start, start))
+    small = longest[0] * jnp.max(tops[0]) <= SAFE * SAFE
+    small = small & (longest[1] * jnp.max(tops[1]) <= SAFE * SAFE)
+    lane = lax.broadcasted_iota(jnp.int32, (256, 128), 1)
+
+    def sum_tile(tile, rows):
+        def sum_step(chunk, sums):
+            lanes = pl.ds(pl.multiple_of(chunk * CHUNK, CHUNK), CHUNK)
+            probs = [
+                jnp.exp2(dot_nn(qrow[head, rows, :], kx[head, :, lanes])).astype(BF16)
+                for head in range(2)
+            ]
+            return tuple(sums[head] + dot_nn(probs[head], vrow[head, lanes, :]) for head in range(2))
+
+        start = jnp.zeros((256, 128), F32)
+        return lax.fori_loop(bounds_ref[tile, 0], bounds_ref[tile, 1], sum_step, (start, start))
+
+    def write(head, rows, sums, top_row):
+        out = sums.T
+        total_row = out[80:81, :]
+        o_ref[pl.ds(head * HEAD_DIM, HEAD_DIM), rows] = (out[:80] * (1.0 / total_row)).astype(BF16)
+        log_ref[head : head + 1, rows] = top_row + jnp.log(total_row) * LOG2E
+
+    def plain_step(tile, carry):
+        rows = pl.ds(pl.multiple_of(tile * 256, 256), 256)
+        sums = sum_tile(tile, rows)
+        for head in range(2):
+            write(head, rows, sums[head], 0.0)
         return carry
 
-    lax.fori_loop(bounds_ref[0, 0], bounds_ref[3, 1], build, 0)
-
-    def tile_step(tile, carry):
+    def shifted_step(tile, carry):
         low, high = bounds_ref[tile, 0], bounds_ref[tile, 1]
         rows = pl.ds(pl.multiple_of(tile * 256, 256), 256)
-        queries = [qrow[head, rows, :] for head in range(2)]
 
         def score_step(chunk, tops):
             lanes = pl.ds(pl.multiple_of(chunk * CHUNK, CHUNK), CHUNK)
             found = []
             for head in range(2):
-                part = dot_nn(queries[head], kx[head, :, lanes])
-                scores[head, :, lanes] = part
+                part = dot_nn(qrow[head, rows, :], kx[head, :, lanes])
                 found.append(jnp.maximum(tops[head], jnp.maximum(part[:, :128], part[:, 128:])))
             return tuple(found)
 
         start = jnp.full((256, 128), BIG, F32)
         tops = lax.fori_loop(low, high, score_step, (start, start))
-        columns = [jnp.max(top, axis=1, keepdims=True) for top in tops]
-
-        def sum_step(chunk, carry):
-            lanes = pl.ds(pl.multiple_of(chunk * CHUNK, CHUNK), CHUNK)
-            found = []
-            for head in range(2):
-                total, out = carry[head]
-                feats = pl.ds(head * HEAD_DIM, HEAD_DIM)
-                probs = jnp.exp2(scores[head, :, lanes] - columns[head])
-                out = out + dot_nt(kv_ref[1, feats, lanes], probs.astype(BF16))
-                found.append((total + (probs[:, :128] + probs[:, 128:]), out))
-            return tuple(found)
-
-        start = (jnp.zeros((256, 128), F32), jnp.zeros((HEAD_DIM, 256), F32))
-        sums = lax.fori_loop(low, high, sum_step, (start, start))
         for head in range(2):
-            total, out = sums[head]
-            top_row = jnp.max(tops[head].T, axis=0, keepdims=True)
-            total_row = jnp.sum(total.T, axis=0, keepdims=True)
-            o_ref[pl.ds(head * HEAD_DIM, HEAD_DIM), rows] = (out * (1.0 / total_row)).astype(BF16)
-            log_ref[head : head + 1, rows] = top_row + jnp.log(total_row) * LOG2E
+            shift = -jnp.max(tops[head], axis=1, keepdims=True)
+            part_one = shift.astype(BF16).astype(F32)
+            part_two = (shift - part_one).astype(BF16).astype(F32)
+            part_three = shift - part_one - part_two
+            moved = jnp.where(lane == 112, part_one, qrow[head, rows, :].astype(F32))
+            moved = jnp.where(lane == 113, part_two, moved)
+            qrow[head, rows, :] = jnp.where(lane == 114, part_three, moved).astype(BF16)
+
+        sums = sum_tile(tile, rows)
+        for head in range(2):
+            write(head, rows, sums[head], jnp.max(tops[head].T, axis=0, keepdims=True))
         return carry
 
-    lax.fori_loop(0, 4, tile_step, 0)
+    @pl.when(small)
+    def _():
+        lax.fori_loop(0, 4, plain_step, 0)
+
+    @pl.when(jnp.logical_not(small))
+    def _():
+        lax.fori_loop(0, 4, shifted_step, 0)
+
+    keep_o = pltpu.make_async_copy(o_ref, o_hbm, sems.at[1])
+    keep_o.start()
     perm = permutation(False)
     for half in range(2):
         moved = dot_nn(o_ref[:, half * 512 : half * 512 + 512], perm).astype(BF16)
         for part in range(4):
             op_ref[half, part] = moved[:, part * 128 : part * 128 + 128]
+    keep.wait()
+    keep_o.wait()
 
 
 def backward_body(
-    bounds_ref, ends_ref, q_ref, kv_ref, o_ref, log_ref, gp_ref, dq_ref, dkv_ref,
-    qrow, kx, vx, grow, gnat, acc,
+    seg_ref, sizes_ref, receiver_ref, q_ref, kv_hbm, o_hbm, log_ref, gp_ref,
+    dq_ref, dkv_ref, starts_ref, here_ref,
+    spans_ref, bounds_ref, kv_ref, o_ref, qrow, kx, vx, krow, grow, gnat, acc, sems,
 ):
-    chip = lax.axis_index("seq") // 2
-    first = chip * 1024
+    seq = lax.axis_index("seq")
+    first = (seq // 2) * 1024
+    load_kv = pltpu.make_async_copy(kv_hbm, kv_ref, sems.at[0])
+    load_o = pltpu.make_async_copy(o_hbm, o_ref, sems.at[1])
+    load_kv.start()
+    load_o.start()
+    spans_and_bounds(seg_ref, first, spans_ref, bounds_ref)
+    start = jnp.int32(0)
+    my_start, my_size = jnp.int32(0), jnp.int32(0)
+    for batch in range(32):
+        size, receiver = sizes_ref[batch], receiver_ref[batch]
+        starts_ref[pl.ds(pl.multiple_of(receiver * 16, 16), 16), :] = jnp.full((16, 128), start)
+        my_start = jnp.where(receiver == seq, start, my_start)
+        my_size = jnp.where(receiver == seq, size, my_size)
+        start = start + size
+    here_ref[0:8, :] = jnp.full((8, 512), my_start)
+    here_ref[8:16, :] = jnp.full((8, 512), my_size)
     back = permutation(True)
     for half in range(2):
         joined = jnp.concatenate([gp_ref[half, part] for part in range(4)], axis=1)
         gnat[:, half * 512 : half * 512 + 512] = dot_nn(joined, back).astype(BF16)
+    load_kv.wait()
+    load_o.wait()
     for head in range(2):
         feats = pl.ds(head * HEAD_DIM, HEAD_DIM)
         for block in range(4):
             lanes = pl.ds(block * 256, 256)
-            inside = membership(ends_ref, first + block * 256, 256)
+            inside = membership(spans_ref, first + block * 256, 256)
             joined = jnp.concatenate(
                 [
                     q_ref[feats, lanes],
@@ -285,13 +389,14 @@
 
     def build(chunk, carry):
         lanes = pl.ds(pl.multiple_of(chunk * CHUNK, CHUNK), CHUNK)
-        inside = membership(ends_ref, first - 1024 + chunk * CHUNK, CHUNK)
+        inside = membership(spans_ref, first - 1024 + chunk * CHUNK, CHUNK)
         hot = jnp.where(inside, 1.0, 0.0).astype(BF16)
         for head in range(2):
             feats = pl.ds(head * HEAD_DIM, HEAD_DIM)
             kx[head, 0:80, lanes] = kv_ref[0, feats, lanes]
             kx[head, 80:112, lanes] = hot
             kx[head, 112:128, lanes] = ones
+            krow[head, lanes, :] = kx[head, :, lanes].T
             vx[head, 0:80, lanes] = kv_ref[1, feats, lanes]
             vx[head, 80:96, lanes] = ones
             vx[head, 96:128, lanes] = jnp.zeros((32, CHUNK), BF16)
@@ -315,13 +420,13 @@
                 dscores = (probs * shifted).astype(BF16)
                 acc[0, feats, lanes] += dot_nn(q_ref[feats, rows], dscores)
                 acc[1, feats, lanes] += dot_nn(gnat[feats, rows], probs.astype(BF16))
-                found.append(sums[head] + dot_nt(kv_ref[0, feats, lanes], dscores))
+                found.append(sums[head] + dot_nn(dscores, krow[head, lanes, :]))
             return tuple(found)
 
-        start = jnp.zeros((HEAD_DIM, 256), F32)
+        start = jnp.zeros((256, 128), F32)
         sums = lax.fori_loop(low, high, step, (start, start))
         for head in range(2):
-            dq_ref[features[head], rows] = (sums[head] * FACTOR).astype(BF16)
+            dq_ref[features[head], rows] = (sums[head].T[:80] * FACTOR).astype(BF16)
         return carry
 
     lax.fori_loop(0, 4, tile_step, 0)
@@ -330,12 +435,16 @@
 
 
 def middle_body(
-    op_ref, w_ref, tokens_ref, mgrad_ref, gain_ref,
-    gl_ref, glt_ref, gp_ref, own_ref, table_ref,
-    att, gat, packed, send, recv,
+    op_ref, w_hbm, tokens_hbm, mgrad_hbm, gain_ref,
+    gp_ref, gl_hbm, glt_hbm, own_ref, table_ref,
+    w_ref, tokens_ref, mgrad_ref, gl_ref, glt_ref, att, gat, packed, send, recv,
 ):
     section, chip, core = place()
     copies = Copies(send, recv)
+    columns = pl.ds(pl.multiple_of(section * 1280, 128), 1280)
+    load_mgrad = copies.start(mgrad_hbm.at[:, columns], mgrad_ref, None)
+    load_tokens = copies.start(tokens_hbm, tokens_ref, None)
+    load_w = copies.start(w_hbm, w_ref, None)
     greet(row_peers(section, chip, core) + core_peers(section, chip, core))
     rows = pl.ds(pl.multiple_of((section * 2 + core) * PAIR, 16), PAIR)
     waits = []
@@ -351,13 +460,16 @@
     row = lax.broadcasted_iota(jnp.int32, (128, 512), 0)
     column = lax.broadcasted_iota(jnp.int32, (128, 512), 1)
     chosen = jnp.where(column == 4 * row + section, 1.0, 0.0).astype(BF16)
+    load_tokens.wait()
+    load_mgrad.wait()
     values = dot_nn(chosen, tokens_ref[...])
-    gain = gain_ref[...].astype(F32)
+    gain = gain_ref[...].reshape(1, 1280).astype(F32)
     scaled = mgrad_ref[...].astype(F32) * gain
     scaled_mean = jnp.mean(scaled, axis=1, keepdims=True)
     row = lax.broadcasted_iota(jnp.int32, (128, 128), 0)
     column = lax.broadcasted_iota(jnp.int32, (128, 128), 1)
     order = jnp.where(column == 16 * (row % 8) + row // 8, 1.0, 0.0).astype(BF16)
+    load_w.wait()
     wait_all(waits)
     layer = values + dot_nn(att[...].T, w_ref[...])
     centered = layer - jnp.mean(layer, axis=1, keepdims=True)
@@ -384,14 +496,17 @@
         late.append(copies.start(packed.at[to_chip], table_ref.at[chip], device))
     gl_ref[...] = grad_layer
     glt_ref[...] = grad_layer.T
+    late.append(copies.start(gl_ref, gl_hbm, None))
+    late.append(copies.start(glt_ref, glt_hbm, None))
     wait_all(late)
 
 
 def tail_body(
-    dq_ref, dkv_ref, glt_ref, own_ref, table_ref, starts_ref, live_ref, gl_ref, tokens_ref,
-    gain_ref, w_ref, normed_t_ref,
-    delivered_ref, gx_ref, weights_ref,
-    dq_in, dkv_in, dj, rows_ref, gn, gn_in, gx_own, gx_all, att, glt,
+    dq_ref, dkv_ref, starts_ref, live_ref, glt_hbm, own_hbm, table_hbm, gl_hbm, tokens_hbm,
+    gain_ref, w_hbm, normed_t_hbm,
+    delivered_ref, gx_all, weights_ref,
+    table_ref, gl_ref, tokens_ref, w_ref, normed_t_ref,
+    dkv_in, dj, rows_ref, gn, gn_in, gx_own, att, glt,
     parcels, arrived, p_mine, p_away, p_in,
     sum_a, sum_b, in_a, in_b, sub_a, sub_b, late_a, late_b, total, send, recv,
 ):
@@ -414,10 +529,28 @@
             lanes = pl.ds(pl.multiple_of(1024 + target * 512 + half * 256, 256), 256)
             waits.append(copies.start(dkv_ref.at[:, :, lanes], dkv_in.at[half, 2, core], device))
             lanes = pl.ds(pl.multiple_of(target * 512 + half * 256, 256), 256)
-            waits.append(copies.start(dq_ref.at[:, lanes], dq_in.at[half, core], device))
+            into = dj.at[pl.ds(pl.multiple_of(core * PAIR, 16), PAIR), half * 256 : half * 256 + 256]
+            waits.append(copies.start(dq_ref.at[:, lanes], into, device))
         back.append(waits)
-
-    begin = starts_ref[...]
+    gathered = []
+    lanes = pl.ds(pl.multiple_of(section * 128, 128), 128)
+    for step in (2, 1, 3, 0):
+        device = dev(chip, core, (section + step) % 4) if step else None
+        gathered.append(copies.start(glt_hbm, glt.at[:, lanes], device))
+    load_table = copies.start(table_hbm, table_ref, None)
+    load_w = copies.start(w_hbm, w_ref, None)
+    loads = [
+        copies.start(source, target, None)
+        for source, target in (
+            (normed_t_hbm, normed_t_ref), (tokens_hbm, tokens_ref), (gl_hbm, gl_ref)
+        )
+    ]
+    for head in range(2):
+        for part in range(4):
+            target = att.at[head * PAIR : head * PAIR + PAIR, part * 128 : part * 128 + 128]
+            loads.append(copies.start(own_hbm.at[head, part], target, None))
+
+    begin = starts_ref[:, 0:1]
     block, offset = begin // 128, begin % 128
     first = 8 * ((block + 1 - core) // 2)
     first = first + jnp.where(block % 2 == core, (offset - chip + 15) // 16, 0)
@@ -426,26 +559,20 @@
     wanted = first + out_row % 8
     wanted = (wanted // 8) * 16 + wanted % 8 + 8 * ((out_row // 8) % 2)
     hot = jnp.where(in_row == wanted, 1.0, 0.0).astype(BF16)
+    load_table.wait()
     table = table_ref[...].reshape(256, 640)
     parcels[...] = dot_nn(hot, table).astype(BF16).reshape(32, 16, 640)
-
-    for head in range(2):
-        for part in range(4):
-            att[head * PAIR : head * PAIR + PAIR, part * 128 : part * 128 + 128] = own_ref[head, part]
-    for part in range(4):
-        glt[:, part * 128 : part * 128 + 128] = glt_ref[part]
 
     row = lax.broadcasted_iota(jnp.int32, (256, 256), 0)
     column = lax.broadcasted_iota(jnp.int32, (256, 256), 1)
     by_part = jnp.where(column == 4 * (row % 64) + row // 64, 1.0, 0.0).astype(BF16)
-    natural = jnp.where(row == 4 * (column % 64) + column // 64, 1.0, 0.0).astype(BF16)
-    w_all = w_ref[...]
+    load_w.wait()
+    w_all = w_ref[...].reshape(960, 1280)
     sums = []
     for half in range(2):
         wait_all(back[half])
         lanes = pl.ds(half * 256, 256)
         for head in range(2):
-            dj[head * PAIR : head * PAIR + PAIR, lanes] = dq_in[half, head]
             for which in range(2):
                 grad = dkv_in[half, 0, head, which].astype(F32)
                 grad = grad + dkv_in[half, 1, head, which].astype(F32)
@@ -479,6 +606,8 @@
             [dot_nt(normed, dj[640:960, :]), dot_nt(glt[rows, :], att[...])], axis=1
         )
 
+    wait_all(gathered)
+    wait_all(loads)
     pairs = []
     for index in range(4):
         for core_of in range(2):
@@ -506,7 +635,7 @@
         wait_all(sums[half])
         grad = gn[half, section].astype(F32) + gn_in[half, 0].astype(F32)
         grad = grad + (gn_in[half, 1].astype(F32) + gn_in[half, 2].astype(F32))
-        scaled = grad * gain_ref[...].astype(F32)
+        scaled = grad * gain_ref[...].reshape(1, 1280).astype(F32)
         grad = inv * (
             scaled
             - jnp.mean(scaled, axis=1, keepdims=True)
@@ -554,7 +683,7 @@
 
     lane = lax.broadcasted_iota(jnp.int32, (1, 512), 1)
     from_chip, from_core, side, number = lane // 32, (lane // 16) % 2, (lane // 8) % 2, lane % 8
-    begin, live = live_ref[0:1, :], live_ref[1:2, :]
+    begin, live = live_ref[0:1, :], live_ref[8:9, :]
     block, offset = begin // 128, begin % 128
     spot = 8 * ((block + 1 - from_core) // 2) + number
     spot = spot + jnp.where(block % 2 == from_core, (offset - from_chip + 15) // 16, 0)
@@ -576,11 +705,23 @@
     for target, device in ((1 - core, mate), (core, None)):
         rows = pl.ds(pl.multiple_of(target * 40, 8), 40)
         lasts.append(copies.start(total.at[rows, :], weights_ref.at[core], device))
+    wait_all(lasts)
+    for waits in gathers:
+        wait_all(waits)
+
+
+def results_body(gx_ref, both_ref, arrived_ref, gx_out, w_qkv_out, w_out_out, delivered_out):
+    row = lax.broadcasted_iota(jnp.int32, (256, 256), 0)
+    column = lax.broadcasted_iota(jnp.int32, (256, 256), 1)
+    natural = jnp.where(row == 4 * (column % 64) + column // 64, 1.0, 0.0).astype(BF16)
     for half in range(2):
-        wait_all(gathers[half])
-        rows = gx_all[half].reshape(256, 1280)
-        gx_ref[half * 256 : half * 256 + 256, :] = dot_nn(natural, rows).astype(BF16)
-    wait_all(lasts)
+        rows = gx_ref[half].reshape(256, 1280)
+        gx_out[half * 256 : half * 256 + 256, :] = dot_nn(natural, rows).astype(BF16)
+    w_qkv_out[0] = both_ref[0, :, :320]
+    w_qkv_out[1] = both_ref[0, :, 320:]
+    w_qkv_out[2] = both_ref[1, :, :320]
+    w_out_out[...] = both_ref[1, :, 320:]
+    delivered_out[...] = arrived_ref[...]
 
 
 def halo_peers(section, chip, core):
@@ -619,98 +760,123 @@
 def local(
     tokens, norm_gain, w_qkv, w_out, merge_gain, seg_blocks, mb_sizes, mb_receiver, merged_grad
 ):
-    section = lax.axis_index("section")
-    seq = lax.axis_index("seq")
-    chip = seq // 2
-    w_full = lax.all_gather(w_out, "section", axis=0, tiled=True)
     w_rows = w_qkv.transpose(0, 2, 1)
-    ends = 64 * jnp.cumsum(seg_blocks)
-    spans = jnp.stack([ends - 64 * seg_blocks, ends], axis=1)
-    tile_first = chip * 1024 + 256 * jnp.arange(4, dtype=jnp.int32)[:, None]
-    starts_in = jnp.max(jnp.where(spans[None, :, 0] <= tile_first, spans[None, :, 0], 0), axis=1)
-    ends_in = jnp.min(jnp.where(ends[None, :] >= tile_first + 256, ends[None, :], 16384), axis=1)
-    base = (chip - 1) * 1024
-    bounds = jnp.stack(
-        [(starts_in - base) // CHUNK, (ends_in - base + CHUNK - 1) // CHUNK], axis=1
-    ).astype(jnp.int32)
-    mine = mb_receiver[None, :] == jnp.arange(32, dtype=jnp.int32)[:, None]
-    starts = jnp.cumsum(mb_sizes) - mb_sizes
-    starts = jnp.sum(jnp.where(mine, starts[None, :], 0), axis=1)
-    lives = jnp.sum(jnp.where(mine, mb_sizes[None, :], 0), axis=1)
-    start_rows = jnp.repeat(starts, 16).reshape(512, 1)
-    here = jnp.broadcast_to(jnp.stack([starts[seq], lives[seq]])[:, None], (2, 512))
-    gain_one, gain_two = norm_gain.reshape(1, -1), merge_gain.reshape(1, -1)
-    mgrad = lax.dynamic_slice_in_dim(merged_grad, section * 1280, 1280, 1)
-
-    q, kv, normed_t = linked_call(
-        1,
+    q, kv, normed_t, w_full = call(
         project_body,
-        [shape((PAIR, 1024)), shape((2, PAIR, 3072)), shape((1280, 512))],
-        [tokens, gain_one, w_rows],
-        [pltpu.VMEM((512, 1280), BF16), pltpu.VMEM((3, 320, 512), BF16)],
-        16,
+        [
+            (VMEM, shape((PAIR, 1024))),
+            (VMEM, shape((2, PAIR, 3072))),
+            (HBM, shape((1280, 512))),
+            (HBM, shape((1280, 1280))),
+        ],
+        [(HBM, tokens), (VMEM, norm_gain), (HBM, w_rows), (HBM, w_out)],
+        [
+            pltpu.VMEM((512, 1280), BF16),
+            pltpu.VMEM((3, 320, 1280), BF16),
+            pltpu.VMEM((512, 1280), BF16),
+            pltpu.VMEM((1280, 512), BF16),
+            pltpu.VMEM((3, 320, 512), BF16),
+        ],
+        copies=32,
+        number=1,
+        limit=20,
     )
-    o, op, log_total = local_call(
+    o, kv_kept, op, log_total = call(
         forward_body,
-        [shape((PAIR, 1024)), shape((2, 4, PAIR, 128)), shape((2, 1024), F32)],
-        [bounds, spans, q, kv],
-        [
+        [
+            (HBM, shape((PAIR, 1024))),
+            (HBM, shape((2, PAIR, 3072))),
+            (VMEM, shape((2, 4, PAIR, 128))),
+            (VMEM, shape((2, 1024), F32)),
+        ],
+        [(SMEM, seg_blocks), (VMEM, q), (VMEM, kv)],
+        [
+            pltpu.VMEM((2, 32, 128), jnp.int32),
+            pltpu.SMEM((4, 2), jnp.int32),
+            pltpu.VMEM((PAIR, 1024), BF16),
             pltpu.VMEM((2, 1024, 128), BF16),
             pltpu.VMEM((2, 128, 3072), BF16),
-            pltpu.VMEM((2, 256, 3072), F32),
-        ],
-        smem=1,
+            pltpu.VMEM((2, 3072, 128), BF16),
+        ],
+        copies=2,
+        limit=16,
     )
-    grad_layer, glt, gp, att_own, table = linked_call(
-        2,
+    gp, grad_layer, glt, att_own, table = call(
         middle_body,
         [
-            shape((128, 1280)),
-            shape((1280, 128)),
-            shape((2, 4, PAIR, 128)),
-            shape((2, 4, PAIR, 128)),
-            shape((16, 16, 640)),
-        ],
-        [op, w_full, tokens, mgrad, gain_two],
-        [
+            (VMEM, shape((2, 4, PAIR, 128))),
+            (HBM, shape((128, 1280))),
+            (HBM, shape((1280, 128))),
+            (HBM, shape((2, 4, PAIR, 128))),
+            (HBM, shape((16, 16, 640))),
+        ],
+        [(VMEM, op), (HBM, w_full), (HBM, tokens), (HBM, merged_grad), (VMEM, merge_gain)],
+        [
+            pltpu.VMEM((1280, 1280), BF16),
+            pltpu.VMEM((512, 1280), BF16),
+            pltpu.VMEM((128, 1280), BF16),
+            pltpu.VMEM((128, 1280), BF16),
+            pltpu.VMEM((1280, 128), BF16),
             pltpu.VMEM((1280, 128), BF16),
             pltpu.VMEM((1280, 128), BF16),
             pltpu.VMEM((16, 16, 640), BF16),
         ],
-        34,
+        copies=40,
+        number=2,
+        limit=20,
     )
-    glt_all = lax.all_gather(glt, "section")
-    dq, dkv = local_call(
+    dq, dkv, start_rows, here = call(
         backward_body,
-        [shape((PAIR, 1024)), shape((2, PAIR, 3072))],
-        [bounds, spans, q, kv, o, log_total, gp],
-        [
+        [
+            (VMEM, shape((PAIR, 1024))),
+            (VMEM, shape((2, PAIR, 3072))),
+            (VMEM, shape((512, 128), jnp.int32)),
+            (VMEM, shape((16, 512), jnp.int32)),
+        ],
+        [
+            (SMEM, seg_blocks), (SMEM, mb_sizes), (SMEM, mb_receiver),
+            (VMEM, q), (HBM, kv_kept), (HBM, o), (VMEM, log_total), (VMEM, gp),
+        ],
+        [
+            pltpu.VMEM((2, 32, 128), jnp.int32),
+            pltpu.SMEM((4, 2), jnp.int32),
+            pltpu.VMEM((2, PAIR, 3072), BF16),
+            pltpu.VMEM((PAIR, 1024), BF16),
             pltpu.VMEM((2, 1024, 128), BF16),
             pltpu.VMEM((2, 128, 3072), BF16),
             pltpu.VMEM((2, 128, 3072), BF16),
+            pltpu.VMEM((2, 3072, 128), BF16),
             pltpu.VMEM((2, 1024, 128), BF16),
             pltpu.VMEM((PAIR, 1024), BF16),
             pltpu.VMEM((2, PAIR, 3072), F32),
         ],
-        smem=1,
+        copies=2,
+        limit=26,
     )
-    delivered, grad_x, weights = linked_call(
-        3,
+    arrived, gx_all, weights = call(
         tail_body,
-        [shape((256, 1280)), shape((512, 1280)), shape((2, 40, 640), F32)],
-        [
-            dq, dkv, glt_all, att_own, table, start_rows, here, grad_layer, tokens,
-            gain_one, w_rows.reshape(960, 1280), normed_t,
-        ],
-        [
-            pltpu.VMEM((2, 2, PAIR, 256), BF16),
+        [
+            (VMEM, shape((256, 1280))),
+            (VMEM, shape((2, 4, 64, 1280))),
+            (VMEM, shape((2, 40, 640), F32)),
+        ],
+        [
+            (VMEM, dq), (VMEM, dkv), (VMEM, start_rows), (VMEM, here), (HBM, glt), (HBM, att_own),
+            (HBM, table), (HBM, grad_layer), (HBM, tokens), (VMEM, norm_gain), (HBM, w_rows),
+            (HBM, normed_t),
+        ],
+        [
+            pltpu.VMEM((16, 16, 640), BF16),
+            pltpu.VMEM((128, 1280), BF16),
+            pltpu.VMEM((512, 1280), BF16),
+            pltpu.VMEM((3, 320, 1280), BF16),
+            pltpu.VMEM((1280, 512), BF16),
             pltpu.VMEM((2, 3, 2, 2, PAIR, 256), BF16),
             pltpu.VMEM((960, 512), BF16),
             pltpu.VMEM((256, 960), BF16),
             pltpu.VMEM((2, 4, 64, 1280), BF16),
             pltpu.VMEM((2, 3, 64, 1280), BF16),
             pltpu.VMEM((2, 64, 1280), BF16),
-            pltpu.VMEM((2, 4, 64, 1280), BF16),
             pltpu.VMEM((320, 512), BF16),
             pltpu.VMEM((1280, 512), BF16),
             pltpu.VMEM((32, 16, 640), BF16),
@@ -728,12 +894,22 @@
             pltpu.VMEM((3, 80, 256), BF16),
             pltpu.VMEM((80, 640), F32),
         ],
-        90,
+        copies=112,
+        number=3,
+        limit=42,
     )
-    sums = weights.transpose(1, 0, 2).reshape(40, 4, 320)
-    grad_w_qkv = sums[:, :3].transpose(1, 0, 2)
-    grad_w_out = sums[:, 3].T
-    return (delivered, grad_x, grad_w_qkv, grad_w_out)
+    grad_x, grad_w_qkv, grad_w_out, delivered = call(
+        results_body,
+        [
+            (VMEM, shape((512, 1280))),
+            (VMEM, shape((3, 40, 320), F32)),
+            (VMEM, shape((40, 320), F32)),
+            (VMEM, shape((256, 1280))),
+        ],
+        [(VMEM, gx_all), (VMEM, weights), (VMEM, arrived)],
+        limit=14,
+    )
+    return (delivered, grad_x, grad_w_qkv, grad_w_out.T)
 
 
 def solution(mesh):

time: 181 us -> 141 us (0.78)
  local copies, waits for them, and re-layouts: 29.7 us -> 4.88 us
  between operations: 14.3 us -> 0.79 us
  other arithmetic: 3.04 us -> 0 us
  Pallas kernels: 132 us -> 135 us
    unnamed x54 -> x24, local copies, waits for them, and re-layouts: 23.6 us -> 4.88 us
    reshape x4 -> x0, local copies, waits for them, and re-layouts: 3.32 us -> none  [the longest x2 1.38 us: local(): gain_one, gain_two = (norm_gain.reshape(1, -1), merge_gain.reshape(1, -1))]
    pallas_call x5 -> x6, Pallas kernels: 132 us -> 135 us  [call(): pl.pallas_call(body, out_shape=[array for _, array in outs], in_specs=[pl...]
  transfers between devices with their start and end apart: 2 -> 0, of which waited for: 0 -> 0; matrix products, arithmetic and copies ran while one was open for 4% -> 0% of each run, Pallas kernels for 28% -> 0%
where the time goes in v3:
time: 141 us; the launch traced here: 140 us
  Pallas kernels  135 us (96%)
  local copies, waits for them, and re-layouts  4.88 us (3%)
    pallas_call x6, Pallas kernels, call(): pl.pallas_call(body, out_shape=[array for _, array in outs], in_specs=[pl...  135 us
    unnamed x24, local copies, waits for them, and re-layouts  4.88 us

profile of v3, /device:TPU:1, one launch (start us, length us, event | category | flops | bytes accessed | tf_op | source)
XLA Modules:
  0.0 140.3 jit_solution(7302952087991752163)
XLA Ops:
  0.6 0.0 copy-start
  0.6 1.3 copy-done
  2.0 0.0 copy-start.2
  2.0 1.7 %copy-done.2 = bf16[3,1280,320]{1,2,0:T(8,128)(2,1)S(1)} copy-done((bf16[3,1280,320]{1,2,0:T(8,128)(2,1)S(1)}, bf16[3,1280,320]{1,2,0:T(8,128)(2,1)}, u32[]{:S(2)}) %copy-start.2) | copy-done | bytes 2457624
  3.6 0.0 copy-start.5
  3.6 1.1 copy-done.5
  4.8 0.0 copy-start.6
  4.8 0.7 copy-done.6
  5.5 0.0 copy-start.9
  5.5 0.0 copy-start.4
  5.5 28.4 %shard_map.120 = (bf16[160,1024]{1,0:T(8,128)(2,1)S(1)}, bf16[2,160,3072]{2,1,0:T(8,128)(2,1)S(1)}, bf16[1280,512]{1,0:T(8,128)(2,1)S(1)}, bf16[1280,1280]{1,0:T(8,128)(2,1)S(1)}) custom-call(bf16[512,1280]{1,0:T(8,128)(2,1)S(1)} %copy-done, bf16[1280]{0:T(1024)(128)(2,1)S(1)} %copy-done.6, bf16[3,320,1280]{2,1,0:T(8,128)(2,1)S(1)} %bitcast.2, ...), custom_call_target="tpu_custom_call" | custom-call | tf_op jit(solution)/shard_map/pallas_call | solution.py:85
  33.9 0.0 copy-start.1
  33.9 0.0 copy-start.8
  33.9 0.0 copy-done.9
  34.0 10.4 %shard_map.121 = (bf16[160,1024]{1,0:T(8,128)(2,1)S(1)}, bf16[2,160,3072]{2,1,0:T(8,128)(2,1)S(1)}, bf16[2,4,160,128]{3,2,1,0:T(8,128)(2,1)S(1)}, f32[2,1024]{1,0:T(2,128)S(1)}) custom-call(s32[32]{0:T(128)S(1)} %copy-done.9, bf16[160,1024]{1,0:T(8,128)(2,1)S(1)} %get-tuple-element.28.q_ref, bf16[2,160,3072]{2,1,0:T(8,128)(2,1)S(1)} %get-tuple-element.29.kv_ref), custom_call_target="tpu_custom_call" | custom-call | tf_op jit(solution)/shard_map/pallas_call | solution.py:85
  44.4 0.0 copy-done.4
  44.4 0.0 copy-done.1
  44.4 0.0 copy-done.8
  44.4 0.0 copy-start.10
  44.4 0.0 copy-start.11
  44.4 22.9 %shard_map.122 = (bf16[2,4,160,128]{3,2,1,0:T(8,128)(2,1)S(1)}, bf16[128,1280]{1,0:T(8,128)(2,1)S(1)}, bf16[1280,128]{1,0:T(8,128)(2,1)S(1)}, bf16[2,4,160,128]{...) custom-call(bf16[2,4,160,128]{3,2,1,0:T(8,128)(2,1)S(1)} %get-tuple-element.33.op_ref, ...), custom_call_target="tpu_custom_call" | custom-call | tf_op jit(solution)/shard_map/pallas_call | solution.py:85
  67.3 0.0 copy-start.3
  67.4 0.0 copy-start.7
  67.4 0.0 copy-done.10
  67.4 0.0 copy-done.11
  67.4 11.1 %shard_map.123 = (bf16[160,1024]{1,0:T(8,128)(2,1)S(1)}, bf16[2,160,3072]{2,1,0:T(8,128)(2,1)S(1)}, s32[512,128]{1,0:T(8,128)S(1)}, s32[16,512]{1,0:T(8,128)S(1)}) custom-call(s32[32]{0:T(128)S(1)} %copy-done.9, s32[32]{0:T(128)S(1)} %copy-done.10, s32[32]{0:T(128)S(1)} %copy-done.11, bf16[160,1024]{1,0:T(8,128)(2,1)S(1)} %get-tuple-element.28.q_ref, ...), custom_call_target="tpu_custom_call" | custom-call | tf_op jit(solution)/shard_map/pallas_call | solution.py:85
  78.5 0.0 copy-done.3
  78.5 0.0 copy-done.7
  78.5 60.0 %shard_map.124 = (bf16[256,1280]{1,0:T(8,128)(2,1)S(1)}, bf16[2,4,64,1280]{3,2,1,0:T(8,128)(2,1)S(1)}, f32[2,40,640]{2,1,0:T(8,128)S(1)}) custom-call(bf16[160,1024]{1,0:T(8,128)(2,1)S(1)} %get-tuple-element.36.dq_ref, bf16[2,160,3072]{2,1,0:T(8,128)(2,1)S(1)} %get-tuple-element.37.dkv_ref, s32[512,128]{1,0:T(8,128)S(1)} %get-tuple-element.38.starts_ref, ...), custom_call_target="tpu_custom_call" | custom-call | tf_op jit(solution)/shard_map/pallas_call | solution.py:85
  138.5 1.8 %shard_map.125 = (bf16[512,1280]{1,0:T(8,128)(2,1)}, f32[3,40,320]{2,1,0:T(8,128)}, f32[40,320]{1,0:T(8,128)}, bf16[256,1280]{1,0:T(8,128)(2,1)}) custom-call(bf16[2,4,64,1280]{3,2,1,0:T(8,128)(2,1)S(1)} %get-tuple-element.45.gx_ref, f32[2,40,640]{2,1,0:T(8,128)S(1)} %get-tuple-element.46.both_ref, bf16[256,1280]{1,0:T(8,128)(2,1)S(1)} %get-tuple-element.47.arrived_ref), custom_call_target="tpu_custom_call" | custom-call | tf_op jit(solution)/shard_map/pallas_call | solution.py:85
Async XLA Ops:
  0.6 1.3 copy-start
  2.0 1.7 %copy-start.2 = (bf16[3,1280,320]{1,2,0:T(8,128)(2,1)S(1)}, bf16[3,1280,320]{1,2,0:T(8,128)(2,1)}, u32[]{:S(2)}) copy-start(bf16[3,1280,320]{1,2,0:T(8,128)(2,1)} %param.11) | copy-start | bytes 7372804
  3.6 1.1 copy-start.5
  4.8 0.7 copy-start.6
  5.5 28.5 %copy-start.9 = (s32[32]{0:T(128)S(1)}, s32[32]{0:T(128)}, u32[]{:S(2)}) copy-start(s32[32]{0:T(128)} %seg_ref.3) | copy-start | bytes 388
  5.5 38.9 %copy-start.4 = (bf16[128,5120]{1,0:T(8,128)(2,1)S(1)}, bf16[128,5120]{1,0:T(8,128)(2,1)}, u32[]{:S(2)}) copy-start(bf16[128,5120]{1,0:T(8,128)(2,1)} %mgrad_hbm.1) | copy-start | bytes 3932164
  33.9 10.5 %copy-start.1 = (bf16[512,1280]{1,0:T(8,128)(2,1)S(1)}, bf16[512,1280]{1,0:T(8,128)(2,1)}, u32[]{:S(2)}) copy-start(bf16[512,1280]{1,0:T(8,128)(2,1)} %tokens_hbm.5) | copy-start | bytes 3932164
  33.9 10.5 %copy-start.8 = (bf16[1280]{0:T(1024)(128)(2,1)S(1)}, bf16[1280]{0:T(1024)(128)(2,1)}, u32[]{:S(2)}) copy-start(bf16[1280]{0:T(1024)(128)(2,1)} %gain_ref.4) | copy-start | bytes 7684
  44.4 23.0 %copy-start.10 = (s32[32]{0:T(128)S(1)}, s32[32]{0:T(128)}, u32[]{:S(2)}) copy-start(s32[32]{0:T(128)} %sizes_ref.1) | copy-start | bytes 388
  44.4 23.0 %copy-start.11 = (s32[32]{0:T(128)S(1)}, s32[32]{0:T(128)}, u32[]{:S(2)}) copy-start(s32[32]{0:T(128)} %receiver_ref.1) | copy-start | bytes 388
  67.3 11.1 %copy-start.3 = (bf16[3,1280,320]{1,2,0:T(8,128)(2,1)S(1)}, bf16[3,1280,320]{1,2,0:T(8,128)(2,1)}, u32[]{:S(2)}) copy-start(bf16[3,1280,320]{1,2,0:T(8,128)(2,1)} %param.11) | copy-start | bytes 7372804
  67.4 11.1 %copy-start.7 = (bf16[1280]{0:T(1024)(128)(2,1)S(1)}, bf16[1280]{0:T(1024)(128)(2,1)}, u32[]{:S(2)}) copy-start(bf16[1280]{0:T(1024)(128)(2,1)} %gain_ref.5) | copy-start | bytes 7684

commit v4 on v3

--- a/solution.py
+++ b/solution.py
@@ -334,10 +334,41 @@
     keep_o.wait()
 
 
+def build_keys(spans_ref, position, kv_ref, lanes, kx, vx, krow, into):
+    ones = jnp.where(lax.broadcasted_iota(jnp.int32, (16, CHUNK), 0) < 3, 1.0, 0.0).astype(BF16)
+    hot = jnp.where(membership(spans_ref, position, CHUNK), 1.0, 0.0).astype(BF16)
+    for head in range(2):
+        feats = pl.ds(head * HEAD_DIM, HEAD_DIM)
+        keys = jnp.concatenate([kv_ref[0, feats, lanes], hot, ones], axis=0)
+        kx[head, :, into] = keys
+        krow[head, into, :] = keys.T
+        vx[head, :, into] = jnp.concatenate(
+            [kv_ref[1, feats, lanes], ones, jnp.zeros((32, CHUNK), BF16)], axis=0
+        )
+
+
+def backward_step(rows, chunks, q_ref, g_ref, qrow, grow, kx, vx, krow, dk_acc, dv_acc, sums):
+    pairs = [(head, lanes) for lanes in chunks for head in range(2)]
+    feats = [pl.ds(head * HEAD_DIM, HEAD_DIM) for head in range(2)]
+    probs = [jnp.exp2(dot_nn(qrow[head, rows, :], kx[head, :, lanes])) for head, lanes in pairs]
+    shifted = [dot_nn(grow[head, rows, :], vx[head, :, lanes]) for head, lanes in pairs]
+    dscores = [(prob * part).astype(BF16) for prob, part in zip(probs, shifted)]
+    weights = [prob.astype(BF16) for prob in probs]
+    dk = [dot_nn(q_ref[feats[head], rows], part) for (head, _), part in zip(pairs, dscores)]
+    dv = [dot_nn(g_ref[feats[head], rows], part) for (head, _), part in zip(pairs, weights)]
+    sums = list(sums)
+    for (head, lanes), part in zip(pairs, dscores):
+        sums[head] = sums[head] + dot_nn(part, krow[head, lanes, :])
+    for (head, lanes), dk_part, dv_part in zip(pairs, dk, dv):
+        dk_acc[head, :, lanes] += dk_part
+        dv_acc[head, :, lanes] += dv_part
+    return tuple(sums)
+
+
 def backward_body(
     seg_ref, sizes_ref, receiver_ref, q_ref, kv_hbm, o_hbm, log_ref, gp_ref,
-    dq_ref, dkv_ref, starts_ref, here_ref,
-    spans_ref, bounds_ref, kv_ref, o_ref, qrow, kx, vx, krow, grow, gnat, acc, sems,
+    dq_ref, dkv_ref, starts_ref, here_ref, qrow, grow, gnat, spans_ref,
+    bounds_ref, kv_ref, o_ref, kx, vx, krow, dk_acc, dv_acc, sems,
 ):
     seq = lax.axis_index("seq")
     first = (seq // 2) * 1024
@@ -385,53 +416,43 @@
             )
             grow[head, lanes, :] = joined.T
 
-    ones = jnp.where(lax.broadcasted_iota(jnp.int32, (16, CHUNK), 0) < 3, 1.0, 0.0).astype(BF16)
+    def outside(low, high, step, carry):
+        carry = lax.fori_loop(low, jnp.minimum(high, 4), step, carry)
+        return lax.fori_loop(jnp.maximum(low, 8), high, step, carry)
+
+    def place_of(chunk):
+        return pl.ds(pl.multiple_of(jnp.where(chunk < 4, chunk, chunk - 4) * CHUNK, CHUNK), CHUNK)
 
     def build(chunk, carry):
         lanes = pl.ds(pl.multiple_of(chunk * CHUNK, CHUNK), CHUNK)
-        inside = membership(spans_ref, first - 1024 + chunk * CHUNK, CHUNK)
-        hot = jnp.where(inside, 1.0, 0.0).astype(BF16)
+        build_keys(
+            spans_ref, first - 1024 + chunk * CHUNK, kv_ref, lanes, kx, vx, krow, place_of(chunk)
+        )
+        return carry
+
+    outside(bounds_ref[0, 0], bounds_ref[3, 1], build, 0)
+    dk_acc[...] = jnp.zeros_like(dk_acc)
+    dv_acc[...] = jnp.zeros_like(dv_acc)
+
+    def tile_step(tile, carry):
+        rows = pl.ds(pl.multiple_of(tile * 256, 256), 256)
+
+        def step(chunk, sums):
+            return backward_step(
+                rows, [place_of(chunk)], q_ref, gnat, qrow, grow, kx, vx, krow, dk_acc, dv_acc, sums
+            )
+
+        start = jnp.zeros((256, 128), F32)
+        sums = outside(bounds_ref[tile, 0], bounds_ref[tile, 1], step, (start, start))
         for head in range(2):
-            feats = pl.ds(head * HEAD_DIM, HEAD_DIM)
-            kx[head, 0:80, lanes] = kv_ref[0, feats, lanes]
-            kx[head, 80:112, lanes] = hot
-            kx[head, 112:128, lanes] = ones
-            krow[head, lanes, :] = kx[head, :, lanes].T
-            vx[head, 0:80, lanes] = kv_ref[1, feats, lanes]
-            vx[head, 80:96, lanes] = ones
-            vx[head, 96:128, lanes] = jnp.zeros((32, CHUNK), BF16)
+            dq_ref[head, rows, :] = sums[head]
         return carry
 
-    lax.fori_loop(bounds_ref[0, 0], bounds_ref[3, 1], build, 0)
-    acc[...] = jnp.zeros_like(acc)
-
-    def tile_step(tile, carry):
-        low, high = bounds_ref[tile, 0], bounds_ref[tile, 1]
-        rows = pl.ds(pl.multiple_of(tile * 256, 256), 256)
-        features = [pl.ds(head * HEAD_DIM, HEAD_DIM) for head in range(2)]
-
-        def step(chunk, sums):
-            lanes = pl.ds(pl.multiple_of(chunk * CHUNK, CHUNK), CHUNK)
-            found = []
-            for head in range(2):
-                feats = features[head]
-                probs = jnp.exp2(dot_nn(qrow[head, rows, :], kx[head, :, lanes]))
-                shifted = dot_nn(grow[head, rows, :], vx[head, :, lanes])
-                dscores = (probs * shifted).astype(BF16)
-                acc[0, feats, lanes] += dot_nn(q_ref[feats, rows], dscores)
-                acc[1, feats, lanes] += dot_nn(gnat[feats, rows], probs.astype(BF16))
-                found.append(sums[head] + dot_nn(dscores, krow[head, lanes, :]))
-            return tuple(found)
-
-        start = jnp.zeros((256, 128), F32)
-        sums = lax.fori_loop(low, high, step, (start, start))
-        for head in range(2):
-            dq_ref[features[head], rows] = (sums[head].T[:80] * FACTOR).astype(BF16)
-        return carry
-
     lax.fori_loop(0, 4, tile_step, 0)
-    dkv_ref[0] = (acc[0] * LN2).astype(BF16)
-    dkv_ref[1] = acc[1].astype(BF16)
+    for head in range(2):
+        feats = pl.ds(head * HEAD_DIM, HEAD_DIM)
+        dkv_ref[0, feats, :] = (dk_acc[head] * LN2).astype(BF16)
+        dkv_ref[1, feats, :] = dv_acc[head].astype(BF16)
 
 
 def middle_body(
@@ -502,10 +523,11 @@
 
 
 def tail_body(
-    dq_ref, dkv_ref, starts_ref, live_ref, glt_hbm, own_hbm, table_hbm, gl_hbm, tokens_hbm,
-    gain_ref, w_hbm, normed_t_hbm,
+    dkv_ref, starts_ref, live_ref, dq_ref, qrow, grow, gnat, spans_ref, q_ref, kv_hbm,
+    glt_hbm, own_hbm, table_hbm, gl_hbm, tokens_hbm, gain_ref, w_hbm, normed_t_hbm,
     delivered_ref, gx_all, weights_ref,
     table_ref, gl_ref, tokens_ref, w_ref, normed_t_ref,
+    kv_ref, kx, vx, krow, dk_acc, dv_acc, dq_acc, own_out, mate_in,
     dkv_in, dj, rows_ref, gn, gn_in, gx_own, att, glt,
     parcels, arrived, p_mine, p_away, p_in,
     sum_a, sum_b, in_a, in_b, sub_a, sub_b, late_a, late_b, total, send, recv,
@@ -518,25 +540,20 @@
     back = []
     for half in range(2):
         waits = []
-        for step, base, slot in ((-1, 0, 0), (1, 2048, 1)):
+        for step, base, slot in ((-1, 0, 0), (1, 1024, 1)):
             for target in (core, 1 - core):
                 lanes = pl.ds(pl.multiple_of(base + target * 512 + half * 256, 256), 256)
                 device = dev(around(chip, step), target, section)
                 waits.append(
                     copies.start(dkv_ref.at[:, :, lanes], dkv_in.at[half, slot, core], device)
                 )
-        for target, device in ((1 - core, mate), (core, None)):
-            lanes = pl.ds(pl.multiple_of(1024 + target * 512 + half * 256, 256), 256)
-            waits.append(copies.start(dkv_ref.at[:, :, lanes], dkv_in.at[half, 2, core], device))
-            lanes = pl.ds(pl.multiple_of(target * 512 + half * 256, 256), 256)
-            into = dj.at[pl.ds(pl.multiple_of(core * PAIR, 16), PAIR), half * 256 : half * 256 + 256]
-            waits.append(copies.start(dq_ref.at[:, lanes], into, device))
         back.append(waits)
     gathered = []
     lanes = pl.ds(pl.multiple_of(section * 128, 128), 128)
     for step in (2, 1, 3, 0):
         device = dev(chip, core, (section + step) % 4) if step else None
         gathered.append(copies.start(glt_hbm, glt.at[:, lanes], device))
+    load_kv = copies.start(kv_hbm.at[:, :, 1024:2048], kv_ref, None)
     load_table = copies.start(table_hbm, table_ref, None)
     load_w = copies.start(w_hbm, w_ref, None)
     loads = [
@@ -550,6 +567,55 @@
             target = att.at[head * PAIR : head * PAIR + PAIR, part * 128 : part * 128 + 128]
             loads.append(copies.start(own_hbm.at[head, part], target, None))
 
+    load_kv.wait()
+    for chunk in range(4):
+        lanes = pl.ds(chunk * CHUNK, CHUNK)
+        build_keys(
+            spans_ref, chip * 1024 + chunk * CHUNK, kv_ref, lanes, kx, vx, krow, lanes
+        )
+    dk_acc[...] = jnp.zeros_like(dk_acc)
+    dv_acc[...] = jnp.zeros_like(dv_acc)
+    dq_acc[...] = dq_ref[...]
+
+    def own_step(tile, group):
+        rows = pl.ds(pl.multiple_of(tile * 256, 256), 256)
+        chunks = [pl.ds((group + 2 * which) * CHUNK, CHUNK) for which in range(2)]
+        sums = backward_step(
+            rows, chunks, q_ref, gnat, qrow, grow, kx, vx, krow, dk_acc, dv_acc,
+            (dq_acc[0, rows, :], dq_acc[1, rows, :]),
+        )
+        for head in range(2):
+            dq_acc[head, rows, :] = sums[head]
+
+    def finish_own(half):
+        for of_core in range(2):
+            lanes = pl.ds(of_core * 512 + half * 256, 256)
+            for head in range(2):
+                feats = pl.ds(head * HEAD_DIM, HEAD_DIM)
+                part = dq_acc[head, lanes, :].T[:80] * FACTOR
+                own_out[half, of_core, 0, feats, :] = part.astype(BF16)
+                own_out[half, of_core, 1, feats, :] = (dk_acc[head, :, lanes] * LN2).astype(BF16)
+                own_out[half, of_core, 2, feats, :] = dv_acc[head, :, lanes].astype(BF16)
+        back[half].append(copies.start(own_out.at[half, 1 - core], mate_in.at[half], mate))
+
+    def first_step(tile, carry):
+        own_step(tile, 0)
+        return carry
+
+    def even_step(index, carry):
+        own_step(index * 2, 1)
+        return carry
+
+    def odd_step(index, carry):
+        own_step(index * 2 + 1, 1)
+        return carry
+
+    lax.fori_loop(0, 4, first_step, 0)
+    lax.fori_loop(0, 2, even_step, 0)
+    finish_own(0)
+    lax.fori_loop(0, 2, odd_step, 0)
+    finish_own(1)
+
     begin = starts_ref[:, 0:1]
     block, offset = begin // 128, begin % 128
     first = 8 * ((block + 1 - core) // 2)
@@ -572,13 +638,13 @@
     for half in range(2):
         wait_all(back[half])
         lanes = pl.ds(half * 256, 256)
-        for head in range(2):
-            for which in range(2):
-                grad = dkv_in[half, 0, head, which].astype(F32)
-                grad = grad + dkv_in[half, 1, head, which].astype(F32)
-                grad = grad + dkv_in[half, 2, head, which].astype(F32)
-                start = 320 * (which + 1) + head * PAIR
-                dj[start : start + PAIR, lanes] = grad.astype(BF16)
+        for near, head in ((True, core), (False, 1 - core)):
+            for which in range(3):
+                grad = own_out[half, core, which] if near else mate_in[half, which]
+                if which:
+                    grad = grad.astype(F32) + dkv_in[half, 0, head, which - 1].astype(F32)
+                    grad = (grad + dkv_in[half, 1, head, which - 1].astype(F32)).astype(BF16)
+                dj[pl.ds(pl.multiple_of(320 * which + head * PAIR, 16), PAIR), lanes] = grad
         rows_ref[...] = dot_nt(by_part, dj[:, lanes]).astype(BF16)
         gn[half] = dot_nn(rows_ref[...], w_all).astype(BF16).reshape(4, 64, 1280)
         waits = []
@@ -825,33 +891,34 @@
         number=2,
         limit=20,
     )
-    dq, dkv, start_rows, here = call(
+    dq, dkv, start_rows, here, qrow, grow, gnat, spans = call(
         backward_body,
         [
-            (VMEM, shape((PAIR, 1024))),
-            (VMEM, shape((2, PAIR, 3072))),
+            (VMEM, shape((2, 1024, 128), F32)),
+            (VMEM, shape((2, PAIR, 2048))),
             (VMEM, shape((512, 128), jnp.int32)),
             (VMEM, shape((16, 512), jnp.int32)),
+            (VMEM, shape((2, 1024, 128))),
+            (VMEM, shape((2, 1024, 128))),
+            (VMEM, shape((PAIR, 1024))),
+            (VMEM, shape((2, 32, 128), jnp.int32)),
         ],
         [
             (SMEM, seg_blocks), (SMEM, mb_sizes), (SMEM, mb_receiver),
             (VMEM, q), (HBM, kv_kept), (HBM, o), (VMEM, log_total), (VMEM, gp),
         ],
         [
-            pltpu.VMEM((2, 32, 128), jnp.int32),
             pltpu.SMEM((4, 2), jnp.int32),
             pltpu.VMEM((2, PAIR, 3072), BF16),
             pltpu.VMEM((PAIR, 1024), BF16),
-            pltpu.VMEM((2, 1024, 128), BF16),
-            pltpu.VMEM((2, 128, 3072), BF16),
-            pltpu.VMEM((2, 128, 3072), BF16),
-            pltpu.VMEM((2, 3072, 128), BF16),
-            pltpu.VMEM((2, 1024, 128), BF16),
-            pltpu.VMEM((PAIR, 1024), BF16),
-            pltpu.VMEM((2, PAIR, 3072), F32),
+            pltpu.VMEM((2, 128, 2048), BF16),
+            pltpu.VMEM((2, 128, 2048), BF16),
+            pltpu.VMEM((2, 2048, 128), BF16),
+            pltpu.VMEM((2, HEAD_DIM, 2048), F32),
+            pltpu.VMEM((2, HEAD_DIM, 2048), F32),
         ],
         copies=2,
-        limit=26,
+        limit=22,
     )
     arrived, gx_all, weights = call(
         tail_body,
@@ -861,7 +928,8 @@
             (VMEM, shape((2, 40, 640), F32)),
         ],
         [
-            (VMEM, dq), (VMEM, dkv), (VMEM, start_rows), (VMEM, here), (HBM, glt), (HBM, att_own),
+            (VMEM, dkv), (VMEM, start_rows), (VMEM, here), (VMEM, dq), (VMEM, qrow), (VMEM, grow),
+            (VMEM, gnat), (VMEM, spans), (VMEM, q), (HBM, kv_kept), (HBM, glt), (HBM, att_own),
             (HBM, table), (HBM, grad_layer), (HBM, tokens), (VMEM, norm_gain), (HBM, w_rows),
             (HBM, normed_t),
         ],
@@ -871,7 +939,16 @@
             pltpu.VMEM((512, 1280), BF16),
             pltpu.VMEM((3, 320, 1280), BF16),
             pltpu.VMEM((1280, 512), BF16),
-            pltpu.VMEM((2, 3, 2, 2, PAIR, 256), BF16),
+            pltpu.VMEM((2, PAIR, 1024), BF16),
+            pltpu.VMEM((2, 128, 1024), BF16),
+            pltpu.VMEM((2, 128, 1024), BF16),
+            pltpu.VMEM((2, 1024, 128), BF16),
+            pltpu.VMEM((2, HEAD_DIM, 1024), F32),
+            pltpu.VMEM((2, HEAD_DIM, 1024), F32),
+            pltpu.VMEM((2, 1024, 128), F32),
+            pltpu.VMEM((2, 2, 3, PAIR, 256), BF16),
+            pltpu.VMEM((2, 3, PAIR, 256), BF16),
+            pltpu.VMEM((2, 2, 2, 2, PAIR, 256), BF16),
             pltpu.VMEM((960, 512), BF16),
             pltpu.VMEM((256, 960), BF16),
             pltpu.VMEM((2, 4, 64, 1280), BF16),
@@ -896,7 +973,7 @@
         ],
         copies=112,
         number=3,
-        limit=42,
+        limit=48,
     )
     grad_x, grad_w_qkv, grad_w_out, delivered = call(
         results_body,

time: 141 us -> 137 us (0.972)
  Pallas kernels: 135 us -> 129 us
  local copies, waits for them, and re-layouts: 4.88 us -> 7.24 us
    pallas_call x6, Pallas kernels: 135 us -> 129 us  [call(): pl.pallas_call(body, out_shape=[array for _, array in outs], in_specs=[pl...]
    unnamed x24 -> x30, local copies, waits for them, and re-layouts: 4.88 us -> 7.24 us
where the time goes in v4:
time: 137 us
  Pallas kernels  129 us (94%)
  local copies, waits for them, and re-layouts  7.24 us (5%)
    pallas_call x6, Pallas kernels, call(): pl.pallas_call(body, out_shape=[array for _, array in outs], in_specs=[pl...  129 us
    unnamed x30, local copies, waits for them, and re-layouts  7.24 us

profile of v4, /device:TPU:1, one launch (start us, length us, event | category | flops | bytes accessed | tf_op | source)
XLA Modules:
  0.0 136.7 jit_solution(11353971629344057781)
XLA Ops:
  0.6 0.0 copy-start
  0.6 1.3 copy-done
  2.0 0.0 copy-start.2
  2.0 1.7 %copy-done.2 = bf16[3,1280,320]{1,2,0:T(8,128)(2,1)S(1)} copy-done((bf16[3,1280,320]{1,2,0:T(8,128)(2,1)S(1)}, bf16[3,1280,320]{1,2,0:T(8,128)(2,1)}, u32[]{:S(2)}) %copy-start.2) | copy-done | bytes 2457624
  3.6 1.1 copy-done.8
  4.8 0.7 copy-done.9
  5.5 28.4 %shard_map.120 = (bf16[160,1024]{1,0:T(8,128)(2,1)S(1)}, bf16[2,160,3072]{2,1,0:T(8,128)(2,1)S(1)}, bf16[1280,512]{1,0:T(8,128)(2,1)S(1)}, bf16[1280,1280]{1,0:T(8,128)(2,1)S(1)}) custom-call(bf16[512,1280]{1,0:T(8,128)(2,1)S(1)} %copy-done, bf16[1280]{0:T(1024)(128)(2,1)S(1)} %copy-done.9, bf16[3,320,1280]{2,1,0:T(8,128)(2,1)S(1)} %bitcast.3, ...), custom_call_target="tpu_custom_call" | custom-call | tf_op jit(solution)/shard_map/pallas_call | solution.py:85
  33.9 0.0 copy-start.4
  33.9 0.0 copy-start.1
  33.9 0.0 copy-start.11
  34.0 0.0 copy-done.12
  34.0 11.4 %shard_map.121 = (bf16[160,1024]{1,0:T(8,128)(2,1)S(1)}, bf16[2,160,3072]{2,1,0:T(8,128)(2,1)S(1)}, bf16[2,4,160,128]{3,2,1,0:T(8,128)(2,1)S(1)}, f32[2,1024]{1,0:T(2,128)S(1)}) custom-call(s32[32]{0:T(128)S(1)} %copy-done.12, bf16[160,1024]{1,0:T(8,128)(2,1)S(1)} %get-tuple-element.32.q_ref, bf16[2,160,3072]{2,1,0:T(8,128)(2,1)S(1)} %get-tuple-element.33.kv_ref), custom_call_target="tpu_custom_call" | custom-call | tf_op jit(solution)/shard_map/pallas_call | solution.py:85
  45.3 0.0 copy-done.4
  45.4 0.0 copy-start.3
  45.4 0.0 copy-done.7
  45.4 0.0 copy-done.1
  45.4 0.0 copy-done.11
  45.4 0.0 copy-start.13
  45.4 0.0 copy-start.14
  45.4 24.4 %shard_map.122 = (bf16[2,4,160,128]{3,2,1,0:T(8,128)(2,1)S(1)}, bf16[128,1280]{1,0:T(8,128)(2,1)S(1)}, bf16[1280,128]{1,0:T(8,128)(2,1)S(1)}, bf16[2,4,160,128]{...) custom-call(bf16[2,4,160,128]{3,2,1,0:T(8,128)(2,1)S(1)} %get-tuple-element.37.op_ref, ...), custom_call_target="tpu_custom_call" | custom-call | tf_op jit(solution)/shard_map/pallas_call | solution.py:85
  69.8 0.0 copy-done.3
  69.8 0.0 copy-done.13
  69.9 0.0 copy-done.14
  69.9 0.0 copy-start.10
  69.9 2.9 %shard_map.123 = (f32[2,1024,128]{2,1,0:T(8,128)S(1)}, bf16[2,160,2048]{2,1,0:T(8,128)(2,1)S(1)}, s32[512,128]{1,0:T(8,128)S(1)}, s32[16,512]{1,0:T(8,128)S(1)},...) custom-call(s32[32]{0:T(128)S(1)} %copy-done.12, ...), custom_call_target="tpu_custom_call" | custom-call | tf_op jit(solution)/shard_map/pallas_call | solution.py:85
  72.8 0.0 copy-start.5
  72.8 1.0 copy-done.5
  73.8 0.0 copy-done.10
  73.8 59.8 %shard_map.124 = (bf16[256,1280]{1,0:T(8,128)(2,1)S(1)}, bf16[2,4,64,1280]{3,2,1,0:T(8,128)(2,1)}, f32[2,40,640]{2,1,0:T(8,128)S(1)}) custom-call(bf16[2,160,2048]{2,1,0:T(8,128)(2,1)} %copy-done.5, s32[512,128]{1,0:T(8,128)S(1)} %get-tuple-element.41.starts_ref, s32[16,512]{1,0:T(8,128)S(1)} %get-tuple-element.42.live_ref, ...), custom_call_target="tpu_custom_call" | custom-call | tf_op jit(solution)/shard_map/pallas_call | solution.py:85
  133.6 0.0 copy-start.6
  133.6 1.3 copy-done.6
  134.9 1.8 %shard_map.125 = (bf16[512,1280]{1,0:T(8,128)(2,1)}, f32[3,40,320]{2,1,0:T(8,128)}, f32[40,320]{1,0:T(8,128)}, bf16[256,1280]{1,0:T(8,128)(2,1)}) custom-call(bf16[2,4,64,1280]{3,2,1,0:T(8,128)(2,1)S(1)} %copy-done.6, f32[2,40,640]{2,1,0:T(8,128)S(1)} %get-tuple-element.54.both_ref, bf16[256,1280]{1,0:T(8,128)(2,1)S(1)} %get-tuple-element.55.arrived_ref), custom_call_target="tpu_custom_call" | custom-call | tf_op jit(solution)/shard_map/pallas_call | solution.py:85
  (4 shorter events, 0.0 us)
Async XLA Ops:
  0.6 1.3 copy-start
  2.0 1.7 %copy-start.2 = (bf16[3,1280,320]{1,2,0:T(8,128)(2,1)S(1)}, bf16[3,1280,320]{1,2,0:T(8,128)(2,1)}, u32[]{:S(2)}) copy-start(bf16[3,1280,320]{1,2,0:T(8,128)(2,1)} %param.11) | copy-start | bytes 7372804
  3.6 1.1 copy-start.8
  4.8 0.7 copy-start.9
  5.5 28.5 %copy-start.12 = (s32[32]{0:T(128)S(1)}, s32[32]{0:T(128)}, u32[]{:S(2)}) copy-start(s32[32]{0:T(128)} %seg_ref.3) | copy-start | bytes 388
  5.5 39.9 %copy-start.7 = (bf16[128,5120]{1,0:T(8,128)(2,1)S(1)}, bf16[128,5120]{1,0:T(8,128)(2,1)}, u32[]{:S(2)}) copy-start(bf16[128,5120]{1,0:T(8,128)(2,1)} %mgrad_hbm.1) | copy-start | bytes 3932164
  33.9 11.4 %copy-start.4 = (bf16[1280,512]{1,0:T(8,128)(2,1)}, bf16[1280,512]{1,0:T(8,128)(2,1)S(1)}, u32[]{:S(2)}) copy-start(bf16[1280,512]{1,0:T(8,128)(2,1)S(1)} %get-tuple-element.52.normed_t_hbm) | copy-start | bytes 3932164
  33.9 11.4 %copy-start.1 = (bf16[512,1280]{1,0:T(8,128)(2,1)S(1)}, bf16[512,1280]{1,0:T(8,128)(2,1)}, u32[]{:S(2)}) copy-start(bf16[512,1280]{1,0:T(8,128)(2,1)} %tokens_hbm.5) | copy-start | bytes 3932164
  33.9 11.4 %copy-start.11 = (bf16[1280]{0:T(1024)(128)(2,1)S(1)}, bf16[1280]{0:T(1024)(128)(2,1)}, u32[]{:S(2)}) copy-start(bf16[1280]{0:T(1024)(128)(2,1)} %gain_ref.4) | copy-start | bytes 7684
  45.4 24.5 %copy-start.3 = (bf16[2,160,3072]{2,1,0:T(8,128)(2,1)}, bf16[2,160,3072]{2,1,0:T(8,128)(2,1)S(1)}, u32[]{:S(2)}) copy-start(bf16[2,160,3072]{2,1,0:T(8,128)(2,1)S(1)} %get-tuple-element.34.kv_hbm) | copy-start | bytes 5898244
  45.4 24.4 %copy-start.13 = (s32[32]{0:T(128)S(1)}, s32[32]{0:T(128)}, u32[]{:S(2)}) copy-start(s32[32]{0:T(128)} %sizes_ref.1) | copy-start | bytes 388
  45.4 24.4 %copy-start.14 = (s32[32]{0:T(128)S(1)}, s32[32]{0:T(128)}, u32[]{:S(2)}) copy-start(s32[32]{0:T(128)} %receiver_ref.1) | copy-start | bytes 388
  69.9 4.0 %copy-start.10 = (bf16[1280]{0:T(1024)(128)(2,1)S(1)}, bf16[1280]{0:T(1024)(128)(2,1)}, u32[]{:S(2)}) copy-start(bf16[1280]{0:T(1024)(128)(2,1)} %gain_ref.5) | copy-start | bytes 7684
  72.8 1.1 copy-start.5
  133.6 1.3 copy-start.6

commit v5 on v4

--- a/solution.py
+++ b/solution.py
@@ -101,13 +101,16 @@
 
 
 def project_body(
-    tokens_hbm, gain_ref, w_hbm, w_out_hbm, q_ref, kv_ref, normed_t_hbm, w_full,
-    tokens_ref, w_ref, normed_ref, normed_t_ref, out_ref, send, recv,
+    seg_ref, tokens_hbm, gain_hbm, w_hbm, w_out_hbm,
+    q_hbm, kv_hbm, normed_t_hbm, w_full, qrow_hbm, sums_hbm, norms_hbm,
+    tokens_ref, gain_ref, w_ref, normed_t_ref, out_ref,
+    q_ref, kv_ref, spans_ref, qrow, kx, vrow, sums_ref, norms_ref, send, recv,
 ):
     section, chip, core = place()
     copies = Copies(send, recv)
     load_tokens = copies.start(tokens_hbm, tokens_ref, None)
     load_w = copies.start(w_hbm, w_ref, None)
+    load_gain = copies.start(gain_hbm, gain_ref, None)
     greet(halo_peers(section, chip, core) + section_peers(section, chip, core)[::2])
     mate = dev(chip, 1 - core, section)
     ahead, behind = (section + 1) % 4, (section + 3) % 4
@@ -119,54 +122,139 @@
     mine = w_out_hbm.at[pl.ds(pl.multiple_of(core * PAIR, 16), PAIR), :]
     to_ahead = copies.start(mine, w_rows(section, 0, PAIR), ahead_dev)
     to_behind = copies.start(mine, w_rows(section, 0, PAIR), behind_dev)
-    keep = w_full.at[pl.ds(pl.multiple_of(section * 320, 16), 320), :]
-    waits = [copies.start(w_out_hbm, keep, None)]
+    waits, inner = [], []
+    image_spans(seg_ref, spans_ref)
     load_tokens.wait()
+    load_gain.wait()
     gain = gain_ref[...].reshape(1, 1280).astype(F32)
     for tile in range(4):
         rows = pl.ds(tile * 128, 128)
         values = tokens_ref[rows, :].astype(F32)
         centered = values - jnp.mean(values, axis=1, keepdims=True)
         inv = lax.rsqrt(jnp.mean(centered * centered, axis=1, keepdims=True) + EPS)
-        normed_ref[rows, :] = (centered * inv * gain).astype(BF16)
+        normed_t_ref[:, rows] = (centered * inv * gain).astype(BF16).T
     own = pl.ds(pl.multiple_of(core * PAIR, 16), PAIR)
     other = pl.ds(pl.multiple_of((1 - core) * PAIR, 16), PAIR)
     load_w.wait()
     for which in (1, 2, 0):
-        out = dot_nt(w_ref[which], normed_ref[...])
+        out = dot_nn(w_ref[which], normed_t_ref[...])
         if which == 0:
             out = out * (FACTOR * LOG2E)
         out_ref[which] = out.astype(BF16)
+        mine = pl.ds(pl.multiple_of(core * 512, 512), 512)
+        target = q_ref.at[:, mine]
         if which:
             for step, base in ((1, 0), (-1, 2048)):
                 lanes = pl.ds(pl.multiple_of(base + core * 512, 512), 512)
-                for rows, target in ((own, core), (other, 1 - core)):
-                    device = dev(around(chip, step), target, section)
+                for rows, to_core in ((own, core), (other, 1 - core)):
+                    device = dev(around(chip, step), to_core, section)
                     waits.append(
-                        copies.start(out_ref.at[which, rows, :], kv_ref.at[which - 1, :, lanes], device)
+                        copies.start(out_ref.at[which, rows, :], kv_hbm.at[which - 1, :, lanes], device)
                     )
-            lanes = pl.ds(pl.multiple_of(1024 + core * 512, 512), 512)
-            target = kv_ref.at[which - 1, :, lanes]
-        else:
-            target = q_ref.at[:, pl.ds(pl.multiple_of(core * 512, 512), 512)]
-        waits.append(copies.start(out_ref.at[which, other, :], target, mate))
-        waits.append(copies.start(out_ref.at[which, own, :], target, None))
-    for tile in range(4):
-        rows = pl.ds(tile * 128, 128)
-        normed_t_ref[:, rows] = normed_ref[rows, :].T
+            target = kv_ref.at[which - 1, :, mine]
+        inner.append(copies.start(out_ref.at[which, other, :], target, mate))
+        inner.append(copies.start(out_ref.at[which, own, :], target, None))
     waits.append(copies.start(normed_t_ref, normed_t_hbm, None))
-
+    wait_all(inner)
+    waits.append(copies.start(q_ref, q_hbm, None))
+    waits.append(copies.start(kv_ref, kv_hbm.at[:, :, 1024:2048], None))
+    first = chip * 1024
+    for block in range(4):
+        lanes = pl.ds(block * 256, 256)
+        build_queries(spans_ref, first + block * 256, q_ref, lanes, qrow)
+        build_values(spans_ref, first + block * 256, kv_ref, lanes, kx, vrow, lanes)
+    for head in range(2):
+        feats = pl.ds(head * HEAD_DIM, HEAD_DIM)
+        for which, values in enumerate((q_ref[feats, :], kv_ref[0, feats, :])):
+            norms_ref[which * 2 + head, :, :] = squares(values)
+
+    def tile_step(tile, carry):
+        rows = pl.ds(pl.multiple_of(tile * 256, 256), 256)
+        sums = (jnp.zeros((256, 128), F32),) * 2
+        for chunk in range(0, 4, 2):
+            lanes = [pl.ds((chunk + which) * CHUNK, CHUNK) for which in range(2)]
+            sums = forward_step(rows, lanes, qrow, kx, vrow, sums)
+        for head in range(2):
+            sums_ref[head, rows, :] = sums[head]
+        return carry
+
+    lax.fori_loop(0, 2, tile_step, 0)
     to_ahead.wait()
     relay = [copies.start(w_rows(behind, 0, 80), w_rows(behind, 0, 80), ahead_dev)]
     to_behind.wait()
     relay.append(copies.start(w_rows(ahead, 80, 80), w_rows(ahead, 80, 80), behind_dev))
     waits.append(copies.start(w_rows(behind, 0, PAIR), w_rows(behind, 0, PAIR), mate))
     waits.append(copies.start(w_rows(ahead, 0, PAIR), w_rows(ahead, 0, PAIR), mate))
+    lax.fori_loop(2, 4, tile_step, 0)
+    waits.append(copies.start(qrow, qrow_hbm, None))
+    waits.append(copies.start(sums_ref, sums_hbm, None))
+    waits.append(copies.start(norms_ref, norms_hbm, None))
     far = (section + 2) % 4
     for copy, start in zip(relay, (0, 80)):
         copy.wait()
         waits.append(copies.start(w_rows(far, start, 80), w_rows(far, start, 80), mate))
     wait_all(waits)
+
+
+def image_spans(seg_ref, spans_ref):
+    row = lax.broadcasted_iota(jnp.int32, (32, 128), 0)
+    begins, ends = jnp.zeros((32, 128), jnp.int32), jnp.zeros((32, 128), jnp.int32)
+    end = jnp.int32(0)
+    for image in range(32):
+        begin = end
+        end = begin + 64 * seg_ref[image]
+        begins = jnp.where(row == image, begin, begins)
+        ends = jnp.where(row == image, end, ends)
+    spans_ref[0] = begins
+    spans_ref[1] = ends
+
+
+def squares(values):
+    values = values.astype(F32)
+    total = jnp.sum(values * values, axis=0, keepdims=True)
+    blocks = [total[:, start : start + 128] for start in range(0, total.shape[1], 128)]
+    top = blocks[0]
+    for block in blocks[1:]:
+        top = jnp.maximum(top, block)
+    return jnp.broadcast_to(top, (8, 128))
+
+
+def build_queries(spans_ref, position, q_ref, lanes, qrow):
+    inside = membership(spans_ref, position, 256)
+    for head in range(2):
+        joined = jnp.concatenate(
+            [
+                q_ref[pl.ds(head * HEAD_DIM, HEAD_DIM), lanes],
+                jnp.where(inside, 0.0, BIG).astype(BF16),
+                jnp.zeros((16, 256), BF16),
+            ],
+            axis=0,
+        )
+        qrow[head, lanes, :] = joined.T
+
+
+def build_values(spans_ref, position, kv_ref, lanes, kx, vrow, into):
+    ones = jnp.where(lax.broadcasted_iota(jnp.int32, (16, CHUNK), 0) < 3, 1.0, 0.0).astype(BF16)
+    hot = jnp.where(membership(spans_ref, position, CHUNK), 1.0, 0.0).astype(BF16)
+    for head in range(2):
+        feats = pl.ds(head * HEAD_DIM, HEAD_DIM)
+        kx[head, :, into] = jnp.concatenate([kv_ref[0, feats, lanes], hot, ones], axis=0)
+        joined = jnp.concatenate(
+            [kv_ref[1, feats, lanes], ones, jnp.zeros((32, CHUNK), BF16)], axis=0
+        )
+        vrow[head, into, :] = joined.T
+
+
+def forward_step(rows, chunks, qrow, kx, vrow, sums):
+    pairs = [(head, lanes) for lanes in chunks for head in range(2)]
+    probs = [
+        jnp.exp2(dot_nn(qrow[head, rows, :], kx[head, :, lanes])).astype(BF16)
+        for head, lanes in pairs
+    ]
+    sums = list(sums)
+    for (head, lanes), part in zip(pairs, probs):
+        sums[head] = sums[head] + dot_nn(part, vrow[head, lanes, :])
+    return tuple(sums)
 
 
 def spans_and_bounds(seg_ref, first, spans_ref, bounds_ref):
@@ -211,68 +299,44 @@
 
 
 def forward_body(
-    seg_ref, q_ref, kv_ref, o_hbm, kv_hbm, op_ref, log_ref,
-    spans_ref, bounds_ref, o_ref, qrow, kx, vrow, sems,
+    seg_ref, kv_hbm, qrow_hbm, sums_hbm, norms_hbm, o_hbm, op_hbm, log_hbm,
+    spans_ref, bounds_ref, o_ref, kv_ref, qrow, kx, vrow, sums_ref, norms_ref, op_ref, log_ref, sems,
 ):
     first = (lax.axis_index("seq") // 2) * 1024
-    keep = pltpu.make_async_copy(kv_ref, kv_hbm, sems.at[0])
-    keep.start()
+    loads = [
+        pltpu.make_async_copy(source, target, sems.at[index])
+        for index, (source, target) in enumerate(
+            (
+                (kv_hbm.at[:, :, 0:1024], kv_ref.at[:, :, 0:1024]),
+                (kv_hbm.at[:, :, 2048:3072], kv_ref.at[:, :, 2048:3072]),
+                (qrow_hbm, qrow),
+                (norms_hbm, norms_ref),
+                (sums_hbm, sums_ref),
+            )
+        )
+    ]
+    for load in loads:
+        load.start()
     spans_and_bounds(seg_ref, first, spans_ref, bounds_ref)
-    longest = []
-    for head in range(2):
-        feats = pl.ds(head * HEAD_DIM, HEAD_DIM)
-        for block in range(4):
-            lanes = pl.ds(block * 256, 256)
-            inside = membership(spans_ref, first + block * 256, 256)
-            joined = jnp.concatenate(
-                [
-                    q_ref[feats, lanes],
-                    jnp.where(inside, 0.0, BIG).astype(BF16),
-                    jnp.zeros((16, 256), BF16),
-                ],
-                axis=0,
-            )
-            qrow[head, lanes, :] = joined.T
-        values = q_ref[feats, :].astype(F32)
-        longest.append(jnp.max(jnp.sum(values * values, axis=0, keepdims=True)))
-
-    ones = jnp.where(lax.broadcasted_iota(jnp.int32, (16, CHUNK), 0) < 3, 1.0, 0.0).astype(BF16)
+    perm = permutation(False)
+    for load in loads:
+        load.wait()
+
+    def outside(low, high, step, carry):
+        carry = lax.fori_loop(low, jnp.minimum(high, 4), step, carry)
+        return lax.fori_loop(jnp.maximum(low, 8), high, step, carry)
 
     def build(chunk, tops):
-        found = []
         lanes = pl.ds(pl.multiple_of(chunk * CHUNK, CHUNK), CHUNK)
-        inside = membership(spans_ref, first - 1024 + chunk * CHUNK, CHUNK)
-        hot = jnp.where(inside, 1.0, 0.0).astype(BF16)
-        for head in range(2):
-            feats = pl.ds(head * HEAD_DIM, HEAD_DIM)
-            kx[head, 0:80, lanes] = kv_ref[0, feats, lanes]
-            kx[head, 80:112, lanes] = hot
-            kx[head, 112:128, lanes] = ones
-            joined = jnp.concatenate(
-                [kv_ref[1, feats, lanes], ones, jnp.zeros((32, CHUNK), BF16)], axis=0
-            )
-            vrow[head, lanes, :] = joined.T
-            values = kv_ref[0, feats, lanes].astype(F32)
-            found.append(jnp.maximum(tops[head], jnp.sum(values * values, axis=0, keepdims=True)))
-        return tuple(found)
-
-    start = jnp.zeros((1, CHUNK), F32)
-    tops = lax.fori_loop(bounds_ref[0, 0], bounds_ref[3, 1], build, (start, start))
-    small = longest[0] * jnp.max(tops[0]) <= SAFE * SAFE
-    small = small & (longest[1] * jnp.max(tops[1]) <= SAFE * SAFE)
-    lane = lax.broadcasted_iota(jnp.int32, (256, 128), 1)
-
-    def sum_tile(tile, rows):
-        def sum_step(chunk, sums):
-            lanes = pl.ds(pl.multiple_of(chunk * CHUNK, CHUNK), CHUNK)
-            probs = [
-                jnp.exp2(dot_nn(qrow[head, rows, :], kx[head, :, lanes])).astype(BF16)
-                for head in range(2)
-            ]
-            return tuple(sums[head] + dot_nn(probs[head], vrow[head, lanes, :]) for head in range(2))
-
-        start = jnp.zeros((256, 128), F32)
-        return lax.fori_loop(bounds_ref[tile, 0], bounds_ref[tile, 1], sum_step, (start, start))
+        build_values(spans_ref, first - 1024 + chunk * CHUNK, kv_ref, lanes, kx, vrow, lanes)
+        return tuple(
+            jnp.maximum(tops[head], squares(kv_ref[0, pl.ds(head * HEAD_DIM, HEAD_DIM), lanes]))
+            for head in range(2)
+        )
+
+    tops = outside(bounds_ref[0, 0], bounds_ref[3, 1], build, (norms_ref[2], norms_ref[3]))
+    small = jnp.max(norms_ref[0]) * jnp.max(tops[0]) <= SAFE * SAFE
+    small = small & (jnp.max(norms_ref[1]) * jnp.max(tops[1]) <= SAFE * SAFE)
 
     def write(head, rows, sums, top_row):
         out = sums.T
@@ -282,10 +346,18 @@
 
     def plain_step(tile, carry):
         rows = pl.ds(pl.multiple_of(tile * 256, 256), 256)
-        sums = sum_tile(tile, rows)
+
+        def step(chunk, sums):
+            lanes = pl.ds(pl.multiple_of(chunk * CHUNK, CHUNK), CHUNK)
+            return forward_step(rows, [lanes], qrow, kx, vrow, sums)
+
+        start = (sums_ref[0, rows, :], sums_ref[1, rows, :])
+        sums = outside(bounds_ref[tile, 0], bounds_ref[tile, 1], step, start)
         for head in range(2):
             write(head, rows, sums[head], 0.0)
         return carry
+
+    lane = lax.broadcasted_iota(jnp.int32, (256, 128), 1)
 
     def shifted_step(tile, carry):
         low, high = bounds_ref[tile, 0], bounds_ref[tile, 1]
@@ -310,7 +382,12 @@
             moved = jnp.where(lane == 113, part_two, moved)
             qrow[head, rows, :] = jnp.where(lane == 114, part_three, moved).astype(BF16)
 
-        sums = sum_tile(tile, rows)
+        def step(chunk, sums):
+            lanes = pl.ds(pl.multiple_of(chunk * CHUNK, CHUNK), CHUNK)
+            return forward_step(rows, [lanes], qrow, kx, vrow, sums)
+
+        start = jnp.zeros((256, 128), F32)
+        sums = lax.fori_loop(low, high, step, (start, start))
         for head in range(2):
             write(head, rows, sums[head], jnp.max(tops[head].T, axis=0, keepdims=True))
         return carry
@@ -321,17 +398,29 @@
 
     @pl.when(jnp.logical_not(small))
     def _():
+        middle = pltpu.make_async_copy(
+            kv_hbm.at[:, :, 1024:2048], kv_ref.at[:, :, 1024:2048], sems.at[5]
+        )
+        middle.start()
+        middle.wait()
+        for chunk in range(4, 8):
+            lanes = pl.ds(chunk * CHUNK, CHUNK)
+            build_values(spans_ref, first - 1024 + chunk * CHUNK, kv_ref, lanes, kx, vrow, lanes)
         lax.fori_loop(0, 4, shifted_step, 0)
 
-    keep_o = pltpu.make_async_copy(o_ref, o_hbm, sems.at[1])
+    keep_o = pltpu.make_async_copy(o_ref, o_hbm, sems.at[6])
+    keep_log = pltpu.make_async_copy(log_ref, log_hbm, sems.at[7])
     keep_o.start()
-    perm = permutation(False)
+    keep_log.start()
     for half in range(2):
         moved = dot_nn(o_ref[:, half * 512 : half * 512 + 512], perm).astype(BF16)
         for part in range(4):
             op_ref[half, part] = moved[:, part * 128 : part * 128 + 128]
-    keep.wait()
+    keep_op = pltpu.make_async_copy(op_ref, op_hbm, sems.at[8])
+    keep_op.start()
     keep_o.wait()
+    keep_log.wait()
+    keep_op.wait()
 
 
 def build_keys(spans_ref, position, kv_ref, lanes, kx, vx, krow, into):
@@ -366,16 +455,22 @@
 
 
 def backward_body(
-    seg_ref, sizes_ref, receiver_ref, q_ref, kv_hbm, o_hbm, log_ref, gp_ref,
-    dq_ref, dkv_ref, starts_ref, here_ref, qrow, grow, gnat, spans_ref,
-    bounds_ref, kv_ref, o_ref, kx, vx, krow, dk_acc, dv_acc, sems,
+    seg_ref, sizes_ref, receiver_ref, q_hbm, kv_hbm, o_hbm, log_hbm, gp_hbm,
+    dq_hbm, dkv_hbm, starts_hbm, here_hbm, qrow_hbm, grow_hbm, gnat_hbm, spans_hbm,
+    dq_ref, dkv_ref, starts_ref, here_ref, qrow, grow, gnat, spans_ref, bounds_ref, q_ref, kv_ref, o_ref, log_ref, gp_ref, kx, vx, krow, dk_acc, dv_acc, sems,
 ):
     seq = lax.axis_index("seq")
     first = (seq // 2) * 1024
     load_kv = pltpu.make_async_copy(kv_hbm, kv_ref, sems.at[0])
     load_o = pltpu.make_async_copy(o_hbm, o_ref, sems.at[1])
+    load_q = pltpu.make_async_copy(q_hbm, q_ref, sems.at[2])
     load_kv.start()
     load_o.start()
+    load_q.start()
+    load_log = pltpu.make_async_copy(log_hbm, log_ref, sems.at[3])
+    load_log.start()
+    load_gp = pltpu.make_async_copy(gp_hbm, gp_ref, sems.at[4])
+    load_gp.start()
     spans_and_bounds(seg_ref, first, spans_ref, bounds_ref)
     start = jnp.int32(0)
     my_start, my_size = jnp.int32(0), jnp.int32(0)
@@ -388,11 +483,14 @@
     here_ref[0:8, :] = jnp.full((8, 512), my_start)
     here_ref[8:16, :] = jnp.full((8, 512), my_size)
     back = permutation(True)
+    load_gp.wait()
     for half in range(2):
         joined = jnp.concatenate([gp_ref[half, part] for part in range(4)], axis=1)
         gnat[:, half * 512 : half * 512 + 512] = dot_nn(joined, back).astype(BF16)
     load_kv.wait()
     load_o.wait()
+    load_q.wait()
+    load_log.wait()
     for head in range(2):
         feats = pl.ds(head * HEAD_DIM, HEAD_DIM)
         for block in range(4):
@@ -416,6 +514,18 @@
             )
             grow[head, lanes, :] = joined.T
 
+    keeps = [
+        pltpu.make_async_copy(source, target, sems.at[5 + index])
+        for index, (source, target) in enumerate(
+            (
+                (starts_ref, starts_hbm), (here_ref, here_hbm), (spans_ref, spans_hbm),
+                (gnat, gnat_hbm), (qrow, qrow_hbm), (grow, grow_hbm),
+            )
+        )
+    ]
+    for keep in keeps:
+        keep.start()
+
     def outside(low, high, step, carry):
         carry = lax.fori_loop(low, jnp.minimum(high, 4), step, carry)
         return lax.fori_loop(jnp.maximum(low, 8), high, step, carry)
@@ -449,23 +559,34 @@
         return carry
 
     lax.fori_loop(0, 4, tile_step, 0)
+    keeps.append(pltpu.make_async_copy(dq_ref, dq_hbm, sems.at[12]))
+    keeps[-1].start()
     for head in range(2):
         feats = pl.ds(head * HEAD_DIM, HEAD_DIM)
         dkv_ref[0, feats, :] = (dk_acc[head] * LN2).astype(BF16)
         dkv_ref[1, feats, :] = dv_acc[head].astype(BF16)
+    keeps.append(pltpu.make_async_copy(dkv_ref, dkv_hbm, sems.at[11]))
+    keeps[-1].start()
+    for keep in keeps:
+        keep.wait()
 
 
 def middle_body(
-    op_ref, w_hbm, tokens_hbm, mgrad_hbm, gain_ref,
+    op_ref, w_hbm, w_out_hbm, tokens_hbm, mgrad_hbm, gain_hbm,
     gp_ref, gl_hbm, glt_hbm, own_ref, table_ref,
-    w_ref, tokens_ref, mgrad_ref, gl_ref, glt_ref, att, gat, packed, send, recv,
+    w_ref, tokens_ref, mgrad_ref, gain_ref, gl_ref, glt_ref, att, gat, packed, send, recv,
 ):
     section, chip, core = place()
     copies = Copies(send, recv)
     columns = pl.ds(pl.multiple_of(section * 1280, 128), 1280)
+    load_gain = copies.start(gain_hbm, gain_ref, None)
     load_mgrad = copies.start(mgrad_hbm.at[:, columns], mgrad_ref, None)
     load_tokens = copies.start(tokens_hbm, tokens_ref, None)
-    load_w = copies.start(w_hbm, w_ref, None)
+    loads = []
+    for step in range(4):
+        w_rows = pl.ds(pl.multiple_of((section + step) % 4 * 320, 16), 320)
+        source = w_hbm.at[w_rows, :] if step else w_out_hbm
+        loads.append(copies.start(source, w_ref.at[w_rows, :], None))
     greet(row_peers(section, chip, core) + core_peers(section, chip, core))
     rows = pl.ds(pl.multiple_of((section * 2 + core) * PAIR, 16), PAIR)
     waits = []
@@ -474,14 +595,12 @@
             to_section, to_core = (section + step) % 4, (core + turn) % 2
             device = dev(chip, to_core, to_section) if step or turn else None
             waits.append(copies.start(op_ref.at[to_core, to_section], att.at[rows, :], device))
-    late = [
-        copies.start(op_ref.at[1 - core], own_ref.at[core], dev(chip, 1 - core, section)),
-        copies.start(op_ref.at[core], own_ref.at[core], None),
-    ]
+    late = [copies.start(op_ref.at[1 - core], own_ref, dev(chip, 1 - core, section))]
     row = lax.broadcasted_iota(jnp.int32, (128, 512), 0)
     column = lax.broadcasted_iota(jnp.int32, (128, 512), 1)
     chosen = jnp.where(column == 4 * row + section, 1.0, 0.0).astype(BF16)
     load_tokens.wait()
+    load_gain.wait()
     load_mgrad.wait()
     values = dot_nn(chosen, tokens_ref[...])
     gain = gain_ref[...].reshape(1, 1280).astype(F32)
@@ -490,7 +609,7 @@
     row = lax.broadcasted_iota(jnp.int32, (128, 128), 0)
     column = lax.broadcasted_iota(jnp.int32, (128, 128), 1)
     order = jnp.where(column == 16 * (row % 8) + row // 8, 1.0, 0.0).astype(BF16)
-    load_w.wait()
+    wait_all(loads)
     wait_all(waits)
     layer = values + dot_nn(att[...].T, w_ref[...])
     centered = layer - jnp.mean(layer, axis=1, keepdims=True)
@@ -523,11 +642,12 @@
 
 
 def tail_body(
-    dkv_ref, starts_ref, live_ref, dq_ref, qrow, grow, gnat, spans_ref, q_ref, kv_hbm,
-    glt_hbm, own_hbm, table_hbm, gl_hbm, tokens_hbm, gain_ref, w_hbm, normed_t_hbm,
-    delivered_ref, gx_all, weights_ref,
+    dkv_ref, starts_hbm, live_hbm, dq_hbm, qrow_hbm, grow_hbm, gnat_hbm, spans_hbm, q_hbm, kv_hbm,
+    glt_hbm, op_hbm, own_hbm, table_hbm, gl_hbm, tokens_hbm, gain_hbm, w_hbm, normed_t_hbm,
+    delivered_hbm, gx_all, weights_ref,
+    starts_ref, live_ref, qrow, grow, gnat, spans_ref, gain_ref, delivered_ref,
     table_ref, gl_ref, tokens_ref, w_ref, normed_t_ref,
-    kv_ref, kx, vx, krow, dk_acc, dv_acc, dq_acc, own_out, mate_in,
+    q_ref, kv_ref, kx, vx, krow, dk_acc, dv_acc, dq_acc, own_out, mate_in,
     dkv_in, dj, rows_ref, gn, gn_in, gx_own, att, glt,
     parcels, arrived, p_mine, p_away, p_in,
     sum_a, sum_b, in_a, in_b, sub_a, sub_b, late_a, late_b, total, send, recv,
@@ -536,6 +656,13 @@
     y, z = chip // 4, chip % 4
     copies = Copies(send, recv)
     mate = dev(chip, 1 - core, section)
+    early = [
+        copies.start(source, target, None)
+        for source, target in (
+            (spans_hbm, spans_ref), (kv_hbm.at[:, :, 1024:2048], kv_ref), (q_hbm, q_ref),
+            (qrow_hbm, qrow), (grow_hbm, grow), (gnat_hbm, gnat), (dq_hbm, dq_acc),
+        )
+    ]
     greet(plane_peers(section, chip, core) + section_peers(section, chip, core))
     back = []
     for half in range(2):
@@ -553,21 +680,24 @@
     for step in (2, 1, 3, 0):
         device = dev(chip, core, (section + step) % 4) if step else None
         gathered.append(copies.start(glt_hbm, glt.at[:, lanes], device))
-    load_kv = copies.start(kv_hbm.at[:, :, 1024:2048], kv_ref, None)
-    load_table = copies.start(table_hbm, table_ref, None)
+    load_table = [
+        copies.start(table_hbm, table_ref, None), copies.start(starts_hbm, starts_ref, None)
+    ]
     load_w = copies.start(w_hbm, w_ref, None)
     loads = [
         copies.start(source, target, None)
         for source, target in (
-            (normed_t_hbm, normed_t_ref), (tokens_hbm, tokens_ref), (gl_hbm, gl_ref)
+            (normed_t_hbm, normed_t_ref), (tokens_hbm, tokens_ref), (gl_hbm, gl_ref),
+            (gain_hbm, gain_ref), (live_hbm, live_ref),
         )
     ]
-    for head in range(2):
+    for near, of_core in ((True, core), (False, 1 - core)):
+        rows = pl.ds(pl.multiple_of(of_core * PAIR, 16), PAIR)
         for part in range(4):
-            target = att.at[head * PAIR : head * PAIR + PAIR, part * 128 : part * 128 + 128]
-            loads.append(copies.start(own_hbm.at[head, part], target, None))
-
-    load_kv.wait()
+            source = op_hbm.at[core, part] if near else own_hbm.at[part]
+            loads.append(copies.start(source, att.at[rows, part * 128 : part * 128 + 128], None))
+
+    wait_all(early)
     for chunk in range(4):
         lanes = pl.ds(chunk * CHUNK, CHUNK)
         build_keys(
@@ -575,7 +705,6 @@
         )
     dk_acc[...] = jnp.zeros_like(dk_acc)
     dv_acc[...] = jnp.zeros_like(dv_acc)
-    dq_acc[...] = dq_ref[...]
 
     def own_step(tile, group):
         rows = pl.ds(pl.multiple_of(tile * 256, 256), 256)
@@ -616,6 +745,7 @@
     lax.fori_loop(0, 2, odd_step, 0)
     finish_own(1)
 
+    wait_all(load_table)
     begin = starts_ref[:, 0:1]
     block, offset = begin // 128, begin % 128
     first = 8 * ((block + 1 - core) // 2)
@@ -625,7 +755,6 @@
     wanted = first + out_row % 8
     wanted = (wanted // 8) * 16 + wanted % 8 + 8 * ((out_row // 8) % 2)
     hot = jnp.where(in_row == wanted, 1.0, 0.0).astype(BF16)
-    load_table.wait()
     table = table_ref[...].reshape(256, 640)
     parcels[...] = dot_nn(hot, table).astype(BF16).reshape(32, 16, 640)
 
@@ -761,6 +890,7 @@
     for which in range(2):
         hot = jnp.where(taken & (side == which), 1.0, 0.0).astype(BF16)
         delivered_ref[:, which * 640 : which * 640 + 640] = dot_nn(hot, rows).astype(BF16)
+    deliver = copies.start(delivered_ref, delivered_hbm, None)
 
     wait_all(seconds)
     grad = sub_a[y].astype(F32) + late_a[0].astype(F32)
@@ -771,23 +901,36 @@
     for target, device in ((1 - core, mate), (core, None)):
         rows = pl.ds(pl.multiple_of(target * 40, 8), 40)
         lasts.append(copies.start(total.at[rows, :], weights_ref.at[core], device))
-    wait_all(lasts)
+    wait_all(lasts + [deliver])
     for waits in gathers:
         wait_all(waits)
 
 
-def results_body(gx_ref, both_ref, arrived_ref, gx_out, w_qkv_out, w_out_out, delivered_out):
+def results_body(
+    gx_hbm, both_hbm, arrived_hbm, gx_out, w_qkv_out, w_out_out, delivered_out,
+    gx_ref, both_ref, sems,
+):
+    loads = [
+        pltpu.make_async_copy(gx_hbm.at[0], gx_ref.at[0], sems.at[0]),
+        pltpu.make_async_copy(gx_hbm.at[1], gx_ref.at[1], sems.at[1]),
+        pltpu.make_async_copy(both_hbm, both_ref, sems.at[2]),
+        pltpu.make_async_copy(arrived_hbm, delivered_out, sems.at[3]),
+    ]
+    for load in loads:
+        load.start()
     row = lax.broadcasted_iota(jnp.int32, (256, 256), 0)
     column = lax.broadcasted_iota(jnp.int32, (256, 256), 1)
     natural = jnp.where(row == 4 * (column % 64) + column // 64, 1.0, 0.0).astype(BF16)
     for half in range(2):
+        loads[half].wait()
         rows = gx_ref[half].reshape(256, 1280)
         gx_out[half * 256 : half * 256 + 256, :] = dot_nn(natural, rows).astype(BF16)
+    loads[2].wait()
     w_qkv_out[0] = both_ref[0, :, :320]
     w_qkv_out[1] = both_ref[0, :, 320:]
     w_qkv_out[2] = both_ref[1, :, :320]
     w_out_out[...] = both_ref[1, :, 320:]
-    delivered_out[...] = arrived_ref[...]
+    loads[3].wait()
 
 
 def halo_peers(section, chip, core):
@@ -827,118 +970,154 @@
     tokens, norm_gain, w_qkv, w_out, merge_gain, seg_blocks, mb_sizes, mb_receiver, merged_grad
 ):
     w_rows = w_qkv.transpose(0, 2, 1)
-    q, kv, normed_t, w_full = call(
+    q, kv, normed_t, w_full, q_rows, sums, norms = call(
         project_body,
         [
-            (VMEM, shape((PAIR, 1024))),
-            (VMEM, shape((2, PAIR, 3072))),
+            (HBM, shape((PAIR, 1024))),
+            (HBM, shape((2, PAIR, 3072))),
             (HBM, shape((1280, 512))),
             (HBM, shape((1280, 1280))),
-        ],
-        [(HBM, tokens), (VMEM, norm_gain), (HBM, w_rows), (HBM, w_out)],
+            (HBM, shape((2, 1024, 128))),
+            (HBM, shape((2, 1024, 128), F32)),
+            (HBM, shape((4, 8, 128), F32)),
+        ],
+        [(SMEM, seg_blocks), (HBM, tokens), (HBM, norm_gain), (HBM, w_rows), (HBM, w_out)],
         [
             pltpu.VMEM((512, 1280), BF16),
+            pltpu.VMEM((1280,), BF16),
             pltpu.VMEM((3, 320, 1280), BF16),
-            pltpu.VMEM((512, 1280), BF16),
             pltpu.VMEM((1280, 512), BF16),
             pltpu.VMEM((3, 320, 512), BF16),
-        ],
-        copies=32,
+            pltpu.VMEM((PAIR, 1024), BF16),
+            pltpu.VMEM((2, PAIR, 1024), BF16),
+            pltpu.VMEM((2, 32, 128), jnp.int32),
+            pltpu.VMEM((2, 1024, 128), BF16),
+            pltpu.VMEM((2, 128, 1024), BF16),
+            pltpu.VMEM((2, 1024, 128), BF16),
+            pltpu.VMEM((2, 1024, 128), F32),
+            pltpu.VMEM((4, 8, 128), F32),
+        ],
+        copies=40,
         number=1,
-        limit=20,
+        limit=62,
     )
-    o, kv_kept, op, log_total = call(
+    o, op, log_total = call(
         forward_body,
         [
             (HBM, shape((PAIR, 1024))),
-            (HBM, shape((2, PAIR, 3072))),
-            (VMEM, shape((2, 4, PAIR, 128))),
-            (VMEM, shape((2, 1024), F32)),
-        ],
-        [(SMEM, seg_blocks), (VMEM, q), (VMEM, kv)],
+            (HBM, shape((2, 4, PAIR, 128))),
+            (HBM, shape((2, 1024), F32)),
+        ],
+        [(SMEM, seg_blocks), (HBM, kv), (HBM, q_rows), (HBM, sums), (HBM, norms)],
         [
             pltpu.VMEM((2, 32, 128), jnp.int32),
             pltpu.SMEM((4, 2), jnp.int32),
             pltpu.VMEM((PAIR, 1024), BF16),
+            pltpu.VMEM((2, PAIR, 3072), BF16),
             pltpu.VMEM((2, 1024, 128), BF16),
             pltpu.VMEM((2, 128, 3072), BF16),
             pltpu.VMEM((2, 3072, 128), BF16),
-        ],
-        copies=2,
-        limit=16,
+            pltpu.VMEM((2, 1024, 128), F32),
+            pltpu.VMEM((4, 8, 128), F32),
+            pltpu.VMEM((2, 4, PAIR, 128), BF16),
+            pltpu.VMEM((2, 1024), F32),
+        ],
+        copies=9,
+        limit=62,
     )
     gp, grad_layer, glt, att_own, table = call(
         middle_body,
         [
-            (VMEM, shape((2, 4, PAIR, 128))),
+            (HBM, shape((2, 4, PAIR, 128))),
             (HBM, shape((128, 1280))),
             (HBM, shape((1280, 128))),
-            (HBM, shape((2, 4, PAIR, 128))),
+            (HBM, shape((4, PAIR, 128))),
             (HBM, shape((16, 16, 640))),
         ],
-        [(VMEM, op), (HBM, w_full), (HBM, tokens), (HBM, merged_grad), (VMEM, merge_gain)],
+        [(HBM, op), (HBM, w_full), (HBM, w_out), (HBM, tokens), (HBM, merged_grad), (HBM, merge_gain)],
         [
             pltpu.VMEM((1280, 1280), BF16),
             pltpu.VMEM((512, 1280), BF16),
             pltpu.VMEM((128, 1280), BF16),
+            pltpu.VMEM((1280,), BF16),
             pltpu.VMEM((128, 1280), BF16),
             pltpu.VMEM((1280, 128), BF16),
             pltpu.VMEM((1280, 128), BF16),
             pltpu.VMEM((1280, 128), BF16),
             pltpu.VMEM((16, 16, 640), BF16),
         ],
-        copies=40,
+        copies=44,
         number=2,
-        limit=20,
+        limit=62,
     )
     dq, dkv, start_rows, here, qrow, grow, gnat, spans = call(
         backward_body,
         [
-            (VMEM, shape((2, 1024, 128), F32)),
-            (VMEM, shape((2, PAIR, 2048))),
-            (VMEM, shape((512, 128), jnp.int32)),
-            (VMEM, shape((16, 512), jnp.int32)),
-            (VMEM, shape((2, 1024, 128))),
-            (VMEM, shape((2, 1024, 128))),
-            (VMEM, shape((PAIR, 1024))),
-            (VMEM, shape((2, 32, 128), jnp.int32)),
+            (HBM, shape((2, 1024, 128), F32)),
+            (HBM, shape((2, PAIR, 2048))),
+            (HBM, shape((512, 128), jnp.int32)),
+            (HBM, shape((16, 512), jnp.int32)),
+            (HBM, shape((2, 1024, 128))),
+            (HBM, shape((2, 1024, 128))),
+            (HBM, shape((PAIR, 1024))),
+            (HBM, shape((2, 32, 128), jnp.int32)),
         ],
         [
             (SMEM, seg_blocks), (SMEM, mb_sizes), (SMEM, mb_receiver),
-            (VMEM, q), (HBM, kv_kept), (HBM, o), (VMEM, log_total), (VMEM, gp),
-        ],
-        [
+            (HBM, q), (HBM, kv), (HBM, o), (HBM, log_total), (HBM, gp),
+        ],
+        [
+            pltpu.VMEM((2, 1024, 128), F32),
+            pltpu.VMEM((2, PAIR, 2048), BF16),
+            pltpu.VMEM((512, 128), jnp.int32),
+            pltpu.VMEM((16, 512), jnp.int32),
+            pltpu.VMEM((2, 1024, 128), BF16),
+            pltpu.VMEM((2, 1024, 128), BF16),
+            pltpu.VMEM((PAIR, 1024), BF16),
+            pltpu.VMEM((2, 32, 128), jnp.int32),
             pltpu.SMEM((4, 2), jnp.int32),
+            pltpu.VMEM((PAIR, 1024), BF16),
             pltpu.VMEM((2, PAIR, 3072), BF16),
             pltpu.VMEM((PAIR, 1024), BF16),
+            pltpu.VMEM((2, 1024), F32),
+            pltpu.VMEM((2, 4, PAIR, 128), BF16),
             pltpu.VMEM((2, 128, 2048), BF16),
             pltpu.VMEM((2, 128, 2048), BF16),
             pltpu.VMEM((2, 2048, 128), BF16),
             pltpu.VMEM((2, HEAD_DIM, 2048), F32),
             pltpu.VMEM((2, HEAD_DIM, 2048), F32),
         ],
-        copies=2,
-        limit=22,
+        copies=13,
+        limit=62,
     )
     arrived, gx_all, weights = call(
         tail_body,
         [
-            (VMEM, shape((256, 1280))),
-            (VMEM, shape((2, 4, 64, 1280))),
-            (VMEM, shape((2, 40, 640), F32)),
-        ],
-        [
-            (VMEM, dkv), (VMEM, start_rows), (VMEM, here), (VMEM, dq), (VMEM, qrow), (VMEM, grow),
-            (VMEM, gnat), (VMEM, spans), (VMEM, q), (HBM, kv_kept), (HBM, glt), (HBM, att_own),
-            (HBM, table), (HBM, grad_layer), (HBM, tokens), (VMEM, norm_gain), (HBM, w_rows),
+            (HBM, shape((256, 1280))),
+            (HBM, shape((2, 4, 64, 1280))),
+            (HBM, shape((2, 40, 640), F32)),
+        ],
+        [
+            (HBM, dkv), (HBM, start_rows), (HBM, here), (HBM, dq), (HBM, qrow), (HBM, grow),
+            (HBM, gnat), (HBM, spans), (HBM, q), (HBM, kv), (HBM, glt), (HBM, op), (HBM, att_own),
+            (HBM, table), (HBM, grad_layer), (HBM, tokens), (HBM, norm_gain), (HBM, w_rows),
             (HBM, normed_t),
         ],
         [
+            pltpu.VMEM((512, 128), jnp.int32),
+            pltpu.VMEM((16, 512), jnp.int32),
+            pltpu.VMEM((2, 1024, 128), BF16),
+            pltpu.VMEM((2, 1024, 128), BF16),
+            pltpu.VMEM((PAIR, 1024), BF16),
+            pltpu.VMEM((2, 32, 128), jnp.int32),
+            pltpu.VMEM((1280,), BF16),
+            pltpu.VMEM((256, 1280), BF16),
             pltpu.VMEM((16, 16, 640), BF16),
             pltpu.VMEM((128, 1280), BF16),
             pltpu.VMEM((512, 1280), BF16),
             pltpu.VMEM((3, 320, 1280), BF16),
             pltpu.VMEM((1280, 512), BF16),
+            pltpu.VMEM((PAIR, 1024), BF16),
             pltpu.VMEM((2, PAIR, 1024), BF16),
             pltpu.VMEM((2, 128, 1024), BF16),
             pltpu.VMEM((2, 128, 1024), BF16),
@@ -971,9 +1150,9 @@
             pltpu.VMEM((3, 80, 256), BF16),
             pltpu.VMEM((80, 640), F32),
         ],
-        copies=112,
+        copies=124,
         number=3,
-        limit=48,
+        limit=62,
     )
     grad_x, grad_w_qkv, grad_w_out, delivered = call(
         results_body,
@@ -983,8 +1162,10 @@
             (VMEM, shape((40, 320), F32)),
             (VMEM, shape((256, 1280))),
         ],
-        [(VMEM, gx_all), (VMEM, weights), (VMEM, arrived)],
-        limit=14,
+        [(HBM, gx_all), (HBM, weights), (HBM, arrived)],
+        [pltpu.VMEM((2, 4, 64, 1280), BF16), pltpu.VMEM((2, 40, 640), F32)],
+        copies=4,
+        limit=62,
     )
     return (delivered, grad_x, grad_w_qkv, grad_w_out.T)
 

time: 137 us -> 135 us (0.985)
  local copies, waits for them, and re-layouts: 7.24 us -> 0 us
  Pallas kernels: 129 us -> 133 us
    unnamed x30 -> x0, local copies, waits for them, and re-layouts: 7.24 us -> none
    pallas_call x6, Pallas kernels: 129 us -> 133 us  [call(): pl.pallas_call(body, out_shape=[array for _, array in outs], in_specs=[pl...]
where the time goes in v5:
time: 135 us; the launch traced here: 134 us
  Pallas kernels  133 us (99%)
    pallas_call x6, Pallas kernels, call(): pl.pallas_call(body, out_shape=[array for _, array in outs], in_specs=[pl...  133 us

profile of v5, /device:TPU:1, one launch (start us, length us, event | category | flops | bytes accessed | tf_op | source)
XLA Modules:
  0.0 134.3 jit_solution(11499366468359924930)
XLA Ops:
  0.6 29.9 %shard_map.120 = (bf16[160,1024]{1,0:T(8,128)(2,1)}, bf16[2,160,3072]{2,1,0:T(8,128)(2,1)}, bf16[1280,512]{1,0:T(8,128)(2,1)}, bf16[1280,1280]{1,0:T(8,128)(2,1)...) custom-call(s32[32]{0:T(128)} %seg_ref.5, bf16[512,1280]{1,0:T(8,128)(2,1)} %tokens_hbm.5, ...), custom_call_target="tpu_custom_call" | custom-call | tf_op jit(solution)/shard_map/pallas_call | solution.py:85
  30.6 15.9 %shard_map.121 = (bf16[160,1024]{1,0:T(8,128)(2,1)}, bf16[2,4,160,128]{3,2,1,0:T(8,128)(2,1)}, f32[2,1024]{1,0:T(2,128)}) custom-call(s32[32]{0:T(128)} %seg_ref.5, bf16[2,160,3072]{2,1,0:T(8,128)(2,1)} %get-tuple-element.35.kv_hbm, bf16[2,1024,128]{2,1,0:T(8,128)(2,1)} %get-tuple-element.36.qrow_hbm, f32[2,1024,128]{2,1,0:T(8,128)} %get-tuple-element.37.sums_hbm, ...), custom_call_target="tpu_custom_call" | custom-call | tf_op jit(solution)/shard_map/pallas_call | solution.py:85
  46.5 21.6 %shard_map.122 = (bf16[2,4,160,128]{3,2,1,0:T(8,128)(2,1)}, bf16[128,1280]{1,0:T(8,128)(2,1)}, bf16[1280,128]{1,0:T(8,128)(2,1)}, bf16[4,160,128]{2,1,0:T(8,128)(2,1)}, bf16[16,16,640]{2,1,0:T(8,128)(2,1)}) custom-call(bf16[2,4,160,128]{3,2,1,0:T(8,128)(2,1)} %get-tuple-element.41.op_ref.op_hbm, bf16[1280,1280]{1,0:T(8,128)(2,1)} %get-tuple-element.42.w_hbm, ...), custom_call_target="tpu_custom_call" | custom-call | tf_op jit(solution)/shard_map/pallas_call | solution.py:85
  68.0 7.6 %shard_map.123 = (f32[2,1024,128]{2,1,0:T(8,128)}, bf16[2,160,2048]{2,1,0:T(8,128)(2,1)}, s32[512,128]{1,0:T(8,128)}, s32[16,512]{1,0:T(8,128)}, bf16[2,1024,128...) custom-call(s32[32]{0:T(128)} %seg_ref.5, s32[32]{0:T(128)} %sizes_ref.1, ...), custom_call_target="tpu_custom_call" | custom-call | tf_op jit(solution)/shard_map/pallas_call | solution.py:85
  75.6 55.2 %shard_map.124 = (bf16[256,1280]{1,0:T(8,128)(2,1)}, bf16[2,4,64,1280]{3,2,1,0:T(8,128)(2,1)}, f32[2,40,640]{2,1,0:T(8,128)}) custom-call(bf16[2,160,2048]{2,1,0:T(8,128)(2,1)} %get-tuple-element.44.dkv_ref, s32[512,128]{1,0:T(8,128)} %get-tuple-element.45.starts_hbm, s32[16,512]{1,0:T(8,128)} %get-tuple-element.46.live_hbm, ...), custom_call_target="tpu_custom_call" | custom-call | tf_op jit(solution)/shard_map/pallas_call | solution.py:85
  130.8 3.3 %shard_map.125 = (bf16[512,1280]{1,0:T(8,128)(2,1)}, f32[3,40,320]{2,1,0:T(8,128)}, f32[40,320]{1,0:T(8,128)}, bf16[256,1280]{1,0:T(8,128)(2,1)}) custom-call(bf16[2,4,64,1280]{3,2,1,0:T(8,128)(2,1)} %get-tuple-element.57.gx_hbm, f32[2,40,640]{2,1,0:T(8,128)} %get-tuple-element.58.both_hbm, bf16[256,1280]{1,0:T(8,128)(2,1)} %get-tuple-element.59.arrived_hbm), custom_call_target="tpu_custom_call" | custom-call | tf_op jit(solution)/shard_map/pallas_call | solution.py:85

commit v6 on v5

--- a/solution.py
+++ b/solution.py
@@ -71,7 +71,10 @@
     barrier = pltpu.get_barrier_semaphore()
     for peer in peers:
         pl.semaphore_signal(barrier, inc=1, device_id=peer, device_id_type=MESH)
-    pl.semaphore_wait(barrier, len(peers))
+
+
+def greeted(peers):
+    pl.semaphore_wait(pltpu.get_barrier_semaphore(), len(peers))
 
 
 VMEM = pl.BlockSpec(memory_space=pltpu.VMEM)
@@ -108,10 +111,15 @@
 ):
     section, chip, core = place()
     copies = Copies(send, recv)
-    load_tokens = copies.start(tokens_hbm, tokens_ref, None)
-    load_w = copies.start(w_hbm, w_ref, None)
+    peers = halo_peers(section, chip, core) + section_peers(section, chip, core)[::2]
+    greet(peers)
     load_gain = copies.start(gain_hbm, gain_ref, None)
-    greet(halo_peers(section, chip, core) + section_peers(section, chip, core)[::2])
+    load_tokens = []
+    for tile in range(4):
+        rows = pl.ds(tile * 128, 128)
+        load_tokens.append(copies.start(tokens_hbm.at[rows, :], tokens_ref.at[rows, :], None))
+    load_w = {which: copies.start(w_hbm.at[which], w_ref.at[which], None) for which in (1, 2, 0)}
+    greeted(peers)
     mate = dev(chip, 1 - core, section)
     ahead, behind = (section + 1) % 4, (section + 3) % 4
     ahead_dev, behind_dev = dev(chip, core, ahead), dev(chip, core, behind)
@@ -123,20 +131,19 @@
     to_ahead = copies.start(mine, w_rows(section, 0, PAIR), ahead_dev)
     to_behind = copies.start(mine, w_rows(section, 0, PAIR), behind_dev)
     waits, inner = [], []
-    image_spans(seg_ref, spans_ref)
-    load_tokens.wait()
     load_gain.wait()
     gain = gain_ref[...].reshape(1, 1280).astype(F32)
     for tile in range(4):
         rows = pl.ds(tile * 128, 128)
+        load_tokens[tile].wait()
         values = tokens_ref[rows, :].astype(F32)
         centered = values - jnp.mean(values, axis=1, keepdims=True)
         inv = lax.rsqrt(jnp.mean(centered * centered, axis=1, keepdims=True) + EPS)
         normed_t_ref[:, rows] = (centered * inv * gain).astype(BF16).T
     own = pl.ds(pl.multiple_of(core * PAIR, 16), PAIR)
     other = pl.ds(pl.multiple_of((1 - core) * PAIR, 16), PAIR)
-    load_w.wait()
     for which in (1, 2, 0):
+        load_w[which].wait()
         out = dot_nn(w_ref[which], normed_t_ref[...])
         if which == 0:
             out = out * (FACTOR * LOG2E)
@@ -155,6 +162,7 @@
         inner.append(copies.start(out_ref.at[which, other, :], target, mate))
         inner.append(copies.start(out_ref.at[which, own, :], target, None))
     waits.append(copies.start(normed_t_ref, normed_t_hbm, None))
+    image_spans(seg_ref, spans_ref)
     wait_all(inner)
     waits.append(copies.start(q_ref, q_hbm, None))
     waits.append(copies.start(kv_ref, kv_hbm.at[:, :, 1024:2048], None))
@@ -461,16 +469,20 @@
 ):
     seq = lax.axis_index("seq")
     first = (seq // 2) * 1024
-    load_kv = pltpu.make_async_copy(kv_hbm, kv_ref, sems.at[0])
+    load_kv = pltpu.make_async_copy(kv_hbm.at[:, :, 0:1024], kv_ref.at[:, :, 0:1024], sems.at[0])
+    load_kv_after = pltpu.make_async_copy(
+        kv_hbm.at[:, :, 2048:3072], kv_ref.at[:, :, 2048:3072], sems.at[13]
+    )
     load_o = pltpu.make_async_copy(o_hbm, o_ref, sems.at[1])
     load_q = pltpu.make_async_copy(q_hbm, q_ref, sems.at[2])
-    load_kv.start()
     load_o.start()
     load_q.start()
     load_log = pltpu.make_async_copy(log_hbm, log_ref, sems.at[3])
     load_log.start()
     load_gp = pltpu.make_async_copy(gp_hbm, gp_ref, sems.at[4])
     load_gp.start()
+    load_kv.start()
+    load_kv_after.start()
     spans_and_bounds(seg_ref, first, spans_ref, bounds_ref)
     start = jnp.int32(0)
     my_start, my_size = jnp.int32(0), jnp.int32(0)
@@ -488,6 +500,7 @@
         joined = jnp.concatenate([gp_ref[half, part] for part in range(4)], axis=1)
         gnat[:, half * 512 : half * 512 + 512] = dot_nn(joined, back).astype(BF16)
     load_kv.wait()
+    load_kv_after.wait()
     load_o.wait()
     load_q.wait()
     load_log.wait()
@@ -578,6 +591,8 @@
 ):
     section, chip, core = place()
     copies = Copies(send, recv)
+    peers = row_peers(section, chip, core) + core_peers(section, chip, core)
+    greet(peers)
     columns = pl.ds(pl.multiple_of(section * 1280, 128), 1280)
     load_gain = copies.start(gain_hbm, gain_ref, None)
     load_mgrad = copies.start(mgrad_hbm.at[:, columns], mgrad_ref, None)
@@ -587,7 +602,7 @@
         w_rows = pl.ds(pl.multiple_of((section + step) % 4 * 320, 16), 320)
         source = w_hbm.at[w_rows, :] if step else w_out_hbm
         loads.append(copies.start(source, w_ref.at[w_rows, :], None))
-    greet(row_peers(section, chip, core) + core_peers(section, chip, core))
+    greeted(peers)
     rows = pl.ds(pl.multiple_of((section * 2 + core) * PAIR, 16), PAIR)
     waits = []
     for step in (2, 1, 3, 0):
@@ -648,14 +663,18 @@
     starts_ref, live_ref, qrow, grow, gnat, spans_ref, gain_ref, delivered_ref,
     table_ref, gl_ref, tokens_ref, w_ref, normed_t_ref,
     q_ref, kv_ref, kx, vx, krow, dk_acc, dv_acc, dq_acc, own_out, mate_in,
-    dkv_in, dj, rows_ref, gn, gn_in, gx_own, att, glt,
+    dkv_in, dj, rows_ref, gn, relay_in, gn_in, gx_own, att, glt,
     parcels, arrived, p_mine, p_away, p_in,
-    sum_a, sum_b, in_a, in_b, sub_a, sub_b, late_a, late_b, total, send, recv,
+    summed, stage_in, subtotal, late_in, total, send, recv,
 ):
     section, chip, core = place()
     y, z = chip // 4, chip % 4
+    ahead, behind, far = (section + 1) % 4, (section + 3) % 4, (section + 2) % 4
+    ahead_dev, behind_dev = dev(chip, core, ahead), dev(chip, core, behind)
     copies = Copies(send, recv)
     mate = dev(chip, 1 - core, section)
+    peers = plane_peers(section, chip, core) + section_peers(section, chip, core)
+    greet(peers)
     early = [
         copies.start(source, target, None)
         for source, target in (
@@ -663,8 +682,8 @@
             (qrow_hbm, qrow), (grow_hbm, grow), (gnat_hbm, gnat), (dq_hbm, dq_acc),
         )
     ]
-    greet(plane_peers(section, chip, core) + section_peers(section, chip, core))
-    back = []
+    greeted(peers)
+    back, mates = [], []
     for half in range(2):
         waits = []
         for step, base, slot in ((-1, 0, 0), (1, 1024, 1)):
@@ -675,11 +694,15 @@
                     copies.start(dkv_ref.at[:, :, lanes], dkv_in.at[half, slot, core], device)
                 )
         back.append(waits)
-    gathered = []
-    lanes = pl.ds(pl.multiple_of(section * 128, 128), 128)
-    for step in (2, 1, 3, 0):
-        device = dev(chip, core, (section + step) % 4) if step else None
-        gathered.append(copies.start(glt_hbm, glt.at[:, lanes], device))
+
+    def glt_part(owner, start, count):
+        lanes = pl.ds(pl.multiple_of(owner * 128, 128), 128)
+        return glt.at[start : start + count, lanes]
+
+    mine = glt_part(section, 0, 1280)
+    glt_ahead = copies.start(glt_hbm, mine, ahead_dev)
+    glt_behind = copies.start(glt_hbm, mine, behind_dev)
+    gathered = [copies.start(glt_hbm, mine, None)]
     load_table = [
         copies.start(table_hbm, table_ref, None), copies.start(starts_hbm, starts_ref, None)
     ]
@@ -725,7 +748,7 @@
                 own_out[half, of_core, 0, feats, :] = part.astype(BF16)
                 own_out[half, of_core, 1, feats, :] = (dk_acc[head, :, lanes] * LN2).astype(BF16)
                 own_out[half, of_core, 2, feats, :] = dv_acc[head, :, lanes].astype(BF16)
-        back[half].append(copies.start(own_out.at[half, 1 - core], mate_in.at[half], mate))
+        mates.append(copies.start(own_out.at[half, 1 - core], mate_in.at[half], mate))
 
     def first_step(tile, carry):
         own_step(tile, 0)
@@ -742,8 +765,167 @@
     lax.fori_loop(0, 4, first_step, 0)
     lax.fori_loop(0, 2, even_step, 0)
     finish_own(0)
+    glt_ahead.wait()
+    there = glt_part(behind, 0, 640)
+    gathered.append(copies.start(there, there, ahead_dev))
+    glt_behind.wait()
+    there = glt_part(ahead, 640, 640)
+    gathered.append(copies.start(there, there, behind_dev))
     lax.fori_loop(0, 2, odd_step, 0)
     finish_own(1)
+
+    row = lax.broadcasted_iota(jnp.int32, (256, 256), 0)
+    column = lax.broadcasted_iota(jnp.int32, (256, 256), 1)
+    by_part = jnp.where(column == 4 * (row % 64) + row // 64, 1.0, 0.0).astype(BF16)
+    load_w.wait()
+
+    def collect(half, kinds):
+        lanes = pl.ds(half * 256, 256)
+        for near, head in ((True, core), (False, 1 - core)):
+            for which in kinds:
+                grad = own_out[half, core, which] if near else mate_in[half, which]
+                if which:
+                    grad = grad.astype(F32) + dkv_in[half, 0, head, which - 1].astype(F32)
+                    grad = (grad + dkv_in[half, 1, head, which - 1].astype(F32)).astype(BF16)
+                dj[pl.ds(pl.multiple_of(320 * which + head * PAIR, 16), PAIR), lanes] = grad
+
+    sums = []
+
+    def send_first(half):
+        rows_ref[...] = dot_nt(by_part, dj[:, half * 256 : half * 256 + 256]).astype(BF16)
+        grad = dot_nn(rows_ref[...], w_ref[...].reshape(960, 1280))
+        gn[half] = grad.astype(BF16).reshape(4, 64, 1280)
+        relays = [
+            copies.start(gn.at[half, far, 0:32], relay_in.at[half, 0], behind_dev),
+            copies.start(gn.at[half, far, 32:64], relay_in.at[half, 1], ahead_dev),
+        ]
+        sums.append([
+            copies.start(gn.at[half, behind, 32:64], gn_in.at[half, 0, 32:64], behind_dev),
+            copies.start(gn.at[half, ahead, 0:32], gn_in.at[half, 1, 0:32], ahead_dev),
+        ])
+        return relays
+
+    def send_second(half, relays):
+        relays[0].wait()
+        grad = gn[half, behind, 0:32].astype(F32) + relay_in[half, 0].astype(F32)
+        gn[half, behind, 0:32] = grad.astype(BF16)
+        source = gn.at[half, behind, 0:32]
+        sums[half].append(copies.start(source, gn_in.at[half, 0, 0:32], behind_dev))
+        relays[1].wait()
+        grad = gn[half, ahead, 32:64].astype(F32) + relay_in[half, 1].astype(F32)
+        gn[half, ahead, 32:64] = grad.astype(BF16)
+        source = gn.at[half, ahead, 32:64]
+        sums[half].append(copies.start(source, gn_in.at[half, 1, 32:64], ahead_dev))
+
+    def products(index, core_of, group):
+        rows = pl.ds(index * 320, 320)
+        if group == 0 and core_of == 1:
+            return dot_nt(glt[rows, :], att[...])
+        which = 0 if group == 0 else 1 + core_of
+        return dot_nt(normed_t_ref[rows, :], dj[320 * which : 320 * which + 320, :])
+
+    def send_products(group):
+        pairs = []
+        for index in range(4):
+            for core_of in range(2):
+                @pl.when(core != core_of)
+                def _():
+                    part = products(index, core_of, group)
+                    p_away[group, index] = part.astype(BF16).reshape(4, 80, 320)
+
+            pairs.append(copies.start(p_away.at[group, index], p_in.at[group, index], mate))
+        for index in range(4):
+            for core_of in range(2):
+                @pl.when(core == core_of)
+                def _():
+                    p_mine[index] = products(index, core_of, group).reshape(4, 80, 320)
+
+        return pairs
+
+    def first_stage(group, pairs):
+        for index in range(4):
+            pairs[index].wait()
+            grad = p_mine[index] + p_in[group, index].astype(F32)
+            summed[group, index] = grad.astype(BF16)
+        waits = []
+        for step in (2, 1, 3):
+            to_z, to_y = (z + step) % 4, (y + step) % 4
+            if group == 0:
+                source, device = summed.at[group, to_y], dev(to_y * 4 + z, core, section)
+            else:
+                source, device = summed.at[group, :, to_z], dev(y * 4 + to_z, core, section)
+            waits.append(copies.start(source, stage_in.at[group, step - 1], device))
+        return waits
+
+    def second_stage(group, waits):
+        wait_all(waits)
+        for index in range(4):
+            grad = (summed[group, y, index] if group == 0 else summed[group, index, z]).astype(F32)
+            for step in range(3):
+                grad = grad + stage_in[group, step, index].astype(F32)
+            subtotal[group, index] = grad.astype(BF16)
+        waits = []
+        for step in (2, 1, 3):
+            to_z, to_y = (z + step) % 4, (y + step) % 4
+            place_to = to_z if group == 0 else to_y
+            device = dev(y * 4 + to_z if group == 0 else to_y * 4 + z, core, section)
+            waits.append(
+                copies.start(subtotal.at[group, place_to], late_in.at[group, step - 1], device)
+            )
+        return waits
+
+    def last_stage(group, waits):
+        wait_all(waits)
+        grad = subtotal[group, z if group == 0 else y].astype(F32)
+        for step in range(3):
+            grad = grad + late_in[group, step].astype(F32)
+        total[group] = grad
+        found = []
+        for target, device in ((1 - core, mate), (core, None)):
+            rows = pl.ds(pl.multiple_of(target * 40, 8), 40)
+            found.append(
+                copies.start(total.at[group, rows, :], weights_ref.at[core, group], device)
+            )
+        return found
+
+    gathers, forwards = [], []
+
+    def finish_norm(half):
+        row = lax.broadcasted_iota(jnp.int32, (64, 256), 0)
+        column = lax.broadcasted_iota(jnp.int32, (64, 256), 1)
+        chosen = jnp.where(column == 4 * row + section, 1.0, 0.0).astype(BF16)
+        values = dot_nn(chosen, tokens_ref[half * 256 : half * 256 + 256, :])
+        centered = values - jnp.mean(values, axis=1, keepdims=True)
+        inv = lax.rsqrt(jnp.mean(centered * centered, axis=1, keepdims=True) + EPS)
+        unit = centered * inv
+        wait_all(sums[half])
+        grad = gn[half, section].astype(F32) + gn_in[half, 0].astype(F32)
+        grad = grad + gn_in[half, 1].astype(F32)
+        scaled = grad * gain_ref[...].reshape(1, 1280).astype(F32)
+        grad = inv * (
+            scaled
+            - jnp.mean(scaled, axis=1, keepdims=True)
+            - unit * jnp.mean(scaled * unit, axis=1, keepdims=True)
+        )
+        grad = grad + gl_ref[half * 64 : half * 64 + 64, :].astype(F32)
+        gx_own[half] = grad.astype(BF16)
+        target = gx_all.at[half, section]
+        gathers.append([copies.start(gx_own.at[half], target, ahead_dev)])
+        gathers[half].append(copies.start(gx_own.at[half], target, behind_dev))
+        forwards.append(copies.start(gx_own.at[half], target, None))
+
+    def forward(half):
+        gathers[half][0].wait()
+        there = gx_all.at[half, behind, 0:32]
+        forwards.append(copies.start(there, there, ahead_dev))
+        gathers[half][1].wait()
+        there = gx_all.at[half, ahead, 32:64]
+        forwards.append(copies.start(there, there, behind_dev))
+
+    wait_all(back[0])
+    mates[0].wait()
+    collect(0, (0, 1, 2))
+    relays_a = send_first(0)
 
     wait_all(load_table)
     begin = starts_ref[:, 0:1]
@@ -758,31 +940,14 @@
     table = table_ref[...].reshape(256, 640)
     parcels[...] = dot_nn(hot, table).astype(BF16).reshape(32, 16, 640)
 
-    row = lax.broadcasted_iota(jnp.int32, (256, 256), 0)
-    column = lax.broadcasted_iota(jnp.int32, (256, 256), 1)
-    by_part = jnp.where(column == 4 * (row % 64) + row // 64, 1.0, 0.0).astype(BF16)
-    load_w.wait()
-    w_all = w_ref[...].reshape(960, 1280)
-    sums = []
-    for half in range(2):
-        wait_all(back[half])
-        lanes = pl.ds(half * 256, 256)
-        for near, head in ((True, core), (False, 1 - core)):
-            for which in range(3):
-                grad = own_out[half, core, which] if near else mate_in[half, which]
-                if which:
-                    grad = grad.astype(F32) + dkv_in[half, 0, head, which - 1].astype(F32)
-                    grad = (grad + dkv_in[half, 1, head, which - 1].astype(F32)).astype(BF16)
-                dj[pl.ds(pl.multiple_of(320 * which + head * PAIR, 16), PAIR), lanes] = grad
-        rows_ref[...] = dot_nt(by_part, dj[:, lanes]).astype(BF16)
-        gn[half] = dot_nn(rows_ref[...], w_all).astype(BF16).reshape(4, 64, 1280)
-        waits = []
-        for step in (2, 1, 3):
-            to_section = (section + step) % 4
-            device = dev(chip, core, to_section)
-            waits.append(copies.start(gn.at[half, to_section], gn_in.at[half, step - 1], device))
-        sums.append(waits)
-
+    wait_all(loads)
+    wait_all(gathered)
+    mates[1].wait()
+    collect(1, (0,))
+    pairs = send_products(0)
+    wait_all(back[1])
+    collect(1, (1, 2))
+    relays_b = send_first(1)
     deliveries = []
     for step in range(16):
         for turn in range(2):
@@ -791,90 +956,16 @@
             deliveries.append(
                 copies.start(parcels.at[to_chip * 2 + to_core], arrived.at[chip * 2 + core], device)
             )
-
-    def products(index, core_of):
-        rows = pl.ds(index * 320, 320)
-        normed = normed_t_ref[rows, :]
-        if core_of == 0:
-            return dot_nt(normed, dj[0:640, :])
-        return jnp.concatenate(
-            [dot_nt(normed, dj[640:960, :]), dot_nt(glt[rows, :], att[...])], axis=1
-        )
-
-    wait_all(gathered)
-    wait_all(loads)
-    pairs = []
-    for index in range(4):
-        for core_of in range(2):
-            @pl.when(core != core_of)
-            def _():
-                p_away[index] = products(index, core_of).astype(BF16).reshape(4, 80, 640)
-
-        pairs.append(copies.start(p_away.at[index], p_in.at[index], mate))
-    for index in range(4):
-        for core_of in range(2):
-            @pl.when(core == core_of)
-            def _():
-                p_mine[index] = products(index, core_of).reshape(4, 80, 640)
-
-    gathers = []
-
-    def finish_norm(half):
-        row = lax.broadcasted_iota(jnp.int32, (64, 256), 0)
-        column = lax.broadcasted_iota(jnp.int32, (64, 256), 1)
-        chosen = jnp.where(column == 4 * row + section, 1.0, 0.0).astype(BF16)
-        values = dot_nn(chosen, tokens_ref[half * 256 : half * 256 + 256, :])
-        centered = values - jnp.mean(values, axis=1, keepdims=True)
-        inv = lax.rsqrt(jnp.mean(centered * centered, axis=1, keepdims=True) + EPS)
-        unit = centered * inv
-        wait_all(sums[half])
-        grad = gn[half, section].astype(F32) + gn_in[half, 0].astype(F32)
-        grad = grad + (gn_in[half, 1].astype(F32) + gn_in[half, 2].astype(F32))
-        scaled = grad * gain_ref[...].reshape(1, 1280).astype(F32)
-        grad = inv * (
-            scaled
-            - jnp.mean(scaled, axis=1, keepdims=True)
-            - unit * jnp.mean(scaled * unit, axis=1, keepdims=True)
-        )
-        grad = grad + gl_ref[half * 64 : half * 64 + 64, :].astype(F32)
-        gx_own[half] = grad.astype(BF16)
-        waits = []
-        for step in (2, 1, 3, 0):
-            device = dev(chip, core, (section + step) % 4) if step else None
-            waits.append(copies.start(gx_own.at[half], gx_all.at[half, section], device))
-        gathers.append(waits)
-
+    send_second(0, relays_a)
+    stage_y = first_stage(0, pairs)
+    pairs = send_products(1)
+    stage_z = first_stage(1, pairs)
+    send_second(1, relays_b)
     finish_norm(0)
-    firsts = [[], []]
-    for index in range(4):
-        pairs[index].wait()
-        summed = (p_mine[index] + p_in[index].astype(F32)).astype(BF16)
-        sum_a[index] = summed[:, :, :384]
-        sum_b[index] = summed[:, :, 384:]
-    for step in (2, 1, 3):
-        to_z, to_y = (z + step) % 4, (y + step) % 4
-        device = dev(y * 4 + to_z, core, section)
-        firsts[0].append(copies.start(sum_a.at[:, to_z], in_a.at[step - 1], device))
-        device = dev(to_y * 4 + z, core, section)
-        firsts[1].append(copies.start(sum_b.at[to_y], in_b.at[step - 1], device))
     finish_norm(1)
-    seconds = []
-    wait_all(firsts[1])
-    grad = sum_b[y].astype(F32) + in_b[0].astype(F32)
-    sub_b[...] = (grad + (in_b[1].astype(F32) + in_b[2].astype(F32))).astype(BF16)
-    for step in (2, 1, 3):
-        to_z = (z + step) % 4
-        device = dev(y * 4 + to_z, core, section)
-        seconds.append(copies.start(sub_b.at[to_z], late_b.at[step - 1], device))
-    wait_all(firsts[0])
-    for index in range(4):
-        grad = sum_a[index, z].astype(F32) + in_a[0, index].astype(F32)
-        grad = grad + (in_a[1, index].astype(F32) + in_a[2, index].astype(F32))
-        sub_a[index] = grad.astype(BF16)
-    for step in (2, 1, 3):
-        to_y = (y + step) % 4
-        device = dev(to_y * 4 + z, core, section)
-        seconds.append(copies.start(sub_a.at[to_y], late_a.at[step - 1], device))
+    forward(0)
+    later_z = second_stage(0, stage_y)
+    forward(1)
 
     lane = lax.broadcasted_iota(jnp.int32, (1, 512), 1)
     from_chip, from_core, side, number = lane // 32, (lane // 16) % 2, (lane // 8) % 2, lane % 8
@@ -890,47 +981,52 @@
     for which in range(2):
         hot = jnp.where(taken & (side == which), 1.0, 0.0).astype(BF16)
         delivered_ref[:, which * 640 : which * 640 + 640] = dot_nn(hot, rows).astype(BF16)
-    deliver = copies.start(delivered_ref, delivered_hbm, None)
-
-    wait_all(seconds)
-    grad = sub_a[y].astype(F32) + late_a[0].astype(F32)
-    total[:, :384] = grad + (late_a[1].astype(F32) + late_a[2].astype(F32))
-    grad = sub_b[z].astype(F32) + late_b[0].astype(F32)
-    total[:, 384:] = grad + (late_b[1].astype(F32) + late_b[2].astype(F32))
-    lasts = []
-    for target, device in ((1 - core, mate), (core, None)):
-        rows = pl.ds(pl.multiple_of(target * 40, 8), 40)
-        lasts.append(copies.start(total.at[rows, :], weights_ref.at[core], device))
-    wait_all(lasts + [deliver])
-    for waits in gathers:
-        wait_all(waits)
+    lasts = [copies.start(delivered_ref, delivered_hbm, None)]
+
+    later_y = second_stage(1, stage_z)
+    lasts += last_stage(0, later_z)
+    lasts += last_stage(1, later_y)
+    wait_all(lasts)
+    wait_all(forwards)
 
 
 def results_body(
     gx_hbm, both_hbm, arrived_hbm, gx_out, w_qkv_out, w_out_out, delivered_out,
-    gx_ref, both_ref, sems,
+    gx_in, gx_ref, both_ref, delivered_ref, sems,
 ):
     loads = [
-        pltpu.make_async_copy(gx_hbm.at[0], gx_ref.at[0], sems.at[0]),
-        pltpu.make_async_copy(gx_hbm.at[1], gx_ref.at[1], sems.at[1]),
-        pltpu.make_async_copy(both_hbm, both_ref, sems.at[2]),
-        pltpu.make_async_copy(arrived_hbm, delivered_out, sems.at[3]),
+        pltpu.make_async_copy(source, target, sems.at[index])
+        for index, (source, target) in enumerate(
+            (
+                (gx_hbm.at[0], gx_in.at[0]), (gx_hbm.at[1], gx_in.at[1]),
+                (both_hbm, both_ref), (arrived_hbm, delivered_ref),
+            )
+        )
     ]
     for load in loads:
         load.start()
     row = lax.broadcasted_iota(jnp.int32, (256, 256), 0)
     column = lax.broadcasted_iota(jnp.int32, (256, 256), 1)
     natural = jnp.where(row == 4 * (column % 64) + column // 64, 1.0, 0.0).astype(BF16)
+    stores = []
+
+    def store(source, target):
+        stores.append(pltpu.make_async_copy(source, target, sems.at[4 + len(stores)]))
+        stores[-1].start()
+
     for half in range(2):
         loads[half].wait()
-        rows = gx_ref[half].reshape(256, 1280)
-        gx_out[half * 256 : half * 256 + 256, :] = dot_nn(natural, rows).astype(BF16)
+        rows = gx_in[half].reshape(256, 1280)
+        gx_ref[half] = dot_nn(natural, rows).astype(BF16)
+        store(gx_ref.at[half], gx_out.at[half * 256 : half * 256 + 256, :])
     loads[2].wait()
-    w_qkv_out[0] = both_ref[0, :, :320]
-    w_qkv_out[1] = both_ref[0, :, 320:]
-    w_qkv_out[2] = both_ref[1, :, :320]
-    w_out_out[...] = both_ref[1, :, 320:]
+    store(both_ref.at[0], w_qkv_out.at[0:2])
+    store(both_ref.at[1, 1], w_qkv_out.at[2])
+    store(both_ref.at[1, 0], w_out_out)
     loads[3].wait()
+    store(delivered_ref, delivered_out)
+    for copy in stores:
+        copy.wait()
 
 
 def halo_peers(section, chip, core):
@@ -1087,7 +1183,7 @@
             pltpu.VMEM((2, HEAD_DIM, 2048), F32),
             pltpu.VMEM((2, HEAD_DIM, 2048), F32),
         ],
-        copies=13,
+        copies=14,
         limit=62,
     )
     arrived, gx_all, weights = call(
@@ -1095,7 +1191,7 @@
         [
             (HBM, shape((256, 1280))),
             (HBM, shape((2, 4, 64, 1280))),
-            (HBM, shape((2, 40, 640), F32)),
+            (HBM, shape((2, 2, 40, 320), F32)),
         ],
         [
             (HBM, dkv), (HBM, start_rows), (HBM, here), (HBM, dq), (HBM, qrow), (HBM, grow),
@@ -1131,24 +1227,21 @@
             pltpu.VMEM((960, 512), BF16),
             pltpu.VMEM((256, 960), BF16),
             pltpu.VMEM((2, 4, 64, 1280), BF16),
-            pltpu.VMEM((2, 3, 64, 1280), BF16),
+            pltpu.VMEM((2, 2, 32, 1280), BF16),
+            pltpu.VMEM((2, 2, 64, 1280), BF16),
             pltpu.VMEM((2, 64, 1280), BF16),
             pltpu.VMEM((320, 512), BF16),
             pltpu.VMEM((1280, 512), BF16),
             pltpu.VMEM((32, 16, 640), BF16),
             pltpu.VMEM((32, 16, 640), BF16),
-            pltpu.VMEM((4, 4, 80, 640), F32),
-            pltpu.VMEM((4, 4, 80, 640), BF16),
-            pltpu.VMEM((4, 4, 80, 640), BF16),
-            pltpu.VMEM((4, 4, 80, 384), BF16),
-            pltpu.VMEM((4, 4, 80, 256), BF16),
-            pltpu.VMEM((3, 4, 80, 384), BF16),
-            pltpu.VMEM((3, 4, 80, 256), BF16),
-            pltpu.VMEM((4, 80, 384), BF16),
-            pltpu.VMEM((4, 80, 256), BF16),
-            pltpu.VMEM((3, 80, 384), BF16),
-            pltpu.VMEM((3, 80, 256), BF16),
-            pltpu.VMEM((80, 640), F32),
+            pltpu.VMEM((4, 4, 80, 320), F32),
+            pltpu.VMEM((2, 4, 4, 80, 320), BF16),
+            pltpu.VMEM((2, 4, 4, 80, 320), BF16),
+            pltpu.VMEM((2, 4, 4, 80, 320), BF16),
+            pltpu.VMEM((2, 3, 4, 80, 320), BF16),
+            pltpu.VMEM((2, 4, 80, 320), BF16),
+            pltpu.VMEM((2, 3, 80, 320), BF16),
+            pltpu.VMEM((2, 80, 320), F32),
         ],
         copies=124,
         number=3,
@@ -1157,14 +1250,19 @@
     grad_x, grad_w_qkv, grad_w_out, delivered = call(
         results_body,
         [
-            (VMEM, shape((512, 1280))),
-            (VMEM, shape((3, 40, 320), F32)),
-            (VMEM, shape((40, 320), F32)),
-            (VMEM, shape((256, 1280))),
+            (HBM, shape((512, 1280))),
+            (HBM, shape((3, 40, 320), F32)),
+            (HBM, shape((40, 320), F32)),
+            (HBM, shape((256, 1280))),
         ],
         [(HBM, gx_all), (HBM, weights), (HBM, arrived)],
-        [pltpu.VMEM((2, 4, 64, 1280), BF16), pltpu.VMEM((2, 40, 640), F32)],
-        copies=4,
+        [
+            pltpu.VMEM((2, 4, 64, 1280), BF16),
+            pltpu.VMEM((2, 256, 1280), BF16),
+            pltpu.VMEM((2, 2, 40, 320), F32),
+            pltpu.VMEM((256, 1280), BF16),
+        ],
+        copies=10,
         limit=62,
     )
     return (delivered, grad_x, grad_w_qkv, grad_w_out.T)

time: 135 us -> 136 us (level)
  Pallas kernels: 133 us -> 135 us
where the time goes in v6:
time: 136 us; the launch traced here: 135 us
  Pallas kernels  135 us (99%)
    pallas_call x6, Pallas kernels, call(): pl.pallas_call(body, out_shape=[array for _, array in outs], in_specs=[pl...  135 us

profile of v6, /device:TPU:1, one launch (start us, length us, event | category | flops | bytes accessed | tf_op | source)
XLA Modules:
  0.0 135.5 jit_solution(12356134529740410096)
XLA Ops:
  0.6 29.9 %shard_map.120 = (bf16[160,1024]{1,0:T(8,128)(2,1)}, bf16[2,160,3072]{2,1,0:T(8,128)(2,1)}, bf16[1280,512]{1,0:T(8,128)(2,1)}, bf16[1280,1280]{1,0:T(8,128)(2,1)...) custom-call(s32[32]{0:T(128)} %seg_ref.5, bf16[512,1280]{1,0:T(8,128)(2,1)} %tokens_hbm.5, ...), custom_call_target="tpu_custom_call" | custom-call | tf_op jit(solution)/shard_map/pallas_call | solution.py:88
  30.6 16.8 %shard_map.121 = (bf16[160,1024]{1,0:T(8,128)(2,1)}, bf16[2,4,160,128]{3,2,1,0:T(8,128)(2,1)}, f32[2,1024]{1,0:T(2,128)}) custom-call(s32[32]{0:T(128)} %seg_ref.5, bf16[2,160,3072]{2,1,0:T(8,128)(2,1)} %get-tuple-element.35.kv_hbm, bf16[2,1024,128]{2,1,0:T(8,128)(2,1)} %get-tuple-element.36.qrow_hbm, f32[2,1024,128]{2,1,0:T(8,128)} %get-tuple-element.37.sums_hbm, ...), custom_call_target="tpu_custom_call" | custom-call | tf_op jit(solution)/shard_map/pallas_call | solution.py:88
  47.4 21.2 %shard_map.122 = (bf16[2,4,160,128]{3,2,1,0:T(8,128)(2,1)}, bf16[128,1280]{1,0:T(8,128)(2,1)}, bf16[1280,128]{1,0:T(8,128)(2,1)}, bf16[4,160,128]{2,1,0:T(8,128)(2,1)}, bf16[16,16,640]{2,1,0:T(8,128)(2,1)}) custom-call(bf16[2,4,160,128]{3,2,1,0:T(8,128)(2,1)} %get-tuple-element.41.op_ref.op_hbm, bf16[1280,1280]{1,0:T(8,128)(2,1)} %get-tuple-element.42.w_hbm, ...), custom_call_target="tpu_custom_call" | custom-call | tf_op jit(solution)/shard_map/pallas_call | solution.py:88
  68.6 8.1 %shard_map.123 = (f32[2,1024,128]{2,1,0:T(8,128)}, bf16[2,160,2048]{2,1,0:T(8,128)(2,1)}, s32[512,128]{1,0:T(8,128)}, s32[16,512]{1,0:T(8,128)}, bf16[2,1024,128...) custom-call(s32[32]{0:T(128)} %seg_ref.5, s32[32]{0:T(128)} %sizes_ref.1, ...), custom_call_target="tpu_custom_call" | custom-call | tf_op jit(solution)/shard_map/pallas_call | solution.py:88
  76.7 55.6 %shard_map.124 = (bf16[256,1280]{1,0:T(8,128)(2,1)}, bf16[2,4,64,1280]{3,2,1,0:T(8,128)(2,1)}, f32[2,2,40,320]{3,2,1,0:T(8,128)}) custom-call(bf16[2,160,2048]{2,1,0:T(8,128)(2,1)} %get-tuple-element.44.dkv_ref, s32[512,128]{1,0:T(8,128)} %get-tuple-element.45.starts_hbm, s32[16,512]{1,0:T(8,128)} %get-tuple-element.46.live_hbm, ...), custom_call_target="tpu_custom_call" | custom-call | tf_op jit(solution)/shard_map/pallas_call | solution.py:88
  132.2 3.0 %shard_map.125 = (bf16[512,1280]{1,0:T(8,128)(2,1)}, f32[3,40,320]{2,1,0:T(8,128)}, f32[40,320]{1,0:T(8,128)}, bf16[256,1280]{1,0:T(8,128)(2,1)}) custom-call(bf16[2,4,64,1280]{3,2,1,0:T(8,128)(2,1)} %get-tuple-element.57.gx_hbm, f32[2,2,40,320]{3,2,1,0:T(8,128)} %get-tuple-element.58.both_hbm, bf16[256,1280]{1,0:T(8,128)(2,1)} %get-tuple-element.59.arrived_hbm), custom_call_target="tpu_custom_call" | custom-call | tf_op jit(solution)/shard_map/pallas_call | solution.py:88

commit v7 on v6

--- a/solution.py
+++ b/solution.py
@@ -19,7 +19,7 @@
 MESH = pl.DeviceIdType.MESH
 FACTOR = HEAD_DIM ** -0.5
 LOG2E = 1.0 / math.log(2.0)
-LN2 = math.log(2.0)
+SCALE = FACTOR * LOG2E
 
 
 def dot_nn(left, right):
@@ -127,9 +127,13 @@
     def w_rows(owner, start, count):
         return w_full.at[pl.ds(pl.multiple_of(owner * 320 + core * PAIR + start, 16), count), :]
 
-    mine = w_out_hbm.at[pl.ds(pl.multiple_of(core * PAIR, 16), PAIR), :]
-    to_ahead = copies.start(mine, w_rows(section, 0, PAIR), ahead_dev)
-    to_behind = copies.start(mine, w_rows(section, 0, PAIR), behind_dev)
+    def mine(start):
+        return w_out_hbm.at[pl.ds(pl.multiple_of(core * PAIR + start, 16), 80), :]
+
+    to_ahead = copies.start(mine(0), w_rows(section, 0, 80), ahead_dev)
+    to_behind = copies.start(mine(80), w_rows(section, 80, 80), behind_dev)
+    rest_ahead = copies.start(mine(80), w_rows(section, 80, 80), ahead_dev)
+    rest_behind = copies.start(mine(0), w_rows(section, 0, 80), behind_dev)
     waits, inner = [], []
     load_gain.wait()
     gain = gain_ref[...].reshape(1, 1280).astype(F32)
@@ -145,8 +149,6 @@
     for which in (1, 2, 0):
         load_w[which].wait()
         out = dot_nn(w_ref[which], normed_t_ref[...])
-        if which == 0:
-            out = out * (FACTOR * LOG2E)
         out_ref[which] = out.astype(BF16)
         mine = pl.ds(pl.multiple_of(core * 512, 512), 512)
         target = q_ref.at[:, mine]
@@ -191,12 +193,14 @@
     relay = [copies.start(w_rows(behind, 0, 80), w_rows(behind, 0, 80), ahead_dev)]
     to_behind.wait()
     relay.append(copies.start(w_rows(ahead, 80, 80), w_rows(ahead, 80, 80), behind_dev))
-    waits.append(copies.start(w_rows(behind, 0, PAIR), w_rows(behind, 0, PAIR), mate))
-    waits.append(copies.start(w_rows(ahead, 0, PAIR), w_rows(ahead, 0, PAIR), mate))
     lax.fori_loop(2, 4, tile_step, 0)
     waits.append(copies.start(qrow, qrow_hbm, None))
     waits.append(copies.start(sums_ref, sums_hbm, None))
     waits.append(copies.start(norms_ref, norms_hbm, None))
+    rest_ahead.wait()
+    waits.append(copies.start(w_rows(behind, 0, PAIR), w_rows(behind, 0, PAIR), mate))
+    rest_behind.wait()
+    waits.append(copies.start(w_rows(ahead, 0, PAIR), w_rows(ahead, 0, PAIR), mate))
     far = (section + 2) % 4
     for copy, start in zip(relay, (0, 80)):
         copy.wait()
@@ -256,7 +260,7 @@
 def forward_step(rows, chunks, qrow, kx, vrow, sums):
     pairs = [(head, lanes) for lanes in chunks for head in range(2)]
     probs = [
-        jnp.exp2(dot_nn(qrow[head, rows, :], kx[head, :, lanes])).astype(BF16)
+        jnp.exp2(dot_nn(qrow[head, rows, :], kx[head, :, lanes]) * SCALE).astype(BF16)
         for head, lanes in pairs
     ]
     sums = list(sums)
@@ -343,14 +347,15 @@
         )
 
     tops = outside(bounds_ref[0, 0], bounds_ref[3, 1], build, (norms_ref[2], norms_ref[3]))
-    small = jnp.max(norms_ref[0]) * jnp.max(tops[0]) <= SAFE * SAFE
-    small = small & (jnp.max(norms_ref[1]) * jnp.max(tops[1]) <= SAFE * SAFE)
+    limit = (SAFE / SCALE) ** 2
+    small = jnp.max(norms_ref[0]) * jnp.max(tops[0]) <= limit
+    small = small & (jnp.max(norms_ref[1]) * jnp.max(tops[1]) <= limit)
 
     def write(head, rows, sums, top_row):
         out = sums.T
         total_row = out[80:81, :]
         o_ref[pl.ds(head * HEAD_DIM, HEAD_DIM), rows] = (out[:80] * (1.0 / total_row)).astype(BF16)
-        log_ref[head : head + 1, rows] = top_row + jnp.log(total_row) * LOG2E
+        log_ref[head : head + 1, rows] = top_row + jnp.log(total_row) * (LOG2E / SCALE)
 
     def plain_step(tile, carry):
         rows = pl.ds(pl.multiple_of(tile * 256, 256), 256)
@@ -447,7 +452,9 @@
 def backward_step(rows, chunks, q_ref, g_ref, qrow, grow, kx, vx, krow, dk_acc, dv_acc, sums):
     pairs = [(head, lanes) for lanes in chunks for head in range(2)]
     feats = [pl.ds(head * HEAD_DIM, HEAD_DIM) for head in range(2)]
-    probs = [jnp.exp2(dot_nn(qrow[head, rows, :], kx[head, :, lanes])) for head, lanes in pairs]
+    probs = [
+        jnp.exp2(dot_nn(qrow[head, rows, :], kx[head, :, lanes]) * SCALE) for head, lanes in pairs
+    ]
     shifted = [dot_nn(grow[head, rows, :], vx[head, :, lanes]) for head, lanes in pairs]
     dscores = [(prob * part).astype(BF16) for prob, part in zip(probs, shifted)]
     weights = [prob.astype(BF16) for prob in probs]
@@ -576,7 +583,7 @@
     keeps[-1].start()
     for head in range(2):
         feats = pl.ds(head * HEAD_DIM, HEAD_DIM)
-        dkv_ref[0, feats, :] = (dk_acc[head] * LN2).astype(BF16)
+        dkv_ref[0, feats, :] = (dk_acc[head] * FACTOR).astype(BF16)
         dkv_ref[1, feats, :] = dv_acc[head].astype(BF16)
     keeps.append(pltpu.make_async_copy(dkv_ref, dkv_hbm, sems.at[11]))
     keeps[-1].start()
@@ -746,7 +753,7 @@
                 feats = pl.ds(head * HEAD_DIM, HEAD_DIM)
                 part = dq_acc[head, lanes, :].T[:80] * FACTOR
                 own_out[half, of_core, 0, feats, :] = part.astype(BF16)
-                own_out[half, of_core, 1, feats, :] = (dk_acc[head, :, lanes] * LN2).astype(BF16)
+                own_out[half, of_core, 1, feats, :] = (dk_acc[head, :, lanes] * FACTOR).astype(BF16)
                 own_out[half, of_core, 2, feats, :] = dv_acc[head, :, lanes].astype(BF16)
         mates.append(copies.start(own_out.at[half, 1 - core], mate_in.at[half], mate))
 

time: 136 us -> 131 us (0.963)
  Pallas kernels: 135 us -> 130 us
    pallas_call x6, Pallas kernels: 135 us -> 130 us  [call(): pl.pallas_call(body, out_shape=[array for _, array in outs], in_specs=[pl...]
where the time goes in v7:
time: 131 us
  Pallas kernels  130 us (99%)
    pallas_call x6, Pallas kernels, call(): pl.pallas_call(body, out_shape=[array for _, array in outs], in_specs=[pl...  130 us

profile of v7, /device:TPU:1, one launch (start us, length us, event | category | flops | bytes accessed | tf_op | source)
XLA Modules:
  0.0 130.8 jit_solution(15414490004190964855)
XLA Ops:
  0.6 28.3 %shard_map.120 = (bf16[160,1024]{1,0:T(8,128)(2,1)}, bf16[2,160,3072]{2,1,0:T(8,128)(2,1)}, bf16[1280,512]{1,0:T(8,128)(2,1)}, bf16[1280,1280]{1,0:T(8,128)(2,1)...) custom-call(s32[32]{0:T(128)} %seg_ref.5, bf16[512,1280]{1,0:T(8,128)(2,1)} %tokens_hbm.5, ...), custom_call_target="tpu_custom_call" | custom-call | tf_op jit(solution)/shard_map/pallas_call | solution.py:88
  28.9 16.2 %shard_map.121 = (bf16[160,1024]{1,0:T(8,128)(2,1)}, bf16[2,4,160,128]{3,2,1,0:T(8,128)(2,1)}, f32[2,1024]{1,0:T(2,128)}) custom-call(s32[32]{0:T(128)} %seg_ref.5, bf16[2,160,3072]{2,1,0:T(8,128)(2,1)} %get-tuple-element.35.kv_hbm, bf16[2,1024,128]{2,1,0:T(8,128)(2,1)} %get-tuple-element.36.qrow_hbm, f32[2,1024,128]{2,1,0:T(8,128)} %get-tuple-element.37.sums_hbm, ...), custom_call_target="tpu_custom_call" | custom-call | tf_op jit(solution)/shard_map/pallas_call | solution.py:88
  45.2 20.6 %shard_map.122 = (bf16[2,4,160,128]{3,2,1,0:T(8,128)(2,1)}, bf16[128,1280]{1,0:T(8,128)(2,1)}, bf16[1280,128]{1,0:T(8,128)(2,1)}, bf16[4,160,128]{2,1,0:T(8,128)(2,1)}, bf16[16,16,640]{2,1,0:T(8,128)(2,1)}) custom-call(bf16[2,4,160,128]{3,2,1,0:T(8,128)(2,1)} %get-tuple-element.41.op_ref.op_hbm, bf16[1280,1280]{1,0:T(8,128)(2,1)} %get-tuple-element.42.w_hbm, ...), custom_call_target="tpu_custom_call" | custom-call | tf_op jit(solution)/shard_map/pallas_call | solution.py:88
  65.8 7.4 %shard_map.123 = (f32[2,1024,128]{2,1,0:T(8,128)}, bf16[2,160,2048]{2,1,0:T(8,128)(2,1)}, s32[512,128]{1,0:T(8,128)}, s32[16,512]{1,0:T(8,128)}, bf16[2,1024,128...) custom-call(s32[32]{0:T(128)} %seg_ref.5, s32[32]{0:T(128)} %sizes_ref.1, ...), custom_call_target="tpu_custom_call" | custom-call | tf_op jit(solution)/shard_map/pallas_call | solution.py:88
  73.2 54.4 %shard_map.124 = (bf16[256,1280]{1,0:T(8,128)(2,1)}, bf16[2,4,64,1280]{3,2,1,0:T(8,128)(2,1)}, f32[2,2,40,320]{3,2,1,0:T(8,128)}) custom-call(bf16[2,160,2048]{2,1,0:T(8,128)(2,1)} %get-tuple-element.44.dkv_ref, s32[512,128]{1,0:T(8,128)} %get-tuple-element.45.starts_hbm, s32[16,512]{1,0:T(8,128)} %get-tuple-element.46.live_hbm, ...), custom_call_target="tpu_custom_call" | custom-call | tf_op jit(solution)/shard_map/pallas_call | solution.py:88
  127.5 3.0 %shard_map.125 = (bf16[512,1280]{1,0:T(8,128)(2,1)}, f32[3,40,320]{2,1,0:T(8,128)}, f32[40,320]{1,0:T(8,128)}, bf16[256,1280]{1,0:T(8,128)(2,1)}) custom-call(bf16[2,4,64,1280]{3,2,1,0:T(8,128)(2,1)} %get-tuple-element.57.gx_hbm, f32[2,2,40,320]{3,2,1,0:T(8,128)} %get-tuple-element.58.both_hbm, bf16[256,1280]{1,0:T(8,128)(2,1)} %get-tuple-element.59.arrived_hbm), custom_call_target="tpu_custom_call" | custom-call | tf_op jit(solution)/shard_map/pallas_call | solution.py:88

commit v8 on v6

--- a/solution.py
+++ b/solution.py
@@ -127,9 +127,13 @@
     def w_rows(owner, start, count):
         return w_full.at[pl.ds(pl.multiple_of(owner * 320 + core * PAIR + start, 16), count), :]
 
-    mine = w_out_hbm.at[pl.ds(pl.multiple_of(core * PAIR, 16), PAIR), :]
-    to_ahead = copies.start(mine, w_rows(section, 0, PAIR), ahead_dev)
-    to_behind = copies.start(mine, w_rows(section, 0, PAIR), behind_dev)
+    def mine(start):
+        return w_out_hbm.at[pl.ds(pl.multiple_of(core * PAIR + start, 16), 80), :]
+
+    to_ahead = copies.start(mine(0), w_rows(section, 0, 80), ahead_dev)
+    to_behind = copies.start(mine(80), w_rows(section, 80, 80), behind_dev)
+    rest_ahead = copies.start(mine(80), w_rows(section, 80, 80), ahead_dev)
+    rest_behind = copies.start(mine(0), w_rows(section, 0, 80), behind_dev)
     waits, inner = [], []
     load_gain.wait()
     gain = gain_ref[...].reshape(1, 1280).astype(F32)
@@ -191,12 +195,14 @@
     relay = [copies.start(w_rows(behind, 0, 80), w_rows(behind, 0, 80), ahead_dev)]
     to_behind.wait()
     relay.append(copies.start(w_rows(ahead, 80, 80), w_rows(ahead, 80, 80), behind_dev))
-    waits.append(copies.start(w_rows(behind, 0, PAIR), w_rows(behind, 0, PAIR), mate))
-    waits.append(copies.start(w_rows(ahead, 0, PAIR), w_rows(ahead, 0, PAIR), mate))
     lax.fori_loop(2, 4, tile_step, 0)
     waits.append(copies.start(qrow, qrow_hbm, None))
     waits.append(copies.start(sums_ref, sums_hbm, None))
     waits.append(copies.start(norms_ref, norms_hbm, None))
+    rest_ahead.wait()
+    waits.append(copies.start(w_rows(behind, 0, PAIR), w_rows(behind, 0, PAIR), mate))
+    rest_behind.wait()
+    waits.append(copies.start(w_rows(ahead, 0, PAIR), w_rows(ahead, 0, PAIR), mate))
     far = (section + 2) % 4
     for copy, start in zip(relay, (0, 80)):
         copy.wait()

time: 136 us -> 133 us (0.978)
  Pallas kernels: 135 us -> 131 us
    pallas_call x6, Pallas kernels: 135 us -> 131 us  [call(): pl.pallas_call(body, out_shape=[array for _, array in outs], in_specs=[pl...]
where the time goes in v8:
time: 133 us; the launch traced here: 132 us
  Pallas kernels  131 us (98%)
    pallas_call x6, Pallas kernels, call(): pl.pallas_call(body, out_shape=[array for _, array in outs], in_specs=[pl...  131 us

profile of v8, /device:TPU:1, one launch (start us, length us, event | category | flops | bytes accessed | tf_op | source)
XLA Modules:
  0.0 132.1 jit_solution(14028346238390335406)
XLA Ops:
  0.6 28.3 %shard_map.120 = (bf16[160,1024]{1,0:T(8,128)(2,1)}, bf16[2,160,3072]{2,1,0:T(8,128)(2,1)}, bf16[1280,512]{1,0:T(8,128)(2,1)}, bf16[1280,1280]{1,0:T(8,128)(2,1)...) custom-call(s32[32]{0:T(128)} %seg_ref.5, bf16[512,1280]{1,0:T(8,128)(2,1)} %tokens_hbm.5, ...), custom_call_target="tpu_custom_call" | custom-call | tf_op jit(solution)/shard_map/pallas_call | solution.py:88
  28.9 15.9 %shard_map.121 = (bf16[160,1024]{1,0:T(8,128)(2,1)}, bf16[2,4,160,128]{3,2,1,0:T(8,128)(2,1)}, f32[2,1024]{1,0:T(2,128)}) custom-call(s32[32]{0:T(128)} %seg_ref.5, bf16[2,160,3072]{2,1,0:T(8,128)(2,1)} %get-tuple-element.35.kv_hbm, bf16[2,1024,128]{2,1,0:T(8,128)(2,1)} %get-tuple-element.36.qrow_hbm, f32[2,1024,128]{2,1,0:T(8,128)} %get-tuple-element.37.sums_hbm, ...), custom_call_target="tpu_custom_call" | custom-call | tf_op jit(solution)/shard_map/pallas_call | solution.py:88
  44.8 22.0 %shard_map.122 = (bf16[2,4,160,128]{3,2,1,0:T(8,128)(2,1)}, bf16[128,1280]{1,0:T(8,128)(2,1)}, bf16[1280,128]{1,0:T(8,128)(2,1)}, bf16[4,160,128]{2,1,0:T(8,128)(2,1)}, bf16[16,16,640]{2,1,0:T(8,128)(2,1)}) custom-call(bf16[2,4,160,128]{3,2,1,0:T(8,128)(2,1)} %get-tuple-element.41.op_ref.op_hbm, bf16[1280,1280]{1,0:T(8,128)(2,1)} %get-tuple-element.42.w_hbm, ...), custom_call_target="tpu_custom_call" | custom-call | tf_op jit(solution)/shard_map/pallas_call | solution.py:88
  66.8 7.1 %shard_map.123 = (f32[2,1024,128]{2,1,0:T(8,128)}, bf16[2,160,2048]{2,1,0:T(8,128)(2,1)}, s32[512,128]{1,0:T(8,128)}, s32[16,512]{1,0:T(8,128)}, bf16[2,1024,128...) custom-call(s32[32]{0:T(128)} %seg_ref.5, s32[32]{0:T(128)} %sizes_ref.1, ...), custom_call_target="tpu_custom_call" | custom-call | tf_op jit(solution)/shard_map/pallas_call | solution.py:88
  74.0 54.9 %shard_map.124 = (bf16[256,1280]{1,0:T(8,128)(2,1)}, bf16[2,4,64,1280]{3,2,1,0:T(8,128)(2,1)}, f32[2,2,40,320]{3,2,1,0:T(8,128)}) custom-call(bf16[2,160,2048]{2,1,0:T(8,128)(2,1)} %get-tuple-element.44.dkv_ref, s32[512,128]{1,0:T(8,128)} %get-tuple-element.45.starts_hbm, s32[16,512]{1,0:T(8,128)} %get-tuple-element.46.live_hbm, ...), custom_call_target="tpu_custom_call" | custom-call | tf_op jit(solution)/shard_map/pallas_call | solution.py:88
  128.9 3.0 %shard_map.125 = (bf16[512,1280]{1,0:T(8,128)(2,1)}, f32[3,40,320]{2,1,0:T(8,128)}, f32[40,320]{1,0:T(8,128)}, bf16[256,1280]{1,0:T(8,128)(2,1)}) custom-call(bf16[2,4,64,1280]{3,2,1,0:T(8,128)(2,1)} %get-tuple-element.57.gx_hbm, f32[2,2,40,320]{3,2,1,0:T(8,128)} %get-tuple-element.58.both_hbm, bf16[256,1280]{1,0:T(8,128)(2,1)} %get-tuple-element.59.arrived_hbm), custom_call_target="tpu_custom_call" | custom-call | tf_op jit(solution)/shard_map/pallas_call | solution.py:88
